TPU v7x, 128 devices: a whole 4x4x4 slice. The times are simulated.
128 devices in a mesh: dp: 16 (over y, z), fsdp: 8 (over x, core).
Axes of the slice: x: 4, y: 4, z: 4, core: 2. Of those that a mesh axis runs over, the one named last changes fastest.
Arguments:
- head_output: bfloat16 [262144, 2048], P(('dp', 'fsdp')), may hold values from -6 to 6
- router_logits: float32 [262144], P(('dp', 'fsdp')), may hold values from -8 to 8
- chosen_slots: int32 [128, 512], P(('dp', 'fsdp')), may hold values from 0 to 2047, as said below
- block_owner: int32 [128, 16], P(('dp', 'fsdp')), may hold values from 0 to 16, as said below
- out_weight: bfloat16 [2048, 4096], P('fsdp'), may hold values from -0.125 to 0.125
- cotangent: bfloat16 [32768, 4096], P(('dp', 'fsdp')), may hold values from -6 to 6
Outputs:
- update: bfloat16 [32768, 4096], P(('dp', 'fsdp'))
- grad_context: bfloat16 [65536, 2048], P(('dp', 'fsdp'))
- grad_logit: bfloat16 [65536], P(('dp', 'fsdp'))
- grad_weight: float32 [2048, 4096], P('fsdp')
Inputs may be any that keep to these rules, and one draw needn't show every extreme that they name: `chosen_slots`: in each device's row the first (used blocks) * 32 entries are distinct tokens in ascending order; the remaining entries are other distinct tokens of the device and are not read. `block_owner`: used blocks precede unused ones. Within one fsdp index every dp index is owner of exactly 8 blocks, a device gives at most one block to any one owner, and some device has all 16 blocks used.
All inputs are finite; a program needn't handle non-finite values.
Results may differ from a plain program's by a relative error of at most 0.025.
Values may be sent and summed in bfloat16 or wider, within the bound.
No kernel may reach another device: no remote copies, remote signals or barrier semaphores. Data moves between devices by JAX's collectives and lax.ppermute only.
A program may use at most 192 MiB of HBM per device.

v0:
```python
import math

import jax
import jax.numpy as jnp
from jax import lax
from jax.sharding import PartitionSpec as P


def spread_blocks(onehot, blocks):
    return jnp.einsum("pb,bkh->pkh", onehot, blocks, preferred_element_type=jnp.float32).astype(
        blocks.dtype
    )


def local_pass(picked_rows, gating, cotangent_rows, weights_full):
    projected = jnp.dot(picked_rows, weights_full, preferred_element_type=jnp.float32)
    gate_wide = gating.astype(jnp.float32)
    update = (gate_wide[:, None] * projected).astype(jnp.bfloat16)
    weighted = (gate_wide[:, None] * cotangent_rows.astype(jnp.float32)).astype(jnp.bfloat16)
    row_grad = lax.dot_general(
        weighted, weights_full, (((1,), (1,)), ((), ())), preferred_element_type=jnp.float32
    ).astype(jnp.bfloat16)
    inner_sum = jnp.sum(cotangent_rows.astype(jnp.float32) * projected, axis=1)
    grad_router = (gate_wide * (1.0 - gate_wide) * inner_sum).astype(jnp.bfloat16)
    return (update, weighted, row_grad, grad_router)


def on_device(head_output, router_logits, chosen_slots, block_owner, out_weight, cotangent):
    group_size = lax.axis_size("dp")
    my_index = lax.axis_index("dp")
    slot_count = chosen_slots.shape[1]
    block_slots = block_owner.shape[1]
    block_rows = slot_count // block_slots
    model_width = out_weight.shape[1]
    receive_blocks = cotangent.shape[0] // block_rows
    total_rows = cotangent.shape[0] * group_size * lax.axis_size("fsdp")
    grad_scale = 1.0 / math.sqrt(total_rows)
    owner_row = block_owner[0]
    peer_ids = jnp.arange(group_size, dtype=jnp.int32)
    outward = (owner_row[None, :] == peer_ids[:, None]).astype(jnp.bfloat16)
    routing = lax.all_gather(block_owner, "dp", axis=0, tiled=True)
    incoming = jnp.any(routing == my_index, axis=1).astype(jnp.int32)
    position = jnp.cumsum(incoming) - 1
    receive_ids = jnp.arange(receive_blocks, dtype=jnp.int32)
    inward = ((position[None, :] == receive_ids[:, None]) & (incoming[None, :] > 0)).astype(
        jnp.bfloat16
    )
    picked_rows = jnp.take(head_output, chosen_slots[0], axis=0)
    gating = jax.nn.sigmoid(jnp.take(router_logits, chosen_slots[0])).astype(jnp.bfloat16)
    weights_full = lax.all_gather(out_weight, "fsdp", axis=0, tiled=True)
    cot_blocks = spread_blocks(inward.T, cotangent.reshape(receive_blocks, block_rows, model_width))
    got_cot = lax.all_to_all(cot_blocks, "dp", split_axis=0, concat_axis=0, tiled=True)
    slot_cot = spread_blocks(outward.T, got_cot).reshape(slot_count, model_width)
    slot_update, term_weighted, grad_context, grad_logit = local_pass(
        picked_rows, gating, slot_cot, weights_full
    )
    send_update = spread_blocks(outward, slot_update.reshape(block_slots, block_rows, model_width))
    got_update = lax.all_to_all(send_update, "dp", split_axis=0, concat_axis=0, tiled=True)
    update = spread_blocks(inward, got_update).reshape(receive_blocks * block_rows, model_width)
    partial_sum = lax.psum_scatter(
        (
            lax.dot_general(
                picked_rows,
                term_weighted,
                (((0,), (0,)), ((), ())),
                preferred_element_type=jnp.float32,
            )
            * grad_scale
        ).astype(jnp.bfloat16),
        "fsdp",
        scatter_dimension=0,
        tiled=True,
    )
    grad_weight = lax.psum(partial_sum, "dp").astype(jnp.float32)
    return (update, grad_context, grad_logit, grad_weight)


def solution(mesh):
    placed = (
        P(("dp", "fsdp"), None),
        P(("dp", "fsdp")),
        P(("dp", "fsdp"), None),
        P(("dp", "fsdp"), None),
        P("fsdp", None),
        P(("dp", "fsdp"), None),
    )
    return jax.shard_map(
        on_device,
        mesh=mesh,
        in_specs=placed,
        out_specs=(
            P(("dp", "fsdp"), None),
            P(("dp", "fsdp"), None),
            P(("dp", "fsdp")),
            P("fsdp", None),
        ),
        check_vma=False,
    )
```

profile of v0, /device:TPU:0, one launch (start us, length us, event | category | flops | bytes accessed | tf_op | source)
XLA Modules:
  0.0 343.1 jit_solution(6533230055525049731)
XLA Ops:
  7.2 0.7 all-gather.3.cloned.1.call-update
  7.9 22.1 %all-gather = s32[16,1,16]{2,1,0:T(1,128)S(1)} all-gather(s32[1,1,16]{2,1,0:T(1,128)} %bitcast.37), channel_id=1, replica_groups=mesh['dp'=16,'fsdp'=8] {'dp'}, dimensions={0}, use_global_device_ids=true | all-gather | bytes 1088 | tf_op jit(solution)/shard_map/all_gather | solution.py:41
  30.7 2.0 convolution_convert_fusion.1
  32.7 4.3 %copy.22 = bf16[16,32,4096]{2,1,0:T(8,128)(2,1)} copy(bf16[16,32,4096]{2,0,1:T(8,128)(2,1)S(1)} %convolution_convert_fusion.1) | data formatting | bytes 8388608 | tf_op jit(solution)/shard_map/convert_element_type | solution.py:10
  37.0 5.4 %all-to-all-start.1 = ((bf16[16,32,4096]{2,1,0:T(8,128)(2,1)}), bf16[16,32,4096]{2,1,0:T(8,128)(2,1)}, u32[]{:S(2)}, u32[]{:S(2)}) async-start(bf16[16,32,4096]{2,1,0:T(8,128)(2,1)} %copy.22), calls=%async_computation.1 | async-start | bytes 8388608 | tf_op jit(solution)/shard_map/all_to_all | solution.py:52
  42.6 3.1 gather_fusion
  45.7 9.2 %gather_fusion.1 = bf16[512,2048]{1,0:T(8,128)(2,1)S(1)} fusion(bf16[2048,2048]{1,0:T(8,128)(2,1)} %param.6, s32[1024]{0:T(1024)S(1)} %pad_clamp_fusion), kind=kCustom, calls=%fused_computation.1 | custom fusion | bytes 4196352 | tf_op jit(solution)/shard_map/jit(_take)/gather | solution.py:48
  54.9 35.4 %all-to-all-done.1 = bf16[16,32,4096]{2,1,0:T(8,128)(2,1)} async-done(((bf16[16,32,4096]{2,1,0:T(8,128)(2,1)}), bf16[16,32,4096]{2,1,0:T(8,128)(2,1)}, u32[]{:S(2)}, u32[]{:S(2)}) %all-to-all-start.1) | async-done | bytes 4194336 | tf_op jit(solution)/shard_map/all_to_all | solution.py:52
  90.3 7.0 %fusion.2 = f32[16,32,4096]{2,0,1:T(8,128)S(1)} fusion(bf16[16,32,4096]{2,1,0:T(8,128)(2,1)} %all-to-all-done.1, s32[16]{0:T(128)S(1)} %bitcast.38), kind=kOutput, calls=%fused_computation.9 | convolution fusion | flops 71303424 | bytes 12582976 | tf_op jit(solution)/shard_map/pb,bkh->pkh/dot_general | solution.py:10
  97.3 8.1 %copy.24 = f32[16,32,4096]{2,1,0:T(8,128)} copy(f32[16,32,4096]{2,0,1:T(8,128)S(1)} %fusion.2) | data formatting | bytes 16777216 | tf_op jit(solution)/shard_map/convert_element_type | solution.py:19
  105.4 16.3 %fusion.1 = (f32[512]{0:T(512)S(1)}, f32[512,4096]{1,0:T(8,128)}) fusion(f32[16,32,4096]{2,1,0:T(8,128)} %copy.24, bf16[2048,4096]{1,0:T(8,128)(2,1)} %all-gather.3.cloned.1.call-done, bf16[512,2048]{1,0:T(8,128)(2,1)S(1)} %gather_fusion.1, pred[512]{0:T(512)(128)(4,1)S(1)} %compare_and_fusion), kind=kOutput, calls=%fused_computation.6 | convolution fusion | flops 8595177472 | bytes 35654144 | tf_op jit(solution)/shard_map/dot_general | solution.py:16
  121.7 0.6 fusion.18
  122.3 6.1 %fusion = (bf16[512,4096]{1,0:T(8,128)(2,1)S(1)}, bf16[512,4096]{1,0:T(8,128)(2,1)}) fusion(f32[16,32,4096]{2,1,0:T(8,128)S(1)} %copy-done.3, f32[512]{0:T(512)S(1)} %convert_element_type.78, f32[512,4096]{1,0:T(8,128)} %get-tuple-element.11), kind=kLoop, calls=%fused_computation.5 | loop fusion | flops 8388608 | bytes 25167872 | tf_op jit(solution)/shard_map/convert_element_type | solution.py:19
  128.5 2.0 copy-done.4
  130.5 13.0 %multiply_convert_fusion = bf16[2048,4096]{1,0:T(8,128)(2,1)} fusion(bf16[512,4096]{1,0:T(8,128)(2,1)S(1)} %get-tuple-element.6, bf16[512,2048]{1,0:T(8,128)(2,1)S(1)} %gather_fusion.1, pred[512]{0:T(512)(128)(4,1)S(1)} %compare_and_fusion), kind=kOutput, calls=%fused_computation.2 | convolution fusion | flops 8607760384 | bytes 23069184 | tf_op jit(solution)/shard_map/dot_general | solution.py:62
  143.6 7.0 %convolution_convert_fusion.2 = bf16[16,32,4096]{2,0,1:T(8,128)(2,1)S(1)} fusion(bf16[16,32,4096]{2,1,0:T(8,128)(2,1)} %bitcast.32, s32[16]{0:T(128)S(1)} %bitcast.39), kind=kOutput, calls=%fused_computation.11 | convolution fusion | flops 69206272 | bytes 8388672 | tf_op jit(solution)/shard_map/pb,bkh->pkh/dot_general | solution.py:10
  150.6 4.3 %copy.18 = bf16[16,32,4096]{2,1,0:T(8,128)(2,1)} copy(bf16[16,32,4096]{2,0,1:T(8,128)(2,1)S(1)} %convolution_convert_fusion.2) | data formatting | bytes 8388608 | tf_op jit(solution)/shard_map/convert_element_type | solution.py:10
  154.9 9.3 %all-to-all-start = ((bf16[16,32,4096]{2,1,0:T(8,128)(2,1)}), bf16[16,32,4096]{2,1,0:T(8,128)(2,1)}, u32[]{:S(2)}, u32[]{:S(2)}) async-start(bf16[16,32,4096]{2,1,0:T(8,128)(2,1)} %copy.18), calls=%async_computation | async-start | bytes 8388608 | tf_op jit(solution)/shard_map/all_to_all | solution.py:58
  164.2 74.6 %reduce-scatter.2.cloned.1.call-done = bf16[256,4096]{1,0:T(8,128)(2,1)} async-done(((bf16[2048,4096]{1,0:T(8,128)(2,1)}), bf16[256,4096]{1,0:T(8,128)(2,1)}) %reduce-scatter.2.cloned.1.call-update) | async-done | bytes 2097168 | tf_op jit(solution)/shard_map/reduce_scatter | solution.py:60
  238.9 14.8 %convolution_convert_fusion.4 = bf16[512,2048]{1,0:T(8,128)(2,1)} fusion(bf16[512,4096]{1,0:T(8,128)(2,1)} %copy-done.4, bf16[2048,4096]{1,0:T(8,128)(2,1)} %all-gather.3.cloned.1.call-done), kind=kOutput, calls=%fused_computation.16 | convolution fusion | flops 8590983168 | bytes 23068672 | tf_op jit(solution)/shard_map/dot_general | solution.py:20
  253.7 6.8 %convolution_convert_fusion.3 = bf16[8,32,4096]{2,0,1:T(8,128)(2,1)S(1)} fusion(bf16[16,32,4096]{2,1,0:T(8,128)(2,1)} %all-to-all-done, s32[16]{0:T(128)S(1)} %add_reduce_fusion, pred[16]{0:T(512)(128)(4,1)S(1)} %get-tuple-element.8), kind=kOutput, calls=%fused_computation.12 | convolution fusion | flops 34603264 | bytes 6291536 | tf_op jit(solution)/shard_map/pb,bkh->pkh/dot_general | solution.py:10
  260.5 2.5 copy.20
  263.0 69.3 %all-reduce.2.cloned.1.call-done = bf16[256,4096]{1,0:T(8,128)(2,1)} async-done(((bf16[256,4096]{1,0:T(8,128)(2,1)}), bf16[256,4096]{1,0:T(8,128)(2,1)}) %all-reduce.2.cloned.1.call-update) | async-done | bytes 2097168 | tf_op jit(solution)/shard_map/psum | solution.py:74
  332.2 4.1 %convert_element_type.90 = f32[256,4096]{1,0:T(8,128)} convert(bf16[256,4096]{1,0:T(8,128)(2,1)} %all-reduce.2.cloned.1.call-done) | non-fusion elementwise | flops 1048576 | bytes 6291456 | tf_op jit(solution)/shard_map/convert_element_type | solution.py:74
  (29 shorter events, 0.8 us)
Async XLA Ops:
  7.2 23.5 %copy-start = (bf16[256,4096]{1,0:T(8,128)(2,1)S(1)}, bf16[256,4096]{1,0:T(8,128)(2,1)}, u32[]{:S(2)}) copy-start(bf16[256,4096]{1,0:T(8,128)(2,1)} %param.11) | copy-start | bytes 6291460
  7.2 98.2 %all-gather.3.cloned.1.call-start = ((), (), s32[]{:S(2)}) async-start(), calls=%async_computation.3 | async-start | bytes 18874368 | tf_op jit(solution)/shard_map/all_gather | solution.py:50
  37.0 5.5 %copy-start.5 = (s32[1,512]{1,0:T(1,128)S(1)}, s32[1,512]{1,0:T(1,128)}, u32[]{:S(2)}) copy-start(s32[1,512]{1,0:T(1,128)} %param.8) | copy-start | bytes 6148
  37.0 5.5 %copy-start.2 = (f32[2048]{0:T(1024)S(1)}, f32[2048]{0:T(1024)}, u32[]{:S(2)}) copy-start(f32[2048]{0:T(1024)} %param.7) | copy-start | bytes 24580
  37.0 53.3 %all-to-all-start.1 = ((bf16[16,32,4096]{2,1,0:T(8,128)(2,1)}), bf16[16,32,4096]{2,1,0:T(8,128)(2,1)}, u32[]{:S(2)}, u32[]{:S(2)}) async-start(bf16[16,32,4096]{2,1,0:T(8,128)(2,1)} %copy.22), calls=%async_computation.1 | async-start | bytes 8388608 | tf_op jit(solution)/shard_map/all_to_all | solution.py:52
  42.5 196.4 %reduce-scatter.2.cloned.1.call-start = ((), (), s32[]{:S(2)}) async-start(), calls=%async_computation.4 | async-start | bytes 18874368 | tf_op jit(solution)/shard_map/reduce_scatter | solution.py:60
  45.7 44.6 %copy-start.6 = (s32[1,16]{1,0:T(1,128)S(1)}, s32[1,16]{1,0:T(1,128)}, u32[]{:S(2)}) copy-start(s32[1,16]{1,0:T(1,128)} %param.9) | copy-start | bytes 196
  105.4 16.9 %copy-start.3 = (f32[16,32,4096]{2,1,0:T(8,128)S(1)}, f32[16,32,4096]{2,1,0:T(8,128)}, u32[]{:S(2)}) copy-start(f32[16,32,4096]{2,1,0:T(8,128)} %copy.24) | copy-start | bytes 25165828
  128.5 2.0 copy-start.4
  154.9 98.8 %all-to-all-start = ((bf16[16,32,4096]{2,1,0:T(8,128)(2,1)}), bf16[16,32,4096]{2,1,0:T(8,128)(2,1)}, u32[]{:S(2)}, u32[]{:S(2)}) async-start(bf16[16,32,4096]{2,1,0:T(8,128)(2,1)} %copy.18), calls=%async_computation | async-start | bytes 8388608 | tf_op jit(solution)/shard_map/all_to_all | solution.py:58
  164.2 168.1 %all-reduce.2.cloned.1.call-start = ((), (), s32[]{:S(2)}) async-start(), calls=%async_computation.5 | async-start | bytes 4194304 | tf_op jit(solution)/shard_map/psum | solution.py:74
  260.5 75.9 %copy-start.1 = (bf16[256,4096]{1,0:T(8,128)(2,1)S(1)}, bf16[256,4096]{1,0:T(8,128)(2,1)}, u32[]{:S(2)}) copy-start(bf16[256,4096]{1,0:T(8,128)(2,1)} %param.11) | copy-start | bytes 6291460
Sparse Core Ops, SparseCore 0:
  9.7 87.3 all-gather.2
  143.7 95.1 reduce-scatter.1
  242.2 89.9 all-reduce.1
where the time goes:
time: 349 us; the launch traced here: 343 us
  waiting for transfers between devices  180 us (52%)
  matrix products  67 us (19%)
  local copies, waits for them, and re-layouts  33.7 us (10%)
  blocking collectives  22.1 us (6%)
  starting transfers between devices  14.9 us (4%)
  between operations  14.1 us (4%)
  other arithmetic  11.4 us (3%)
    reduce_scatter x1, waiting for transfers between devices, on_device(): lax.psum_scatter((lax.dot_general(picked_rows, term_weighted, (((0,), (0,...  74.6 us
    psum x1, waiting for transfers between devices, on_device(): grad_weight = lax.psum(partial_sum, 'dp').astype(jnp.float32)  69.3 us
    all_to_all x1, waiting for transfers between devices, on_device(): lax.all_to_all(cot_blocks, 'dp', split_axis=0, concat_axis=0, tiled=True)  35.4 us
    dot_general x4, matrix products, spread_blocks(): jnp.einsum('pb,bkh->pkh', onehot, blocks, preferred_element_type=jnp.floa...  22.8 us
    all_gather x1, blocking collectives, on_device(): routing = lax.all_gather(block_owner, 'dp', axis=0, tiled=True)  22.1 us
    dot_general x1, matrix products, local_pass(): jnp.dot(picked_rows, weights_full, preferred_element_type=jnp.float32)  16.3 us
    dot_general x1, matrix products, local_pass(): lax.dot_general(weighted, weights_full, (((1,), (1,)), ((), ())), preferr...  14.8 us
    dot_general x1, matrix products, on_device(): lax.dot_general(picked_rows, term_weighted, (((0,), (0,)), ((), ())), pre...  13 us
  transfers between devices with their start and end apart: 5, of which 3 were waited for; matrix products, arithmetic and copies ran while one was open for 20% of the time, Pallas kernels for 0%

commit v1 on v0

v1 whole, which is shorter than its diff:
```python
import math

import jax
import jax.numpy as jnp
from jax import lax
from jax.experimental import pallas as pl
from jax.experimental.pallas import tpu as pltpu
from jax.sharding import PartitionSpec as P

EXTRA = 128
VMEM_LIMIT = 56 * 1024 * 1024


def params():
    return pltpu.CompilerParams(vmem_limit_bytes=VMEM_LIMIT)


def pick_body(width, token_ref, head_ref, extra_ref, out_ref, onehot_ref):
    step = pl.program_id(0)
    columns = head_ref.shape[1]

    @pl.when(step == 0)
    def _():
        tokens = lax.broadcasted_iota(jnp.int32, onehot_ref.shape, 1)
        onehot_ref[...] = (token_ref[...] == tokens).astype(jnp.bfloat16)
        out_ref[:, width:] = jnp.dot(
            onehot_ref[...], extra_ref[...], preferred_element_type=jnp.float32
        ).astype(jnp.bfloat16)

    out_ref[:, pl.ds(pl.multiple_of(step * columns, columns), columns)] = jnp.dot(
        onehot_ref[...], head_ref[...], preferred_element_type=jnp.float32
    ).astype(jnp.bfloat16)


def pick_rows(tokens, head, extra):
    rows = tokens.shape[0]
    count, width = head.shape
    columns = 256
    return pl.pallas_call(
        lambda *refs: pick_body(width, *refs),
        out_shape=jax.ShapeDtypeStruct((rows, width + EXTRA), jnp.bfloat16),
        grid=(width // columns,),
        in_specs=[
            pl.BlockSpec((rows, 1), lambda n: (0, 0)),
            pl.BlockSpec((count, columns), lambda n: (0, n)),
            pl.BlockSpec((count, EXTRA), lambda n: (0, 0)),
        ],
        out_specs=pl.BlockSpec((rows, width + EXTRA), lambda n: (0, 0)),
        scratch_shapes=[pltpu.VMEM((rows, count), jnp.bfloat16)],
        compiler_params=params(),
        cost_estimate=pl.CostEstimate(
            flops=2 * rows * count * width,
            bytes_accessed=2 * (count * width + rows * width),
            transcendentals=0,
        ),
        name="pick_rows",
    )(tokens[:, None], head, extra)


def move_body(width, index_ref, source_ref, out_ref):
    blocks = source_ref.shape[0]
    for slot in range(out_ref.shape[0]):
        block = index_ref[slot]

        @pl.when(block < blocks)
        def _():
            out_ref[slot] = source_ref[jnp.minimum(block, blocks - 1), :, :width]

        @pl.when(block >= blocks)
        def _():
            out_ref[slot] = jnp.zeros(out_ref.shape[1:], out_ref.dtype)


def move_blocks(source, index, width):
    blocks, rows, _ = source.shape
    copies = index.shape[0]
    return pl.pallas_call(
        lambda *refs: move_body(width, *refs),
        out_shape=jax.ShapeDtypeStruct((copies, rows, width), source.dtype),
        in_specs=[
            pl.BlockSpec(memory_space=pltpu.SMEM),
            pl.BlockSpec(memory_space=pltpu.VMEM),
        ],
        out_specs=pl.BlockSpec(memory_space=pltpu.VMEM),
        compiler_params=params(),
        cost_estimate=pl.CostEstimate(
            flops=0, bytes_accessed=4 * copies * rows * width, transcendentals=0
        ),
        name="move_blocks",
    )(index, source)


def project_body(shards, width, *refs):
    place_ref, rows_ref, cot_ref = refs[:3]
    weights = refs[3 : 3 + shards + 2]
    update_ref, grad_ref, lhs_ref, weight_ref, total_ref, inner_ref = refs[3 + shards + 2 :]
    step, steps = pl.program_id(0), pl.num_programs(0)
    part = width // shards

    @pl.when(step == 0)
    def _():
        total_ref[...] = jnp.zeros_like(total_ref)
        inner_ref[...] = jnp.zeros_like(inner_ref)
        for i in range(shards):
            start = pl.multiple_of(place_ref[i] * part, part)
            lhs_ref[:, i * part : (i + 1) * part] = rows_ref[:, pl.ds(start, part)]

    for i in range(shards - 2):
        weight_ref[i * part : (i + 1) * part, :] = weights[i][...]
    for i in range(2):
        at = (shards - 2 + i) * part

        @pl.when(step < steps // 2)
        def _():
            weight_ref[at : at + part, :] = weights[shards - 2 + 2 * i][...]

        @pl.when(step >= steps // 2)
        def _():
            weight_ref[at : at + part, :] = weights[shards - 1 + 2 * i][...]

    weight = weight_ref[...]
    gate = rows_ref[:, width : width + 1].astype(jnp.float32)
    projected = jnp.dot(lhs_ref[...], weight, preferred_element_type=jnp.float32)
    update_ref[...] = (gate * projected).astype(jnp.bfloat16)
    cot = cot_ref[...].astype(jnp.float32)
    inner_ref[...] += cot * projected
    weighted = (gate * cot).astype(jnp.bfloat16)
    total_ref[...] += lax.dot_general(
        weighted, weight, (((1,), (1,)), ((), ())), preferred_element_type=jnp.float32
    )

    @pl.when(step == steps - 1)
    def _():
        for i in range(shards):
            start = pl.multiple_of(place_ref[i] * part, part)
            grad_ref[:, pl.ds(start, part)] = total_ref[:, i * part : (i + 1) * part].astype(jnp.bfloat16)
        inner = jnp.sum(inner_ref[...], axis=1, keepdims=True)
        logit = gate * (1.0 - gate) * inner
        grad_ref[:, width:] = jnp.broadcast_to(logit, (logit.shape[0], EXTRA)).astype(jnp.bfloat16)


def project(rows, cotangent, places, weights):
    count, wide = rows.shape
    width = wide - EXTRA
    model = cotangent.shape[1]
    shards = len(weights) - 2
    part = width // shards
    columns = 512
    steps = model // columns
    whole = pl.BlockSpec((part, columns), lambda n: (0, n))
    left = pl.BlockSpec((part, columns), lambda n: (0, jnp.minimum(n, steps // 2 - 1)))
    right = pl.BlockSpec((part, columns), lambda n: (0, jnp.maximum(n - steps // 2, 0)))
    return pl.pallas_call(
        lambda *refs: project_body(shards, width, *refs),
        out_shape=(
            jax.ShapeDtypeStruct((count, model), jnp.bfloat16),
            jax.ShapeDtypeStruct((count, wide), jnp.bfloat16),
        ),
        grid=(steps,),
        in_specs=[
            pl.BlockSpec(memory_space=pltpu.SMEM),
            pl.BlockSpec((count, wide), lambda n: (0, 0)),
            pl.BlockSpec((count, columns), lambda n: (0, n)),
        ]
        + [whole] * (shards - 2)
        + [left, right] * 2,
        out_specs=(
            pl.BlockSpec((count, columns), lambda n: (0, n)),
            pl.BlockSpec((count, wide), lambda n: (0, 0)),
        ),
        scratch_shapes=[
            pltpu.VMEM((count, width), jnp.bfloat16),
            pltpu.VMEM((width, columns), jnp.bfloat16),
            pltpu.VMEM((count, width), jnp.float32),
            pltpu.VMEM((count, columns), jnp.float32),
        ],
        compiler_params=params(),
        cost_estimate=pl.CostEstimate(
            flops=4 * count * width * model,
            bytes_accessed=2 * (model * (width + 2 * count) + 2 * count * wide),
            transcendentals=0,
        ),
        name="project",
    )(places, rows, cotangent, *weights)


def place_body(first_ref, second_ref, out_ref):
    side, _, halves, _, _, columns = first_ref.shape
    half = out_ref.shape[1] // halves
    for h in range(halves):
        for k in range(side):
            left = h * half + k * columns
            right = left + half // 2
            out_ref[:, left : left + columns] = first_ref[k, 0, h, 0].astype(jnp.float32)
            out_ref[:, right : right + columns] = second_ref[0, k, h, 0].astype(jnp.float32)


def place_blocks(pieces):
    side, _, halves, _, rows, columns = pieces.shape
    model = halves * 2 * side * columns
    return pl.pallas_call(
        place_body,
        out_shape=jax.ShapeDtypeStruct((side * rows, model), jnp.float32),
        grid=(side,),
        in_specs=[
            pl.BlockSpec((side, 1, halves, 1, rows, columns), lambda r: (0, r, 0, 0, 0, 0)),
            pl.BlockSpec((1, side, halves, 1, rows, columns), lambda r: (r, 0, 0, 1, 0, 0)),
        ],
        out_specs=pl.BlockSpec((rows, model), lambda r: (r, 0)),
        compiler_params=params(),
        cost_estimate=pl.CostEstimate(
            flops=0, bytes_accessed=6 * side * rows * model, transcendentals=0
        ),
        name="place_blocks",
    )(pieces, pieces)


def at(array, index, axis=0):
    return lax.dynamic_index_in_dim(array, index, axis, keepdims=False)


def on_device(head_output, router_logits, chosen_slots, block_owner, out_weight, cotangent):
    n_dp, n_fsdp = lax.axis_size("dp"), lax.axis_size("fsdp")
    dp, fsdp = lax.axis_index("dp"), lax.axis_index("fsdp")
    side, chips = math.isqrt(n_dp), n_fsdp // 2
    y, z = dp // side, dp % side
    chip, core = fsdp // 2, fsdp % 2

    def along_x(value, ahead):
        return lax.ppermute(value, "fsdp", [(f, (f + 2 * ahead) % n_fsdp) for f in range(n_fsdp)])

    def along_y(value, ahead):
        return lax.ppermute(value, "dp", [(d, (d + side * ahead) % n_dp) for d in range(n_dp)])

    def along_z(value, ahead):
        return lax.ppermute(
            value, "dp", [(d, d // side * side + (d + ahead) % side) for d in range(n_dp)]
        )

    def to_partner(value):
        return lax.ppermute(value, "fsdp", [(f, f ^ 1) for f in range(n_fsdp)])

    slots = chosen_slots.shape[1]
    blocks = block_owner.shape[1]
    block = slots // blocks
    tokens, width = head_output.shape
    shard, model = out_weight.shape
    rows = cotangent.shape[0]
    receive = rows // block
    scale = 1.0 / math.sqrt(rows * n_dp * n_fsdp)
    half = model // 2
    owner = block_owner[0]

    below = along_x(out_weight, 1)
    above = along_x(out_weight, -1)
    far_left = along_x(below[:, :half], 1)
    far_right = along_x(above[:, half:], -1)
    mine = (out_weight, below, above, far_left, far_right)
    theirs = tuple(to_partner(w) for w in mine)
    weights = mine[:3] + theirs[:3] + mine[3:] + theirs[3:]
    near = (chip, (chip + chips - 1) % chips, (chip + 1) % chips)
    places = [2 * c + core for c in near] + [2 * c + 1 - core for c in near]
    opposite = 2 * ((chip + 2) % chips)
    places = jnp.stack(places + [opposite + core, opposite + 1 - core]).astype(jnp.int32)

    own_cot = lax.dynamic_slice(cotangent, (0, core * half), (rows, half))
    partner_cot = to_partner(lax.dynamic_slice(cotangent, (0, (1 - core) * half), (rows, half)))

    peers = jnp.arange(n_dp, dtype=jnp.int32)
    match = owner[None, :] == peers[:, None]
    listed = chosen_slots[0].reshape(1, blocks, block) + 1
    token = jnp.sum(jnp.where(match[:, :, None], listed, 0), axis=1).reshape(-1) - 1
    gates = jax.nn.sigmoid(router_logits).astype(jnp.bfloat16)
    lane = lax.broadcasted_iota(jnp.int32, (tokens, EXTRA), 1)
    extra = jnp.where(lane == 0, gates[:, None], (lane == 1).astype(jnp.bfloat16))
    send = pick_rows(token, head_output, extra).reshape(n_dp, block, width + EXTRA)
    got = lax.all_to_all(send, "dp", split_axis=0, concat_axis=0, tiled=True)

    incoming = (got[:, 0, width + 1] > 0.5).astype(jnp.int32)
    position = jnp.cumsum(incoming) - 1
    ids = jnp.arange(receive, dtype=jnp.int32)
    source = jnp.sum(
        jnp.where((position[None, :] == ids[:, None]) & (incoming[None, :] > 0), peers[None, :], 0),
        axis=1,
    )
    held = move_blocks(got, source, width + EXTRA).reshape(rows, width + EXTRA)

    both = jnp.concatenate([held, to_partner(held)], axis=0)
    both_cot = jnp.concatenate([own_cot, partner_cot], axis=0)
    gate = both[:, width].astype(jnp.float32)
    weighted = (gate[:, None] * both_cot.astype(jnp.float32)).astype(jnp.bfloat16)
    both_rows = both[:, :width]
    part = half // (2 * side)
    cut = width // 2

    def term(first, index):
        columns = lax.dynamic_slice(weighted, (0, first + index % side * part), (2 * rows, part))
        product = lax.dot_general(
            both_rows, columns, (((0,), (0,)), ((), ())), preferred_element_type=jnp.float32
        )
        return product * scale

    def wide(value):
        return value.astype(jnp.float32)

    def narrow(value):
        return value.astype(jnp.bfloat16)

    far_y, far_z = narrow(term(0, y + 2)), narrow(term(half // 2, z + 2))
    up_y, up_z = along_y(far_y[:cut], 1), along_z(far_z[:cut], 1)
    down_y, down_z = along_y(far_y[cut:], -1), along_z(far_z[cut:], -1)

    def onward(value, got, upper):
        if upper:
            return narrow(jnp.concatenate([value[:cut] + wide(got), value[cut:]], axis=0))
        return narrow(jnp.concatenate([value[:cut], value[cut:] + wide(got)], axis=0))

    from_y = along_y(onward(term(0, y + 1), up_y, True), 1)
    from_z = along_z(onward(term(half // 2, z + 1), up_z, True), 1)
    to_y = along_y(onward(term(0, y + side - 1), down_y, False), -1)
    to_z = along_z(onward(term(half // 2, z + side - 1), down_z, False), -1)
    sum_y = narrow(term(0, y) + wide(from_y) + wide(to_y))
    sum_z = narrow(term(half // 2, z) + wide(from_z) + wide(to_z))

    share = shard // side

    def exchange(value, axis, place, along):
        count = value.shape[axis]
        total = wide(at(value, place, axis))
        for ahead in range(1, count):
            total += wide(along(at(value, (place + ahead) % count, axis), ahead))
        return narrow(total)

    sum_y = exchange(sum_y.reshape(n_fsdp, side, share, part), 1, z, along_z)
    sum_z = exchange(sum_z.reshape(n_fsdp, side, share, part), 1, y, along_y)
    sums = jnp.stack([sum_y, sum_z]).reshape(2, chips, 2, share, part)
    sums = exchange(sums, 1, chip, along_x)
    keep, take = at(sums, core, 1), to_partner(at(sums, 1 - core, 1))
    first = core == 0
    piece = jnp.stack([jnp.where(first, keep, take), jnp.where(first, take, keep)])
    pieces = lax.all_to_all(
        jnp.broadcast_to(piece[None], (n_dp,) + piece.shape), "dp", split_axis=0, concat_axis=0, tiled=True
    )
    grad_weight = place_blocks(pieces.reshape((side, side) + piece.shape))

    update, grads = project(held, cotangent, places, weights)
    back = move_blocks(
        grads.reshape(receive, block, width + EXTRA), jnp.clip(position, 0, receive - 1), width + EXTRA
    )
    returned = lax.all_to_all(back, "dp", split_axis=0, concat_axis=0, tiled=True)
    grad_context = move_blocks(returned, owner, width).reshape(slots, width)
    logit_blocks = returned[:, :, width]
    grad_logit = jnp.sum(jnp.where(match[:, :, None], logit_blocks[:, None, :], 0), axis=0).reshape(-1)
    return (update, grad_context, narrow(grad_logit), grad_weight)


def solution(mesh):
    placed = (
        P(("dp", "fsdp"), None),
        P(("dp", "fsdp")),
        P(("dp", "fsdp"), None),
        P(("dp", "fsdp"), None),
        P("fsdp", None),
        P(("dp", "fsdp"), None),
    )
    return jax.shard_map(
        on_device,
        mesh=mesh,
        in_specs=placed,
        out_specs=(
            P(("dp", "fsdp"), None),
            P(("dp", "fsdp"), None),
            P(("dp", "fsdp")),
            P("fsdp", None),
        ),
        check_vma=False,
    )
```

time: 349 us -> 261 us (0.75); the launches traced: 343 us -> 260 us
  matrix products: 67 us -> 10.2 us
  waiting for transfers between devices: 180 us -> 126 us
  Pallas kernels: 0 us -> 41.4 us
  starting transfers between devices: 14.9 us -> 50.5 us
  blocking collectives: 22.1 us -> 0 us
  local copies, waits for them, and re-layouts: 33.7 us -> 15.5 us
  between operations: 14.1 us -> 1.09 us
    reduce_scatter x1 -> x0, waiting for transfers between devices: 74.6 us -> none  [on_device(): lax.psum_scatter((lax.dot_general(picked_rows, term_weighted, (((0,), (0,...]
    ppermute x0 -> x29, waiting for transfers between devices: none -> 71.6 us  [the longest x7 32.7 us: along_z(): lax.ppermute(value, 'dp', [(d, d // side * side + (d + ahead) % side) for...]
    psum x1 -> x0, waiting for transfers between devices: 69.3 us -> none  [on_device(): grad_weight = lax.psum(partial_sum, 'dp').astype(jnp.float32)]
    dot_general x7 -> x8, matrix products: 67 us -> 10.2 us  [term(): lax.dot_general(both_rows, columns, (((0,), (0,)), ((), ())), preferred_e...]
    pallas_call x0 -> x6, Pallas kernels: none -> 41.4 us  [the longest x1 16.7 us: project(): pl.pallas_call(lambda *refs: project_body(shards, width, *refs), out_shap...]
    ppermute x0 -> x29, starting transfers between devices: none -> 31.5 us  [the longest x7 11 us: along_y(): lax.ppermute(value, 'dp', [(d, (d + side * ahead) % n_dp) for d in range(...]
    all_gather x1 -> x0, blocking collectives: 22.1 us -> none  [on_device(): routing = lax.all_gather(block_owner, 'dp', axis=0, tiled=True)]
    all_to_all x2 -> x3, waiting for transfers between devices: 35.4 us -> 54.8 us  [the longest x1 28.7 us: on_device(): got = lax.all_to_all(send, 'dp', split_axis=0, concat_axis=0, tiled=True)]
  transfers between devices with their start and end apart: 5 -> 32, of which waited for: 3 -> 14; matrix products, arithmetic and copies ran while one was open for 20% -> 12% of each run, Pallas kernels for 0% -> 10%
where the time goes in v1:
time: 261 us; the launch traced here: 260 us
  waiting for transfers between devices  126 us (48%)
  starting transfers between devices  50.5 us (19%)
  Pallas kernels  41.4 us (16%)
  local copies, waits for them, and re-layouts  15.5 us (6%)
  other arithmetic  14.5 us (6%)
  matrix products  10.2 us (4%)
    ppermute x7, waiting for transfers between devices, along_z(): lax.ppermute(value, 'dp', [(d, d // side * side + (d + ahead) % side) for...  32.7 us
    all_to_all x1, waiting for transfers between devices, on_device(): got = lax.all_to_all(send, 'dp', split_axis=0, concat_axis=0, tiled=True)  28.7 us
    all_to_all x1, waiting for transfers between devices, on_device(): lax.all_to_all(jnp.broadcast_to(piece[None], (n_dp,) + piece.shape), 'dp'...  26.1 us
    ppermute x7, waiting for transfers between devices, along_x(): lax.ppermute(value, 'fsdp', [(f, (f + 2 * ahead) % n_fsdp) for f in range...  24.6 us
    pallas_call x1, Pallas kernels, project(): pl.pallas_call(lambda *refs: project_body(shards, width, *refs), out_shap...  16.7 us
    ppermute x7, waiting for transfers between devices, along_y(): lax.ppermute(value, 'dp', [(d, (d + side * ahead) % n_dp) for d in range(...  13.1 us
    pallas_call x1, Pallas kernels, pick_rows(): pl.pallas_call(lambda *refs: pick_body(width, *refs), out_shape=jax.Shape...  11.5 us
    ppermute x7, starting transfers between devices, along_y(): lax.ppermute(value, 'dp', [(d, (d + side * ahead) % n_dp) for d in range(...  11 us
  transfers between devices with their start and end apart: 32, of which 14 were waited for; matrix products, arithmetic and copies ran while one was open for 12% of the time, Pallas kernels for 10%

profile of v1, /device:TPU:0, one launch (start us, length us, event | category | flops | bytes accessed | tf_op | source)
XLA Modules:
  0.0 259.6 jit_solution(16873927440291088517)
XLA Ops:
  5.0 11.5 %pick_rows.1 = bf16[512,2176]{1,0:T(8,128)(2,1)} custom-call(s32[512,1]{1,0:T(8,128)} %sub.54.refs_0_, bf16[2048,2048]{1,0:T(8,128)(2,1)} %refs_1_.1, bf16[2048,128]{1,0:T(8,128)(2,1)} %broadcast_select_fusion.refs_2_), custom_call_target="tpu_custom_call" | custom-call | flops 4294967296 | bytes 10485760 | tf_op jit(solution)/shard_map/pick_rows/pallas_call | solution.py:39
  16.5 8.1 %all-to-all-start = ((bf16[16,32,2176]{2,1,0:T(8,128)(2,1)}), bf16[16,32,2176]{2,1,0:T(8,128)(2,1)S(1)}, u32[]{:S(2)}, u32[]{:S(2)}) async-start(bf16[16,32,2176]{2,1,0:T(8,128)(2,1)} %bitcast.79), calls=%async_computation | async-start | bytes 4456448 | tf_op jit(solution)/shard_map/all_to_all | solution.py:277
  27.9 28.7 %all-to-all-done.refs_1_ = bf16[16,32,2176]{2,1,0:T(8,128)(2,1)S(1)} async-done(((bf16[16,32,2176]{2,1,0:T(8,128)(2,1)}), bf16[16,32,2176]{2,1,0:T(8,128)(2,1)S(1)}, u32[]{:S(2)}, u32[]{:S(2)}) %all-to-all-start) | async-done | bytes 2228256 | tf_op jit(solution)/shard_map/all_to_all | solution.py:277
  58.0 2.8 %move_blocks.3 = bf16[8,32,2176]{2,1,0:T(8,128)(2,1)} custom-call(s32[8]{0:T(128)} %select_reduce_fusion.2.refs_0_, bf16[16,32,2176]{2,1,0:T(8,128)(2,1)} %copy-done.3), custom_call_target="tpu_custom_call" | custom-call | bytes 2228224 | tf_op jit(solution)/shard_map/move_blocks/pallas_call | solution.py:77
  64.3 9.0 %collective-permute-done.refs_4_ = bf16[256,4096]{1,0:T(8,128)(2,1)} collective-permute-done((bf16[256,4096]{1,0:T(8,128)(2,1)}, bf16[256,4096]{1,0:T(8,128)(2,1)}, u32[]{:S(2)}, u32[]{:S(2)}) %collective-permute-start) | collective-permute-done | bytes 2097184 | tf_op jit(solution)/shard_map/ppermute | solution.py:230
  76.3 3.0 %collective-permute-start.6 = (bf16[256,2048]{1,0:T(8,128)(2,1)S(1)}, bf16[256,2048]{1,0:T(8,128)(2,1)S(1)}, u32[]{:S(2)}, u32[]{:S(2)}) collective-permute-start(bf16[256,2048]{1,0:T(8,128)(2,1)S(1)} %slice.78), channel_id=1, source_target_pairs={{0,6},{1,7},{2,0},{3,1},{4,2},{5,3},{6,4},{7,5},{8,14},{9,15},{10,... | collective-permute-start | bytes 3145736 | tf_op jit(solution)/shard_map/ppermute | solution.py:230
  83.8 3.0 %collective-permute-start.13 = (bf16[1024,256]{1,0:T(8,128)(2,1)S(1)}, bf16[1024,256]{1,0:T(8,128)(2,1)S(1)}, u32[]{:S(2)}, u32[]{:S(2)}) collective-permute-start(bf16[1024,256]{1,0:T(8,128)(2,1)S(1)} %get-tuple-element.21), channel_id=1, source_target_pairs={{0,96},{8,104},{16,112},{24,120},{32,0},{40,8},{48,16},{56,24},{64... | collective-permute-start | bytes 1572872 | tf_op jit(solution)/shard_map/ppermute | solution.py:233
  90.3 9.3 %collective-permute-done.5.refs_9_ = bf16[256,2048]{1,0:T(8,128)(2,1)S(1)} collective-permute-done((bf16[256,2048]{1,0:T(8,128)(2,1)S(1)}, bf16[256,2048]{1,0:T(8,128)(2,1)S(1)}, u32[]{:S(2)}, u32[]{:S(2)}) %collective-permute-start.5) | collective-permute-done | bytes 1048608 | tf_op jit(solution)/shard_map/ppermute | solution.py:230
  101.2 2.7 %collective-permute-start.20 = (bf16[1024,256]{1,0:T(8,128)(2,1)S(1)}, bf16[1024,256]{1,0:T(8,128)(2,1)S(1)}, u32[]{:S(2)}, u32[]{:S(2)}) collective-permute-start(bf16[1024,256]{1,0:T(8,128)(2,1)S(1)} %get-tuple-element.16), channel_id=1, source_target_pairs={{0,24},{8,0},{16,8},{24,16},{32,56},{40,32},{48,40},{56,48},{64,88... | collective-permute-start | bytes 1572872 | tf_op jit(solution)/shard_map/ppermute | solution.py:236
  104.0 11.2 %collective-permute-done.11 = bf16[1024,256]{1,0:T(8,128)(2,1)S(1)} collective-permute-done((bf16[1024,256]{1,0:T(8,128)(2,1)S(1)}, bf16[1024,256]{1,0:T(8,128)(2,1)S(1)}, u32[]{:S(2)}, u32[]{:S(2)}) %collective-permute-start.11) | collective-permute-done | bytes 524320 | tf_op jit(solution)/shard_map/ppermute | solution.py:233
  117.7 12.2 %collective-permute-done.18 = bf16[1024,256]{1,0:T(8,128)(2,1)S(1)} collective-permute-done((bf16[1024,256]{1,0:T(8,128)(2,1)S(1)}, bf16[1024,256]{1,0:T(8,128)(2,1)S(1)}, u32[]{:S(2)}, u32[]{:S(2)}) %collective-permute-start.18) | collective-permute-done | bytes 524320 | tf_op jit(solution)/shard_map/ppermute | solution.py:236
  137.6 16.7 %project.1 = (bf16[256,4096]{1,0:T(8,128)(2,1)}, bf16[256,2176]{1,0:T(8,128)(2,1)}) custom-call(s32[8]{0:T(128)} %stack.53.refs_0_, bf16[256,2176]{1,0:T(8,128)(2,1)} %bitcast.72, bf16[256,4096]{1,0:T(8,128)(2,1)} %refs_2_.1, bf16[256,4096]{1,0:T(8,128)(2,1)} %refs_3_.1, bf16[256,4096]{1,0:T(8,128)(2,1)} %collective-permute-done.refs_4_, ...), custom_call_target="tpu_custom_call" | custom-call | flops 8589934592 | bytes 23199744 | tf_op jit(solution)/shard_map/project/pallas_call | solution.py:153
  154.3 3.0 %move_blocks.4 = bf16[16,32,2176]{2,1,0:T(8,128)(2,1)} custom-call(s32[16]{0:T(128)} %broadcast_clamp_fusion.refs_0_, bf16[8,32,2176]{2,1,0:T(8,128)(2,1)} %bitcast.81), custom_call_target="tpu_custom_call" | custom-call | bytes 4456448 | tf_op jit(solution)/shard_map/move_blocks/pallas_call | solution.py:77
  157.3 5.5 %all-to-all-start.1 = ((bf16[16,32,2176]{2,1,0:T(8,128)(2,1)}), bf16[16,32,2176]{2,1,0:T(8,128)(2,1)S(1)}, u32[]{:S(2)}, u32[]{:S(2)}) async-start(bf16[16,32,2176]{2,1,0:T(8,128)(2,1)} %move_blocks.4), calls=%async_computation.1 | async-start | bytes 4456448 | tf_op jit(solution)/shard_map/all_to_all | solution.py:350
  162.9 3.2 %fusion.7 = bf16[2048,256]{1,0:T(8,128)(2,1)S(1)} fusion(bf16[512,2048]{1,0:T(8,128)(2,1)} %copy-done.4, bf16[2048,256]{1,0:T(8,128)(2,1)} %collective-permute-done.14, bf16[2048,256]{1,0:T(8,128)(2,1)} %collective-permute-done.12, bf16[512,2048]{1,0:T(8,128)(2,1)} %copy-done.6, s32[]{:T(128)S(6)} %select_n.197), kind=kOutput, calls=%fused_computation.16 | convolution fusion | flops 540016640 | bytes 5505028 | tf_op jit(solution)/shard_map/dot_general | solution.py:298
  166.8 3.1 %collective-permute-start.17 = (bf16[8,64,256]{2,1,0:T(8,128)(2,1)S(1)}, bf16[8,64,256]{2,1,0:T(8,128)(2,1)}, u32[]{:S(2)}, u32[]{:S(2)}) collective-permute-start(bf16[8,64,256]{2,1,0:T(8,128)(2,1)S(1)} %get-tuple-element.18), channel_id=1, source_target_pairs={{0,24},{8,0},{16,8},{24,16},{32,56},{40,32},{48,40},{56,48},{64,88... | collective-permute-start | bytes 786440 | tf_op jit(solution)/shard_map/ppermute | solution.py:236
  176.1 2.7 %collective-permute-start.24 = (bf16[8,64,256]{2,1,0:T(8,128)(2,1)}, bf16[8,64,256]{2,1,0:T(8,128)(2,1)}, u32[]{:S(2)}, u32[]{:S(2)}) collective-permute-start(bf16[8,64,256]{2,1,0:T(8,128)(2,1)} %get-tuple-element.13), channel_id=1, source_target_pairs={{0,96},{8,104},{16,112},{24,120},{32,0},{40,8},{48,16},{56,24},{64... | collective-permute-start | bytes 786440 | tf_op jit(solution)/shard_map/ppermute | solution.py:233
  179.6 16.8 %collective-permute-done.17 = bf16[8,64,256]{2,1,0:T(8,128)(2,1)} collective-permute-done((bf16[8,64,256]{2,1,0:T(8,128)(2,1)S(1)}, bf16[8,64,256]{2,1,0:T(8,128)(2,1)}, u32[]{:S(2)}, u32[]{:S(2)}) %collective-permute-start.17) | collective-permute-done | bytes 262176 | tf_op jit(solution)/shard_map/ppermute | solution.py:236
  198.6 2.5 collective-permute-done.15
  207.8 2.9 %collective-permute-done.27 = bf16[2,2,64,256]{3,2,1,0:T(8,128)(2,1)S(1)} collective-permute-done((bf16[2,2,64,256]{3,2,1,0:T(8,128)(2,1)S(1)}, bf16[2,2,64,256]{3,2,1,0:T(8,128)(2,1)S(1)}, u32[]{:S(2)}, u32[]{:S(2)}) %collective-permute-start.27) | collective-permute-done | bytes 131104 | tf_op jit(solution)/shard_map/ppermute | solution.py:230
  217.5 5.4 %all-to-all-start.2 = ((bf16[16,2,2,64,256]{4,3,2,1,0:T(8,128)(2,1)}), bf16[16,2,2,64,256]{4,3,2,1,0:T(8,128)(2,1)S(1)}, u32[]{:S(2)}, u32[]{:S(2)}) async-start(bf16[16,2,2,64,256]{4,3,2,1,0:T(8,128)(2,1)} %broadcast_in_dim.85), calls=%async_computation.2 | async-start | bytes 4194304 | tf_op jit(solution)/shard_map/all_to_all | solution.py:341
  224.7 3.2 %move_blocks.5 = bf16[16,32,2048]{2,1,0:T(8,128)(2,1)} custom-call(s32[16]{0:T(128)} %bitcast.88, bf16[16,32,2176]{2,1,0:T(8,128)(2,1)} %copy-done.2), custom_call_target="tpu_custom_call" | custom-call | bytes 4194304 | tf_op jit(solution)/shard_map/move_blocks/pallas_call | solution.py:77
  228.0 26.1 %all-to-all-done.2 = bf16[16,2,2,64,256]{4,3,2,1,0:T(8,128)(2,1)S(1)} async-done(((bf16[16,2,2,64,256]{4,3,2,1,0:T(8,128)(2,1)}), bf16[16,2,2,64,256]{4,3,2,1,0:T(8,128)(2,1)S(1)}, u32[]{:S(2)}, u32[]{:S(2)}) %all-to-all-start.2) | async-done | bytes 2097184 | tf_op jit(solution)/shard_map/all_to_all | solution.py:341
  255.4 4.2 %place_blocks.1 = f32[256,4096]{1,0:T(8,128)} custom-call(bf16[4,4,2,2,64,256]{5,4,3,2,1,0:T(8,128)(2,1)} %bitcast.69, bf16[4,4,2,2,64,256]{5,4,3,2,1,0:T(8,128)(2,1)} %bitcast.70), custom_call_target="tpu_custom_call" | custom-call | bytes 6291456 | tf_op jit(solution)/shard_map/place_blocks/pallas_call | solution.py:201
  (130 shorter events, 61.5 us)
Async XLA Ops:
  16.5 40.1 %all-to-all-start = ((bf16[16,32,2176]{2,1,0:T(8,128)(2,1)}), bf16[16,32,2176]{2,1,0:T(8,128)(2,1)S(1)}, u32[]{:S(2)}, u32[]{:S(2)}) async-start(bf16[16,32,2176]{2,1,0:T(8,128)(2,1)} %bitcast.79), calls=%async_computation | async-start | bytes 4456448 | tf_op jit(solution)/shard_map/all_to_all | solution.py:277
  24.6 48.7 %collective-permute-start = (bf16[256,4096]{1,0:T(8,128)(2,1)}, bf16[256,4096]{1,0:T(8,128)(2,1)}, u32[]{:S(2)}, u32[]{:S(2)}) collective-permute-start(bf16[256,4096]{1,0:T(8,128)(2,1)} %refs_3_.1), channel_id=1, source_target_pairs={{0,2},{1,3},{2,4},{3,5},{4,6},{5,7},{6,0},{7,1},{8,10},{9,11},{10,... | collective-permute-start | bytes 6291464 | tf_op jit(solution)/shard_map/ppermute | solution.py:230
  26.2 48.8 %collective-permute-start.1 = (bf16[256,4096]{1,0:T(8,128)(2,1)}, bf16[256,4096]{1,0:T(8,128)(2,1)}, u32[]{:S(2)}, u32[]{:S(2)}) collective-permute-start(bf16[256,4096]{1,0:T(8,128)(2,1)} %refs_3_.1), channel_id=1, source_target_pairs={{0,6},{1,7},{2,0},{3,1},{4,2},{5,3},{6,4},{7,5},{8,14},{9,15},{10,... | collective-permute-start | bytes 6291464 | tf_op jit(solution)/shard_map/ppermute | solution.py:230
  60.8 18.5 %collective-permute-start.9 = (bf16[256,2176]{1,0:T(8,128)(2,1)}, bf16[256,2176]{1,0:T(8,128)(2,1)S(1)}, u32[]{:S(2)}, u32[]{:S(2)}) collective-permute-start(bf16[256,2176]{1,0:T(8,128)(2,1)} %bitcast.71), channel_id=1, source_target_pairs={{0,1},{1,0},{2,3},{3,2},{4,5},{5,4},{6,7},{7,6},{8,9},{9,8},{10,11... | collective-permute-start | bytes 3342344 | tf_op jit(solution)/shard_map/ppermute | solution.py:241
  62.5 17.3 %collective-permute-start.10 = (bf16[256,2048]{1,0:T(8,128)(2,1)S(1)}, bf16[256,2048]{1,0:T(8,128)(2,1)}, u32[]{:S(2)}, u32[]{:S(2)}) collective-permute-start(bf16[256,2048]{1,0:T(8,128)(2,1)S(1)} %get-tuple-element.11), channel_id=1, source_target_pairs={{0,1},{1,0},{2,3},{3,2},{4,5},{5,4},{6,7},{7,6},{8,9},{9,8},{10,11... | collective-permute-start | bytes 3145736 | tf_op jit(solution)/shard_map/ppermute | solution.py:241
  63.1 68.1 %collective-permute-start.2 = (bf16[256,4096]{1,0:T(8,128)(2,1)}, bf16[256,4096]{1,0:T(8,128)(2,1)}, u32[]{:S(2)}, u32[]{:S(2)}) collective-permute-start(bf16[256,4096]{1,0:T(8,128)(2,1)} %refs_3_.1), channel_id=1, source_target_pairs={{0,1},{1,0},{2,3},{3,2},{4,5},{5,4},{6,7},{7,6},{8,9},{9,8},{10,11... | collective-permute-start | bytes 6291464 | tf_op jit(solution)/shard_map/ppermute | solution.py:241
  74.6 25.0 %collective-permute-start.5 = (bf16[256,2048]{1,0:T(8,128)(2,1)S(1)}, bf16[256,2048]{1,0:T(8,128)(2,1)S(1)}, u32[]{:S(2)}, u32[]{:S(2)}) collective-permute-start(bf16[256,2048]{1,0:T(8,128)(2,1)S(1)} %slice.77), channel_id=1, source_target_pairs={{0,2},{1,3},{2,4},{3,5},{4,6},{5,7},{6,0},{7,1},{8,10},{9,11},{10,... | collective-permute-start | bytes 3145736 | tf_op jit(solution)/shard_map/ppermute | solution.py:230
  76.3 24.9 %collective-permute-start.6 = (bf16[256,2048]{1,0:T(8,128)(2,1)S(1)}, bf16[256,2048]{1,0:T(8,128)(2,1)S(1)}, u32[]{:S(2)}, u32[]{:S(2)}) collective-permute-start(bf16[256,2048]{1,0:T(8,128)(2,1)S(1)} %slice.78), channel_id=1, source_target_pairs={{0,6},{1,7},{2,0},{3,1},{4,2},{5,3},{6,4},{7,5},{8,14},{9,15},{10,... | collective-permute-start | bytes 3145736 | tf_op jit(solution)/shard_map/ppermute | solution.py:230
  79.4 53.0 %collective-permute-start.3 = (bf16[256,4096]{1,0:T(8,128)(2,1)}, bf16[256,4096]{1,0:T(8,128)(2,1)S(1)}, u32[]{:S(2)}, u32[]{:S(2)}) collective-permute-start(bf16[256,4096]{1,0:T(8,128)(2,1)} %collective-permute-done.refs_4_), channel_id=1, source_target_pairs={{0,1},{1,0},{2,3},{3,2},{4,5},{5,4},{6,7},{7,6},{8,9},{9,8},{10,11... | collective-permute-start | bytes 6291464 | tf_op jit(solution)/shard_map/ppermute | solution.py:241
  83.8 15.8 %collective-permute-start.13 = (bf16[1024,256]{1,0:T(8,128)(2,1)S(1)}, bf16[1024,256]{1,0:T(8,128)(2,1)S(1)}, u32[]{:S(2)}, u32[]{:S(2)}) collective-permute-start(bf16[1024,256]{1,0:T(8,128)(2,1)S(1)} %get-tuple-element.21), channel_id=1, source_target_pairs={{0,96},{8,104},{16,112},{24,120},{32,0},{40,8},{48,16},{56,24},{64... | collective-permute-start | bytes 1572872 | tf_op jit(solution)/shard_map/ppermute | solution.py:233
  99.6 34.7 %collective-permute-start.4 = (bf16[256,4096]{1,0:T(8,128)(2,1)}, bf16[256,4096]{1,0:T(8,128)(2,1)S(1)}, u32[]{:S(2)}, u32[]{:S(2)}) collective-permute-start(bf16[256,4096]{1,0:T(8,128)(2,1)} %collective-permute-done.1.refs_5_), channel_id=1, source_target_pairs={{0,1},{1,0},{2,3},{3,2},{4,5},{5,4},{6,7},{7,6},{8,9},{9,8},{10,11... | collective-permute-start | bytes 6291464 | tf_op jit(solution)/shard_map/ppermute | solution.py:241
  101.2 16.4 %collective-permute-start.20 = (bf16[1024,256]{1,0:T(8,128)(2,1)S(1)}, bf16[1024,256]{1,0:T(8,128)(2,1)S(1)}, u32[]{:S(2)}, u32[]{:S(2)}) collective-permute-start(bf16[1024,256]{1,0:T(8,128)(2,1)S(1)} %get-tuple-element.16), channel_id=1, source_target_pairs={{0,24},{8,0},{16,8},{24,16},{32,56},{40,32},{48,40},{56,48},{64,88... | collective-permute-start | bytes 1572872 | tf_op jit(solution)/shard_map/ppermute | solution.py:236
  117.7 18.0 %collective-permute-start.7 = (bf16[256,2048]{1,0:T(8,128)(2,1)S(1)}, bf16[256,2048]{1,0:T(8,128)(2,1)S(1)}, u32[]{:S(2)}, u32[]{:S(2)}) collective-permute-start(bf16[256,2048]{1,0:T(8,128)(2,1)S(1)} %collective-permute-done.5.refs_9_), channel_id=1, source_target_pairs={{0,1},{1,0},{2,3},{3,2},{4,5},{5,4},{6,7},{7,6},{8,9},{9,8},{10,11... | collective-permute-start | bytes 3145736 | tf_op jit(solution)/shard_map/ppermute | solution.py:241
  131.2 31.7 %collective-permute-start.14 = (bf16[2048,256]{1,0:T(8,128)(2,1)S(1)}, bf16[2048,256]{1,0:T(8,128)(2,1)}, u32[]{:S(2)}, u32[]{:S(2)}) collective-permute-start(bf16[2048,256]{1,0:T(8,128)(2,1)S(1)} %pad_maximum_fusion.1), channel_id=1, source_target_pairs={{0,96},{8,104},{16,112},{24,120},{32,0},{40,8},{48,16},{56,24},{64... | collective-permute-start | bytes 3145736 | tf_op jit(solution)/shard_map/ppermute | solution.py:233
  132.3 30.5 %collective-permute-start.12 = (bf16[2048,256]{1,0:T(8,128)(2,1)}, bf16[2048,256]{1,0:T(8,128)(2,1)}, u32[]{:S(2)}, u32[]{:S(2)}) collective-permute-start(bf16[2048,256]{1,0:T(8,128)(2,1)} %pad_maximum_fusion), channel_id=1, source_target_pairs={{0,32},{8,40},{16,48},{24,56},{32,64},{40,72},{48,80},{56,88},{64,... | collective-permute-start | bytes 3145736 | tf_op jit(solution)/shard_map/ppermute | solution.py:233
  134.3 37.4 %collective-permute-start.21 = (bf16[2048,256]{1,0:T(8,128)(2,1)}, bf16[2048,256]{1,0:T(8,128)(2,1)}, u32[]{:S(2)}, u32[]{:S(2)}) collective-permute-start(bf16[2048,256]{1,0:T(8,128)(2,1)} %pad_maximum_fusion.3), channel_id=1, source_target_pairs={{0,24},{8,0},{16,8},{24,16},{32,56},{40,32},{48,40},{56,48},{64,88... | collective-permute-start | bytes 3145736 | tf_op jit(solution)/shard_map/ppermute | solution.py:236
  135.6 36.1 %collective-permute-start.19 = (bf16[2048,256]{1,0:T(8,128)(2,1)}, bf16[2048,256]{1,0:T(8,128)(2,1)}, u32[]{:S(2)}, u32[]{:S(2)}) collective-permute-start(bf16[2048,256]{1,0:T(8,128)(2,1)} %pad_maximum_fusion.2), channel_id=1, source_target_pairs={{0,8},{8,16},{16,24},{24,0},{32,40},{40,48},{48,56},{56,32},{64,72... | collective-permute-start | bytes 3145736 | tf_op jit(solution)/shard_map/ppermute | solution.py:236
  157.3 58.1 %all-to-all-start.1 = ((bf16[16,32,2176]{2,1,0:T(8,128)(2,1)}), bf16[16,32,2176]{2,1,0:T(8,128)(2,1)S(1)}, u32[]{:S(2)}, u32[]{:S(2)}) async-start(bf16[16,32,2176]{2,1,0:T(8,128)(2,1)} %move_blocks.4), calls=%async_computation.1 | async-start | bytes 4456448 | tf_op jit(solution)/shard_map/all_to_all | solution.py:350
  166.8 29.5 %collective-permute-start.17 = (bf16[8,64,256]{2,1,0:T(8,128)(2,1)S(1)}, bf16[8,64,256]{2,1,0:T(8,128)(2,1)}, u32[]{:S(2)}, u32[]{:S(2)}) collective-permute-start(bf16[8,64,256]{2,1,0:T(8,128)(2,1)S(1)} %get-tuple-element.18), channel_id=1, source_target_pairs={{0,24},{8,0},{16,8},{24,16},{32,56},{40,32},{48,40},{56,48},{64,88... | collective-permute-start | bytes 786440 | tf_op jit(solution)/shard_map/ppermute | solution.py:236
  170.0 28.6 %collective-permute-start.16 = (bf16[8,64,256]{2,1,0:T(8,128)(2,1)}, bf16[8,64,256]{2,1,0:T(8,128)(2,1)}, u32[]{:S(2)}, u32[]{:S(2)}) collective-permute-start(bf16[8,64,256]{2,1,0:T(8,128)(2,1)} %get-tuple-element.19), channel_id=1, source_target_pairs={{0,16},{8,24},{16,0},{24,8},{32,48},{40,56},{48,32},{56,40},{64,80... | collective-permute-start | bytes 786440 | tf_op jit(solution)/shard_map/ppermute | solution.py:236
  170.8 30.3 %collective-permute-start.15 = (bf16[8,64,256]{2,1,0:T(8,128)(2,1)S(1)}, bf16[8,64,256]{2,1,0:T(8,128)(2,1)}, u32[]{:S(2)}, u32[]{:S(2)}) collective-permute-start(bf16[8,64,256]{2,1,0:T(8,128)(2,1)S(1)} %get-tuple-element.17), channel_id=1, source_target_pairs={{0,8},{8,16},{16,24},{24,0},{32,40},{40,48},{48,56},{56,32},{64,72... | collective-permute-start | bytes 786440 | tf_op jit(solution)/shard_map/ppermute | solution.py:236
  176.1 26.3 %collective-permute-start.24 = (bf16[8,64,256]{2,1,0:T(8,128)(2,1)}, bf16[8,64,256]{2,1,0:T(8,128)(2,1)}, u32[]{:S(2)}, u32[]{:S(2)}) collective-permute-start(bf16[8,64,256]{2,1,0:T(8,128)(2,1)} %get-tuple-element.13), channel_id=1, source_target_pairs={{0,96},{8,104},{16,112},{24,120},{32,0},{40,8},{48,16},{56,24},{64... | collective-permute-start | bytes 786440 | tf_op jit(solution)/shard_map/ppermute | solution.py:233
  178.8 23.6 %collective-permute-start.23 = (bf16[8,64,256]{2,1,0:T(8,128)(2,1)}, bf16[8,64,256]{2,1,0:T(8,128)(2,1)}, u32[]{:S(2)}, u32[]{:S(2)}) collective-permute-start(bf16[8,64,256]{2,1,0:T(8,128)(2,1)} %get-tuple-element.14), channel_id=1, source_target_pairs={{0,64},{8,72},{16,80},{24,88},{32,96},{40,104},{48,112},{56,120},{... | collective-permute-start | bytes 786440 | tf_op jit(solution)/shard_map/ppermute | solution.py:233
  217.5 36.6 %all-to-all-start.2 = ((bf16[16,2,2,64,256]{4,3,2,1,0:T(8,128)(2,1)}), bf16[16,2,2,64,256]{4,3,2,1,0:T(8,128)(2,1)S(1)}, u32[]{:S(2)}, u32[]{:S(2)}) async-start(bf16[16,2,2,64,256]{4,3,2,1,0:T(8,128)(2,1)} %broadcast_in_dim.85), calls=%async_computation.2 | async-start | bytes 4194304 | tf_op jit(solution)/shard_map/all_to_all | solution.py:341
  (22 other events, 166.0 us)

commit v2 on v1

v2 whole, which is shorter than its diff:
```python
import math

import jax
import jax.numpy as jnp
from jax import lax
from jax.experimental import pallas as pl
from jax.experimental.pallas import tpu as pltpu
from jax.sharding import PartitionSpec as P

EXTRA = 128
MIB = 1024 * 1024
NO_COST = pl.CostEstimate(flops=0, bytes_accessed=0, transcendentals=0)


def params(limit=24):
    return pltpu.CompilerParams(vmem_limit_bytes=limit * MIB)


def after(value, *others):
    return lax.optimization_barrier((value, others))[0]


def pick_body(width, owner_ref, listed_ref, logit_ref, head_ref, out_ref, onehot_ref):
    step = pl.program_id(0)
    columns = head_ref.shape[1]
    rows, count = onehot_ref.shape
    blocks = owner_ref.shape[0]
    block = rows // blocks

    @pl.when(step == 0)
    def _():
        lane = lax.broadcasted_iota(jnp.int32, (block, EXTRA), 1)
        tokens = lax.broadcasted_iota(jnp.int32, (block, count), 1)
        for peer in range(rows // block):
            found = jnp.int32(blocks)
            for b in range(blocks):
                found = jnp.where(owner_ref[b] == peer, b, found)
            there = found < blocks
            start = pl.multiple_of(jnp.minimum(found, blocks - 1) * block, block)
            listed = jnp.where(there, listed_ref[pl.ds(start, block), :], -1)
            hit = listed == tokens
            span = slice(peer * block, (peer + 1) * block)
            onehot_ref[span, :] = hit.astype(jnp.bfloat16)
            logit = jnp.sum(jnp.where(hit, logit_ref[...], 0.0), axis=1, keepdims=True)
            mark = jnp.where(there, 1.0, 0.0)
            out_ref[span, width:] = jnp.where(lane == 0, jax.nn.sigmoid(logit), mark).astype(jnp.bfloat16)

    out_ref[:, pl.ds(pl.multiple_of(step * columns, columns), columns)] = jnp.dot(
        onehot_ref[...], head_ref[...], preferred_element_type=jnp.float32
    ).astype(jnp.bfloat16)


def pick_rows(owner, listed, logits, head):
    rows = listed.shape[0]
    count, width = head.shape
    columns = 512
    return pl.pallas_call(
        lambda *refs: pick_body(width, *refs),
        out_shape=jax.ShapeDtypeStruct((rows, width + EXTRA), jnp.bfloat16),
        grid=(width // columns,),
        in_specs=[
            pl.BlockSpec(memory_space=pltpu.SMEM),
            pl.BlockSpec((rows, 1), lambda n: (0, 0)),
            pl.BlockSpec((1, count), lambda n: (0, 0)),
            pl.BlockSpec((count, columns), lambda n: (0, n)),
        ],
        out_specs=pl.BlockSpec((rows, width + EXTRA), lambda n: (0, 0)),
        scratch_shapes=[pltpu.VMEM((rows, count), jnp.bfloat16)],
        compiler_params=params(56),
        cost_estimate=NO_COST,
        name="pick_rows",
    )(owner, listed, logits, head)


def move_body(width, index_ref, source_ref, out_ref):
    blocks = source_ref.shape[0]
    for slot in range(out_ref.shape[0]):
        block = index_ref[slot]

        @pl.when(block < blocks)
        def _():
            out_ref[slot] = source_ref[jnp.minimum(block, blocks - 1), :, :width]

        @pl.when(block >= blocks)
        def _():
            out_ref[slot] = jnp.zeros(out_ref.shape[1:], out_ref.dtype)


def move_blocks(source, index, width):
    blocks, rows, _ = source.shape
    copies = index.shape[0]
    return pl.pallas_call(
        lambda *refs: move_body(width, *refs),
        out_shape=jax.ShapeDtypeStruct((copies, rows, width), source.dtype),
        in_specs=[
            pl.BlockSpec(memory_space=pltpu.SMEM),
            pl.BlockSpec(memory_space=pltpu.VMEM),
        ],
        out_specs=pl.BlockSpec(memory_space=pltpu.VMEM),
        compiler_params=params(),
        cost_estimate=NO_COST,
        name="move_blocks",
    )(index, source)


def project_body(width, slot_ref, rows_ref, weight_ref, cot_ref, update_ref, back_ref, total_ref, inner_ref):
    step, steps = pl.program_id(0), pl.num_programs(0)

    @pl.when(step == 0)
    def _():
        total_ref[...] = jnp.zeros_like(total_ref)
        inner_ref[...] = jnp.zeros_like(inner_ref)

    weight = weight_ref[...]
    gate = rows_ref[:, width : width + 1].astype(jnp.float32)
    projected = jnp.dot(rows_ref[:, :width], weight, preferred_element_type=jnp.float32)
    update_ref[...] = (gate * projected).astype(jnp.bfloat16)
    cot = cot_ref[...].astype(jnp.float32)
    inner_ref[...] += cot * projected
    weighted = (gate * cot).astype(jnp.bfloat16)
    total_ref[...] += lax.dot_general(
        weighted, weight, (((1,), (1,)), ((), ())), preferred_element_type=jnp.float32
    )

    @pl.when(step == steps - 1)
    def _():
        inner = jnp.sum(inner_ref[...], axis=1, keepdims=True)
        inner_ref[:, :EXTRA] = jnp.broadcast_to(gate * (1.0 - gate) * inner, (gate.shape[0], EXTRA))
        block = back_ref.shape[1]
        for peer in range(back_ref.shape[0]):
            start = pl.multiple_of(slot_ref[peer] * block, block)
            back_ref[peer, :, :width] = total_ref[pl.ds(start, block), :].astype(jnp.bfloat16)
            back_ref[peer, :, width:] = inner_ref[pl.ds(start, block), :EXTRA].astype(jnp.bfloat16)


def project(rows, weight, cotangent, slots, block):
    count, wide = rows.shape
    width, model = weight.shape
    columns = 512
    return pl.pallas_call(
        lambda *refs: project_body(width, *refs),
        out_shape=(
            jax.ShapeDtypeStruct((count, model), jnp.bfloat16),
            jax.ShapeDtypeStruct((slots.shape[0], block, wide), jnp.bfloat16),
        ),
        grid=(model // columns,),
        in_specs=[
            pl.BlockSpec(memory_space=pltpu.SMEM),
            pl.BlockSpec((count, wide), lambda n: (0, 0)),
            pl.BlockSpec((width, columns), lambda n: (0, n)),
            pl.BlockSpec((count, columns), lambda n: (0, n)),
        ],
        out_specs=(
            pl.BlockSpec((count, columns), lambda n: (0, n)),
            pl.BlockSpec((slots.shape[0], block, wide), lambda n: (0, 0, 0)),
        ),
        scratch_shapes=[
            pltpu.VMEM((count, width), jnp.float32),
            pltpu.VMEM((count, columns), jnp.float32),
        ],
        compiler_params=params(56),
        cost_estimate=NO_COST,
        name="project",
    )(slots, rows, weight, cotangent)


def place_body(side, spot_ref, *refs):
    out_ref = refs[-1]
    rows, columns = refs[0].shape[2:]
    across = out_ref.shape[1] // 2
    for which in range(2):
        line, cross = spot_ref[1 - which], spot_ref[which]
        for j in range(side):
            array = refs[which * side + j]
            place = (cross - j + side) % side * columns + which * across
            for k in range(side):
                top = (line - k + side) % side * rows
                out_ref[pl.ds(pl.multiple_of(top, rows), rows), pl.ds(pl.multiple_of(place, columns), columns)] = array[
                    k, 0
                ].astype(jnp.float32)


def place_blocks(spot, first, second):
    side, halves, rows, columns = first[0].shape
    model = halves * 2 * side * columns
    block = pl.BlockSpec((side, 1, rows, columns), lambda h: (0, h, 0, 0))
    return pl.pallas_call(
        lambda *refs: place_body(side, *refs),
        out_shape=jax.ShapeDtypeStruct((side * rows, model), jnp.float32),
        grid=(halves,),
        in_specs=[pl.BlockSpec(memory_space=pltpu.SMEM)] + [block] * (2 * side),
        out_specs=pl.BlockSpec((side * rows, model // halves), lambda h: (0, h)),
        compiler_params=params(),
        cost_estimate=NO_COST,
        name="place_blocks",
    )(spot, *first, *second)


def at(array, index, axis=0):
    return lax.dynamic_index_in_dim(array, index, axis, keepdims=False)


def on_device(head_output, router_logits, chosen_slots, block_owner, out_weight, cotangent):
    n_dp, n_fsdp = lax.axis_size("dp"), lax.axis_size("fsdp")
    dp, fsdp = lax.axis_index("dp"), lax.axis_index("fsdp")
    side, chips = math.isqrt(n_dp), n_fsdp // 2
    y, z = dp // side, dp % side
    chip, core = fsdp // 2, fsdp % 2

    def along_x(value, ahead):
        return lax.ppermute(value, "fsdp", [(f, (f + 2 * ahead) % n_fsdp) for f in range(n_fsdp)])

    def along_y(value, ahead):
        return lax.ppermute(value, "dp", [(d, (d + side * ahead) % n_dp) for d in range(n_dp)])

    def along_z(value, ahead):
        return lax.ppermute(
            value, "dp", [(d, d // side * side + (d + ahead) % side) for d in range(n_dp)]
        )

    def to_partner(value):
        return lax.ppermute(value, "fsdp", [(f, f ^ 1) for f in range(n_fsdp)])

    slots = chosen_slots.shape[1]
    blocks = block_owner.shape[1]
    block = slots // blocks
    tokens, width = head_output.shape
    shard, model = out_weight.shape
    rows = cotangent.shape[0]
    receive = rows // block
    scale = 1.0 / math.sqrt(rows * n_dp * n_fsdp)
    half = model // 2
    owner = block_owner[0]

    weight = lax.all_gather(out_weight, "fsdp", axis=0, tiled=True)

    own_cot = lax.dynamic_slice(cotangent, (0, core * half), (rows, half))
    partner_cot = to_partner(lax.dynamic_slice(cotangent, (0, (1 - core) * half), (rows, half)))

    peers = jnp.arange(n_dp, dtype=jnp.int32)
    match = owner[None, :] == peers[:, None]
    send = pick_rows(owner, chosen_slots.reshape(slots, 1), router_logits.reshape(1, tokens), head_output)
    send = send.reshape(n_dp, block, width + EXTRA)
    got = lax.all_to_all(send, "dp", split_axis=0, concat_axis=0, tiled=True)

    got = after(got, partner_cot)
    incoming = (got[:, 0, width + 1] > 0.5).astype(jnp.int32)
    position = jnp.cumsum(incoming) - 1
    ids = jnp.arange(receive, dtype=jnp.int32)
    source = jnp.sum(
        jnp.where((position[None, :] == ids[:, None]) & (incoming[None, :] > 0), peers[None, :], 0),
        axis=1,
    )
    held = move_blocks(got, source, width + EXTRA).reshape(rows, width + EXTRA)

    both = jnp.concatenate([held, to_partner(held)], axis=0)
    both_cot = jnp.concatenate([own_cot, partner_cot], axis=0)
    gate = both[:, width].astype(jnp.float32)
    weighted = (gate[:, None] * both_cot.astype(jnp.float32)).astype(jnp.bfloat16)
    both_rows = both[:, :width]
    part = half // (2 * side)
    cut = width // 2

    def term(first, index):
        columns = lax.dynamic_slice(weighted, (0, first + index % side * part), (2 * rows, part))
        product = lax.dot_general(
            both_rows, columns, (((0,), (0,)), ((), ())), preferred_element_type=jnp.float32
        )
        return product * scale

    def wide(value):
        return value.astype(jnp.float32)

    def narrow(value):
        return value.astype(jnp.bfloat16)

    far_y, far_z = narrow(term(0, y + 2)), narrow(term(half // 2, z + 2))
    got_parts = (
        along_y(far_y[:cut], 1), along_z(far_z[:cut], 1), along_y(far_y[cut:], -1), along_z(far_z[cut:], -1)
    )
    ahead_y, ahead_z = term(0, y + 1), term(half // 2, z + 1)
    behind_y, behind_z = term(0, y + side - 1), term(half // 2, z + side - 1)
    got_parts = after(got_parts, ahead_y, ahead_z, behind_y, behind_z)
    low_y, low_z, high_y, high_z = [wide(part_sum) for part_sum in got_parts]
    sent = (
        narrow(jnp.concatenate([ahead_y[:cut] + low_y, ahead_y[cut:]], axis=0)),
        narrow(jnp.concatenate([ahead_z[:cut] + low_z, ahead_z[cut:]], axis=0)),
        narrow(jnp.concatenate([behind_y[:cut], behind_y[cut:] + high_y], axis=0)),
        narrow(jnp.concatenate([behind_z[:cut], behind_z[cut:] + high_z], axis=0)),
    )
    from_y, from_z = along_y(sent[0], 1), along_z(sent[1], 1)
    to_y, to_z = along_y(sent[2], -1), along_z(sent[3], -1)

    slot = after(jnp.clip(position, 0, receive - 1), sent)
    update, back = project(held, weight, cotangent, slot, block)
    returned = lax.all_to_all(back, "dp", split_axis=0, concat_axis=0, tiled=True)
    from_y, to_y, from_z, to_z = after((from_y, to_y, from_z, to_z), back)

    sum_y = narrow(term(0, y) + wide(from_y) + wide(to_y))
    sum_z = narrow(term(half // 2, z) + wide(from_z) + wide(to_z))

    share = shard // side

    def exchange(value, axis, place, along):
        count = value.shape[axis]
        total = wide(at(value, place, axis))
        for ahead in range(1, count):
            total += wide(along(at(value, (place + ahead) % count, axis), ahead))
        return narrow(total)

    sum_y = exchange(sum_y.reshape(n_fsdp, side, share, part), 1, z, along_z)
    sum_z = exchange(sum_z.reshape(n_fsdp, side, share, part), 1, y, along_y)
    sums = jnp.stack([sum_y, sum_z]).reshape(2, chips, 2, share, part)
    sums = exchange(after(sums, returned), 1, chip, along_x)
    keep, take = at(sums, core, 1), to_partner(at(sums, 1 - core, 1))
    first = core == 0
    piece = jnp.stack([jnp.where(first, keep, take), jnp.where(first, take, keep)])

    def around(value, along):
        return [value] + [along(value, ahead) for ahead in range(1, side)]

    line_z = jnp.stack(around(piece[:, 0], along_z))
    line_y = jnp.stack(around(piece[:, 1], along_y))
    spot = jnp.stack([y, z]).astype(jnp.int32)
    grad_weight = place_blocks(spot, around(line_z, along_y), around(line_y, along_z))

    grad_context = move_blocks(returned, owner, width).reshape(slots, width)
    logit_blocks = returned[:, :, width]
    grad_logit = jnp.sum(jnp.where(match[:, :, None], logit_blocks[:, None, :], 0), axis=0).reshape(-1)
    return (update, grad_context, narrow(grad_logit), grad_weight)


def solution(mesh):
    placed = (
        P(("dp", "fsdp"), None),
        P(("dp", "fsdp")),
        P(("dp", "fsdp"), None),
        P(("dp", "fsdp"), None),
        P("fsdp", None),
        P(("dp", "fsdp"), None),
    )
    return jax.shard_map(
        on_device,
        mesh=mesh,
        in_specs=placed,
        out_specs=(
            P(("dp", "fsdp"), None),
            P(("dp", "fsdp"), None),
            P(("dp", "fsdp")),
            P("fsdp", None),
        ),
        check_vma=False,
    )
```

time: 261 us -> 218 us (0.84)
  waiting for transfers between devices: 126 us -> 76 us
  starting transfers between devices: 50.5 us -> 64.8 us
  between operations: 1.09 us -> 14.8 us
  Pallas kernels: 41.4 us -> 32.8 us
  local copies, waits for them, and re-layouts: 15.5 us -> 8.42 us
  other arithmetic: 14.5 us -> 10.2 us
    all_to_all x1 -> x0, waiting for transfers between devices: 26.1 us -> none  [on_device(): lax.all_to_all(jnp.broadcast_to(piece[None], (n_dp,) + piece.shape), 'dp'...]
    ppermute x7 -> x3, waiting for transfers between devices: 24.6 us -> 3.73 us  [along_x(): lax.ppermute(value, 'fsdp', [(f, (f + 2 * ahead) % n_fsdp) for f in range...]
    ppermute x7 -> x13, starting transfers between devices: 11 us -> 23.1 us  [along_y(): lax.ppermute(value, 'dp', [(d, (d + side * ahead) % n_dp) for d in range(...]
    ppermute x7 -> x13, starting transfers between devices: 10.9 us -> 21.4 us  [along_z(): lax.ppermute(value, 'dp', [(d, d // side * side + (d + ahead) % side) for...]
    pallas_call x3 -> x2, Pallas kernels: 9.05 us -> 2.88 us  [move_blocks(): pl.pallas_call(lambda *refs: move_body(width, *refs), out_shape=jax.Shape...]
    ppermute x8 -> x3, waiting for transfers between devices: 1.25 us -> 6.98 us  [to_partner(): return lax.ppermute(value, 'fsdp', [(f, f ^ 1) for f in range(n_fsdp)])]
    all_to_all x1 -> x0, starting transfers between devices: 5.38 us -> none  [on_device(): lax.all_to_all(jnp.broadcast_to(piece[None], (n_dp,) + piece.shape), 'dp'...]
    ppermute x7 -> x13, waiting for transfers between devices: 13.1 us -> 8.48 us  [along_y(): lax.ppermute(value, 'dp', [(d, (d + side * ahead) % n_dp) for d in range(...]
  transfers between devices with their start and end apart: 32 -> 35, of which waited for: 14 -> 18; matrix products, arithmetic and copies ran while one was open for 12% -> 12% of each run, Pallas kernels for 10% -> 14%
where the time goes in v2:
time: 218 us; the launch traced here: 217 us
  waiting for transfers between devices  76 us (35%)
  starting transfers between devices  64.8 us (30%)
  Pallas kernels  32.8 us (15%)
  between operations  14.8 us (7%)
  other arithmetic  10.2 us (5%)
  matrix products  10.2 us (5%)
  local copies, waits for them, and re-layouts  8.42 us (4%)
    ppermute x13, waiting for transfers between devices, along_z(): lax.ppermute(value, 'dp', [(d, d // side * side + (d + ahead) % side) for...  29.4 us
    all_to_all x1, waiting for transfers between devices, on_device(): got = lax.all_to_all(send, 'dp', split_axis=0, concat_axis=0, tiled=True)  26.5 us
    ppermute x13, starting transfers between devices, along_y(): lax.ppermute(value, 'dp', [(d, (d + side * ahead) % n_dp) for d in range(...  23.1 us
    ppermute x13, starting transfers between devices, along_z(): lax.ppermute(value, 'dp', [(d, d // side * side + (d + ahead) % side) for...  21.4 us
    pallas_call x1, Pallas kernels, project(): pl.pallas_call(lambda *refs: project_body(width, *refs), out_shape=(jax.S...  15.9 us
    pallas_call x1, Pallas kernels, pick_rows(): pl.pallas_call(lambda *refs: pick_body(width, *refs), out_shape=jax.Shape...  10.8 us
    dot_general x8, matrix products, term(): lax.dot_general(both_rows, columns, (((0,), (0,)), ((), ())), preferred_e...  10.2 us
    ppermute x13, waiting for transfers between devices, along_y(): lax.ppermute(value, 'dp', [(d, (d + side * ahead) % n_dp) for d in range(...  8.48 us
  transfers between devices with their start and end apart: 35, of which 18 were waited for; matrix products, arithmetic and copies ran while one was open for 12% of the time, Pallas kernels for 14%

profile of v2, /device:TPU:0, one launch (start us, length us, event | category | flops | bytes accessed | tf_op | source)
XLA Modules:
  0.0 217.1 jit_solution(272172478814780421)
XLA Ops:
  8.8 10.8 %pick_rows.1 = bf16[512,2176]{1,0:T(8,128)(2,1)} custom-call(s32[16]{0:T(128)} %bitcast.81, s32[512,1]{1,0:T(8,128)} %copy.15.refs_1_, f32[1,2048]{1,0:T(1,128)} %bitcast.99, bf16[2048,2048]{1,0:T(8,128)(2,1)} %refs_3_.2), custom_call_target="tpu_custom_call" | custom-call | tf_op jit(solution)/shard_map/pick_rows/pallas_call | solution.py:57
  19.6 8.1 %all-to-all-start = ((bf16[16,32,2176]{2,1,0:T(8,128)(2,1)}), bf16[16,32,2176]{2,1,0:T(8,128)(2,1)S(1)}, u32[]{:S(2)}, u32[]{:S(2)}) async-start(bf16[16,32,2176]{2,1,0:T(8,128)(2,1)} %bitcast.84), calls=%async_computation | async-start | bytes 4456448 | tf_op jit(solution)/shard_map/all_to_all | solution.py:244
  27.8 2.7 %constant_dynamic-slice_fusion = (bf16[256,2048]{1,0:T(8,128)(2,1)}, bf16[256,2048]{1,0:T(8,128)(2,1)S(1)}) fusion(bf16[256,4096]{1,0:T(8,128)(2,1)} %refs_3_.3, s32[]{:T(128)S(6)} %select_n.172, s32[]{:T(128)S(6)} %select_n.170), kind=kLoop, calls=%fused_computation.95 | loop fusion | bytes 4194312 | tf_op jit(solution)/shard_map/dynamic_slice | solution.py:237
  30.5 2.8 %collective-permute-done = bf16[256,2048]{1,0:T(8,128)(2,1)} collective-permute-done((bf16[256,2048]{1,0:T(8,128)(2,1)S(1)}, bf16[256,2048]{1,0:T(8,128)(2,1)}, u32[]{:S(2)}, u32[]{:S(2)}) %collective-permute-start) | collective-permute-done | bytes 1048608 | tf_op jit(solution)/shard_map/ppermute | solution.py:222
  33.3 26.5 %all-to-all-done.refs_1_ = bf16[16,32,2176]{2,1,0:T(8,128)(2,1)S(1)} async-done(((bf16[16,32,2176]{2,1,0:T(8,128)(2,1)}), bf16[16,32,2176]{2,1,0:T(8,128)(2,1)S(1)}, u32[]{:S(2)}, u32[]{:S(2)}) %all-to-all-start) | async-done | bytes 2228256 | tf_op jit(solution)/shard_map/all_to_all | solution.py:244
  61.5 3.0 %collective-permute-done.1 = bf16[256,2176]{1,0:T(8,128)(2,1)S(1)} collective-permute-done((bf16[256,2176]{1,0:T(8,128)(2,1)S(1)}, bf16[256,2176]{1,0:T(8,128)(2,1)S(1)}, u32[]{:S(2)}, u32[]{:S(2)}) %collective-permute-start.1) | collective-permute-done | bytes 1114144 | tf_op jit(solution)/shard_map/ppermute | solution.py:222
  68.7 3.0 %collective-permute-start.5 = (bf16[1024,256]{1,0:T(8,128)(2,1)S(1)}, bf16[1024,256]{1,0:T(8,128)(2,1)S(1)}, u32[]{:S(2)}, u32[]{:S(2)}) collective-permute-start(bf16[1024,256]{1,0:T(8,128)(2,1)S(1)} %get-tuple-element.40), channel_id=1, source_target_pairs={{0,24},{8,0},{16,8},{24,16},{32,56},{40,32},{48,40},{56,48},{64,88... | collective-permute-start | bytes 1572872 | tf_op jit(solution)/shard_map/ppermute | solution.py:217
  72.6 3.2 %collective-permute-start.4 = (bf16[1024,256]{1,0:T(8,128)(2,1)S(1)}, bf16[1024,256]{1,0:T(8,128)(2,1)S(1)}, u32[]{:S(2)}, u32[]{:S(2)}) collective-permute-start(bf16[1024,256]{1,0:T(8,128)(2,1)S(1)} %get-tuple-element.42), channel_id=1, source_target_pairs={{0,96},{8,104},{16,112},{24,120},{32,0},{40,8},{48,16},{56,24},{64... | collective-permute-start | bytes 1572872 | tf_op jit(solution)/shard_map/ppermute | solution.py:214
  79.1 4.4 %collective-permute-done.3 = bf16[1024,256]{1,0:T(8,128)(2,1)S(1)} collective-permute-done((bf16[1024,256]{1,0:T(8,128)(2,1)S(1)}, bf16[1024,256]{1,0:T(8,128)(2,1)S(1)}, u32[]{:S(2)}, u32[]{:S(2)}) %collective-permute-start.3) | collective-permute-done | bytes 524320 | tf_op jit(solution)/shard_map/ppermute | solution.py:217
  83.6 3.6 %collective-permute-done.2 = bf16[1024,256]{1,0:T(8,128)(2,1)S(1)} collective-permute-done((bf16[1024,256]{1,0:T(8,128)(2,1)S(1)}, bf16[1024,256]{1,0:T(8,128)(2,1)S(1)}, u32[]{:S(2)}, u32[]{:S(2)}) %collective-permute-start.2) | collective-permute-done | bytes 524320 | tf_op jit(solution)/shard_map/ppermute | solution.py:214
  89.2 3.0 %collective-permute-start.7 = (bf16[2048,256]{1,0:T(8,128)(2,1)}, bf16[2048,256]{1,0:T(8,128)(2,1)}, u32[]{:S(2)}, u32[]{:S(2)}) collective-permute-start(bf16[2048,256]{1,0:T(8,128)(2,1)} %pad_maximum_fusion.2), channel_id=1, source_target_pairs={{0,96},{8,104},{16,112},{24,120},{32,0},{40,8},{48,16},{56,24},{64... | collective-permute-start | bytes 3145736 | tf_op jit(solution)/shard_map/ppermute | solution.py:214
  97.1 15.9 %project.1 = (bf16[256,4096]{1,0:T(8,128)(2,1)}, bf16[16,32,2176]{2,1,0:T(8,128)(2,1)}) custom-call(s32[16]{0:T(128)} %broadcast_clamp_fusion.refs_0_, bf16[256,2176]{1,0:T(8,128)(2,1)} %bitcast.80, bf16[2048,4096]{1,0:T(8,128)(2,1)} %all-gather.2.cloned.1.call-done.refs_2_, bf16[256,4096]{1,0:T(8,128)(2,1)} %refs_3_.3), custom_call_target="tpu_custom_call" | custom-call | tf_op jit(solution)/shard_map/project/pallas_call | solution.py:140
  113.0 7.0 %all-to-all-start.1 = ((bf16[16,32,2176]{2,1,0:T(8,128)(2,1)}), bf16[16,32,2176]{2,1,0:T(8,128)(2,1)S(1)}, u32[]{:S(2)}, u32[]{:S(2)}) async-start(bf16[16,32,2176]{2,1,0:T(8,128)(2,1)} %get-tuple-element.24), calls=%async_computation.1 | async-start | bytes 4456448 | tf_op jit(solution)/shard_map/all_to_all | solution.py:296
  120.6 3.1 %fusion.7 = bf16[2048,256]{1,0:T(8,128)(2,1)S(1)} fusion(bf16[512,2048]{1,0:T(8,128)(2,1)} %copy-done.3, bf16[2048,256]{1,0:T(8,128)(2,1)} %collective-permute-done.7, bf16[2048,256]{1,0:T(8,128)(2,1)} %collective-permute-done.6, bf16[512,2048]{1,0:T(8,128)(2,1)} %copy-done.5, s32[]{:T(128)S(6)} %select_n.190), kind=kOutput, calls=%fused_computation.16 | convolution fusion | flops 540016640 | bytes 5505028 | tf_op jit(solution)/shard_map/dot_general | solution.py:266
  125.9 2.7 %collective-permute-start.11 = (bf16[8,64,256]{2,1,0:T(8,128)(2,1)}, bf16[8,64,256]{2,1,0:T(8,128)(2,1)}, u32[]{:S(2)}, u32[]{:S(2)}) collective-permute-start(bf16[8,64,256]{2,1,0:T(8,128)(2,1)} %get-tuple-element.36), channel_id=1, source_target_pairs={{0,16},{8,24},{16,0},{24,8},{32,48},{40,56},{48,32},{56,40},{64,80... | collective-permute-start | bytes 786440 | tf_op jit(solution)/shard_map/ppermute | solution.py:217
  135.9 2.7 %collective-permute-start.14 = (bf16[8,64,256]{2,1,0:T(8,128)(2,1)}, bf16[8,64,256]{2,1,0:T(8,128)(2,1)}, u32[]{:S(2)}, u32[]{:S(2)}) collective-permute-start(bf16[8,64,256]{2,1,0:T(8,128)(2,1)} %get-tuple-element.39), channel_id=1, source_target_pairs={{0,64},{8,72},{16,80},{24,88},{32,96},{40,104},{48,112},{56,120},{... | collective-permute-start | bytes 786440 | tf_op jit(solution)/shard_map/ppermute | solution.py:214
  138.5 15.6 %collective-permute-done.10 = bf16[8,64,256]{2,1,0:T(8,128)(2,1)} collective-permute-done((bf16[8,64,256]{2,1,0:T(8,128)(2,1)S(1)}, bf16[8,64,256]{2,1,0:T(8,128)(2,1)}, u32[]{:S(2)}, u32[]{:S(2)}) %collective-permute-start.10) | collective-permute-done | bytes 262176 | tf_op jit(solution)/shard_map/ppermute | solution.py:217
  156.2 3.3 %collective-permute-done.11 = bf16[8,64,256]{2,1,0:T(8,128)(2,1)} collective-permute-done((bf16[8,64,256]{2,1,0:T(8,128)(2,1)}, bf16[8,64,256]{2,1,0:T(8,128)(2,1)}, u32[]{:S(2)}, u32[]{:S(2)}) %collective-permute-start.11) | collective-permute-done | bytes 262176 | tf_op jit(solution)/shard_map/ppermute | solution.py:217
  168.7 3.2 %collective-permute-done.16 = bf16[2,2,64,256]{3,2,0,1:T(8,128)(2,1)S(1)} collective-permute-done((bf16[2,2,64,256]{3,2,0,1:T(8,128)(2,1)S(1)}, bf16[2,2,64,256]{3,2,0,1:T(8,128)(2,1)S(1)}, u32[]{:S(2)}, u32[]{:S(2)}) %collective-permute-start.16) | collective-permute-done | bytes 131104 | tf_op jit(solution)/shard_map/ppermute | solution.py:211
  173.9 4.1 %collective-permute-start.26 = (bf16[2,64,256]{2,1,0:T(8,128)(2,1)S(1)}, bf16[2,64,256]{2,1,0:T(8,128)(2,1)S(1)}, u32[]{:S(2)}, u32[]{:S(2)}) collective-permute-start(bf16[2,64,256]{2,1,0:T(8,128)(2,1)S(1)} %get-tuple-element.51), channel_id=1, source_target_pairs={{0,32},{8,40},{16,48},{24,56},{32,64},{40,72},{48,80},{56,88},{64,... | collective-permute-start | bytes 196616 | tf_op jit(solution)/shard_map/ppermute | solution.py:214
  184.1 2.6 %collective-permute-start.22 = (bf16[2,64,256]{2,1,0:T(8,128)(2,1)S(1)}, bf16[2,64,256]{2,1,0:T(8,128)(2,1)S(1)}, u32[]{:S(2)}, u32[]{:S(2)}) collective-permute-start(bf16[2,64,256]{2,1,0:T(8,128)(2,1)S(1)} %get-tuple-element.50), channel_id=1, source_target_pairs={{0,24},{8,0},{16,8},{24,16},{32,56},{40,32},{48,40},{56,48},{64,88... | collective-permute-start | bytes 196616 | tf_op jit(solution)/shard_map/ppermute | solution.py:217
  192.4 2.6 %collective-permute-start.24 = (bf16[4,2,64,256]{3,2,1,0:T(8,128)(2,1)S(1)}, bf16[4,2,64,256]{3,2,1,0:T(8,128)(2,1)}, u32[]{:S(2)}, u32[]{:S(2)}) collective-permute-start(bf16[4,2,64,256]{3,2,1,0:T(8,128)(2,1)S(1)} %pad_maximum_fusion.5.refs_1_), channel_id=1, source_target_pairs={{0,64},{8,72},{16,80},{24,88},{32,96},{40,104},{48,112},{56,120},{... | collective-permute-start | bytes 786440 | tf_op jit(solution)/shard_map/ppermute | solution.py:214
  194.9 5.6 %collective-permute-done.29.refs_6_ = bf16[4,2,64,256]{3,2,1,0:T(8,128)(2,1)S(1)} collective-permute-done((bf16[4,2,64,256]{3,2,1,0:T(8,128)(2,1)S(1)}, bf16[4,2,64,256]{3,2,1,0:T(8,128)(2,1)S(1)}, u32[]{:S(2)}, u32[]{:S(2)}) %collective-permute-start.29) | collective-permute-done | bytes 262176 | tf_op jit(solution)/shard_map/ppermute | solution.py:217
  207.1 3.2 %place_blocks.1 = f32[256,4096]{1,0:T(8,128)} custom-call(s32[2]{0:T(128)S(1)} %pad_add_fusion.refs_0_, bf16[4,2,64,256]{3,2,1,0:T(8,128)(2,1)S(1)} %pad_maximum_fusion.5.refs_1_, bf16[4,2,64,256]{3,2,1,0:T(8,128)(2,1)} %collective-permute-done.23.refs_2_, bf16[4,2,64,256]{3,2,1,0:T(8,128)(2,1)} %collective-permute-done.24.refs_3_, ...), custom_call_target="tpu_custom_call" | custom-call | tf_op jit(solution)/shard_map/place_blocks/pallas_call | solution.py:187
  (117 shorter events, 59.7 us)
Async XLA Ops:
  7.2 90.0 %all-gather.2.cloned.1.call-start = ((), (), s32[]{:S(2)}) async-start(), calls=%async_computation.2 | async-start | bytes 18874368 | tf_op jit(solution)/shard_map/all_gather | solution.py:235
  19.6 40.1 %all-to-all-start = ((bf16[16,32,2176]{2,1,0:T(8,128)(2,1)}), bf16[16,32,2176]{2,1,0:T(8,128)(2,1)S(1)}, u32[]{:S(2)}, u32[]{:S(2)}) async-start(bf16[16,32,2176]{2,1,0:T(8,128)(2,1)} %bitcast.84), calls=%async_computation | async-start | bytes 4456448 | tf_op jit(solution)/shard_map/all_to_all | solution.py:244
  68.3 15.2 %collective-permute-start.3 = (bf16[1024,256]{1,0:T(8,128)(2,1)S(1)}, bf16[1024,256]{1,0:T(8,128)(2,1)S(1)}, u32[]{:S(2)}, u32[]{:S(2)}) collective-permute-start(bf16[1024,256]{1,0:T(8,128)(2,1)S(1)} %get-tuple-element.41), channel_id=1, source_target_pairs={{0,8},{8,16},{16,24},{24,0},{32,40},{40,48},{48,56},{56,32},{64,72... | collective-permute-start | bytes 1572872 | tf_op jit(solution)/shard_map/ppermute | solution.py:217
  68.7 14.9 %collective-permute-start.5 = (bf16[1024,256]{1,0:T(8,128)(2,1)S(1)}, bf16[1024,256]{1,0:T(8,128)(2,1)S(1)}, u32[]{:S(2)}, u32[]{:S(2)}) collective-permute-start(bf16[1024,256]{1,0:T(8,128)(2,1)S(1)} %get-tuple-element.40), channel_id=1, source_target_pairs={{0,24},{8,0},{16,8},{24,16},{32,56},{40,32},{48,40},{56,48},{64,88... | collective-permute-start | bytes 1572872 | tf_op jit(solution)/shard_map/ppermute | solution.py:217
  72.5 14.7 %collective-permute-start.2 = (bf16[1024,256]{1,0:T(8,128)(2,1)S(1)}, bf16[1024,256]{1,0:T(8,128)(2,1)S(1)}, u32[]{:S(2)}, u32[]{:S(2)}) collective-permute-start(bf16[1024,256]{1,0:T(8,128)(2,1)S(1)} %get-tuple-element.43), channel_id=1, source_target_pairs={{0,32},{8,40},{16,48},{24,56},{32,64},{40,72},{48,80},{56,88},{64,... | collective-permute-start | bytes 1572872 | tf_op jit(solution)/shard_map/ppermute | solution.py:214
  72.6 14.6 %collective-permute-start.4 = (bf16[1024,256]{1,0:T(8,128)(2,1)S(1)}, bf16[1024,256]{1,0:T(8,128)(2,1)S(1)}, u32[]{:S(2)}, u32[]{:S(2)}) collective-permute-start(bf16[1024,256]{1,0:T(8,128)(2,1)S(1)} %get-tuple-element.42), channel_id=1, source_target_pairs={{0,96},{8,104},{16,112},{24,120},{32,0},{40,8},{48,16},{56,24},{64... | collective-permute-start | bytes 1572872 | tf_op jit(solution)/shard_map/ppermute | solution.py:214
  87.4 32.7 %collective-permute-start.9 = (bf16[2048,256]{1,0:T(8,128)(2,1)S(1)}, bf16[2048,256]{1,0:T(8,128)(2,1)}, u32[]{:S(2)}, u32[]{:S(2)}) collective-permute-start(bf16[2048,256]{1,0:T(8,128)(2,1)S(1)} %pad_maximum_fusion.3), channel_id=1, source_target_pairs={{0,24},{8,0},{16,8},{24,16},{32,56},{40,32},{48,40},{56,48},{64,88... | collective-permute-start | bytes 3145736 | tf_op jit(solution)/shard_map/ppermute | solution.py:217
  89.2 31.0 %collective-permute-start.7 = (bf16[2048,256]{1,0:T(8,128)(2,1)}, bf16[2048,256]{1,0:T(8,128)(2,1)}, u32[]{:S(2)}, u32[]{:S(2)}) collective-permute-start(bf16[2048,256]{1,0:T(8,128)(2,1)} %pad_maximum_fusion.2), channel_id=1, source_target_pairs={{0,96},{8,104},{16,112},{24,120},{32,0},{40,8},{48,16},{56,24},{64... | collective-permute-start | bytes 3145736 | tf_op jit(solution)/shard_map/ppermute | solution.py:214
  93.4 26.7 %collective-permute-start.8 = (bf16[2048,256]{1,0:T(8,128)(2,1)}, bf16[2048,256]{1,0:T(8,128)(2,1)}, u32[]{:S(2)}, u32[]{:S(2)}) collective-permute-start(bf16[2048,256]{1,0:T(8,128)(2,1)} %pad_maximum_fusion.1), channel_id=1, source_target_pairs={{0,8},{8,16},{16,24},{24,0},{32,40},{40,48},{48,56},{56,32},{64,72... | collective-permute-start | bytes 3145736 | tf_op jit(solution)/shard_map/ppermute | solution.py:217
  96.4 24.2 %collective-permute-start.6 = (bf16[2048,256]{1,0:T(8,128)(2,1)}, bf16[2048,256]{1,0:T(8,128)(2,1)}, u32[]{:S(2)}, u32[]{:S(2)}) collective-permute-start(bf16[2048,256]{1,0:T(8,128)(2,1)} %pad_maximum_fusion), channel_id=1, source_target_pairs={{0,32},{8,40},{16,48},{24,56},{32,64},{40,72},{48,80},{56,88},{64,... | collective-permute-start | bytes 3145736 | tf_op jit(solution)/shard_map/ppermute | solution.py:214
  113.0 50.6 %all-to-all-start.1 = ((bf16[16,32,2176]{2,1,0:T(8,128)(2,1)}), bf16[16,32,2176]{2,1,0:T(8,128)(2,1)S(1)}, u32[]{:S(2)}, u32[]{:S(2)}) async-start(bf16[16,32,2176]{2,1,0:T(8,128)(2,1)} %get-tuple-element.24), calls=%async_computation.1 | async-start | bytes 4456448 | tf_op jit(solution)/shard_map/all_to_all | solution.py:296
  124.5 29.6 %collective-permute-start.10 = (bf16[8,64,256]{2,1,0:T(8,128)(2,1)S(1)}, bf16[8,64,256]{2,1,0:T(8,128)(2,1)}, u32[]{:S(2)}, u32[]{:S(2)}) collective-permute-start(bf16[8,64,256]{2,1,0:T(8,128)(2,1)S(1)} %get-tuple-element.34), channel_id=1, source_target_pairs={{0,8},{8,16},{16,24},{24,0},{32,40},{40,48},{48,56},{56,32},{64,72... | collective-permute-start | bytes 786440 | tf_op jit(solution)/shard_map/ppermute | solution.py:217
  125.9 33.5 %collective-permute-start.11 = (bf16[8,64,256]{2,1,0:T(8,128)(2,1)}, bf16[8,64,256]{2,1,0:T(8,128)(2,1)}, u32[]{:S(2)}, u32[]{:S(2)}) collective-permute-start(bf16[8,64,256]{2,1,0:T(8,128)(2,1)} %get-tuple-element.36), channel_id=1, source_target_pairs={{0,16},{8,24},{16,0},{24,8},{32,48},{40,56},{48,32},{56,40},{64,80... | collective-permute-start | bytes 786440 | tf_op jit(solution)/shard_map/ppermute | solution.py:217
  128.6 31.3 %collective-permute-start.12 = (bf16[8,64,256]{2,1,0:T(8,128)(2,1)S(1)}, bf16[8,64,256]{2,1,0:T(8,128)(2,1)}, u32[]{:S(2)}, u32[]{:S(2)}) collective-permute-start(bf16[8,64,256]{2,1,0:T(8,128)(2,1)S(1)} %get-tuple-element.35), channel_id=1, source_target_pairs={{0,24},{8,0},{16,8},{24,16},{32,56},{40,32},{48,40},{56,48},{64,88... | collective-permute-start | bytes 786440 | tf_op jit(solution)/shard_map/ppermute | solution.py:217
  134.4 26.8 %collective-permute-start.13 = (bf16[8,64,256]{2,1,0:T(8,128)(2,1)}, bf16[8,64,256]{2,1,0:T(8,128)(2,1)}, u32[]{:S(2)}, u32[]{:S(2)}) collective-permute-start(bf16[8,64,256]{2,1,0:T(8,128)(2,1)} %get-tuple-element.37), channel_id=1, source_target_pairs={{0,32},{8,40},{16,48},{24,56},{32,64},{40,72},{48,80},{56,88},{64,... | collective-permute-start | bytes 786440 | tf_op jit(solution)/shard_map/ppermute | solution.py:214
  135.9 25.6 %collective-permute-start.14 = (bf16[8,64,256]{2,1,0:T(8,128)(2,1)}, bf16[8,64,256]{2,1,0:T(8,128)(2,1)}, u32[]{:S(2)}, u32[]{:S(2)}) collective-permute-start(bf16[8,64,256]{2,1,0:T(8,128)(2,1)} %get-tuple-element.39), channel_id=1, source_target_pairs={{0,64},{8,72},{16,80},{24,88},{32,96},{40,104},{48,112},{56,120},{... | collective-permute-start | bytes 786440 | tf_op jit(solution)/shard_map/ppermute | solution.py:214
  173.9 10.1 %collective-permute-start.26 = (bf16[2,64,256]{2,1,0:T(8,128)(2,1)S(1)}, bf16[2,64,256]{2,1,0:T(8,128)(2,1)S(1)}, u32[]{:S(2)}, u32[]{:S(2)}) collective-permute-start(bf16[2,64,256]{2,1,0:T(8,128)(2,1)S(1)} %get-tuple-element.51), channel_id=1, source_target_pairs={{0,32},{8,40},{16,48},{24,56},{32,64},{40,72},{48,80},{56,88},{64,... | collective-permute-start | bytes 196616 | tf_op jit(solution)/shard_map/ppermute | solution.py:214
  178.1 8.6 %collective-permute-start.27 = (bf16[2,64,256]{2,1,0:T(8,128)(2,1)S(1)}, bf16[2,64,256]{2,1,0:T(8,128)(2,1)S(1)}, u32[]{:S(2)}, u32[]{:S(2)}) collective-permute-start(bf16[2,64,256]{2,1,0:T(8,128)(2,1)S(1)} %get-tuple-element.51), channel_id=1, source_target_pairs={{0,64},{8,72},{16,80},{24,88},{32,96},{40,104},{48,112},{56,120},{... | collective-permute-start | bytes 196616 | tf_op jit(solution)/shard_map/ppermute | solution.py:214
  181.5 9.7 %collective-permute-start.21 = (bf16[2,64,256]{2,1,0:T(8,128)(2,1)S(1)}, bf16[2,64,256]{2,1,0:T(8,128)(2,1)S(1)}, u32[]{:S(2)}, u32[]{:S(2)}) collective-permute-start(bf16[2,64,256]{2,1,0:T(8,128)(2,1)S(1)} %get-tuple-element.50), channel_id=1, source_target_pairs={{0,16},{8,24},{16,0},{24,8},{32,48},{40,56},{48,32},{56,40},{64,80... | collective-permute-start | bytes 196616 | tf_op jit(solution)/shard_map/ppermute | solution.py:217
  186.7 13.9 %collective-permute-start.29 = (bf16[4,2,64,256]{3,2,1,0:T(8,128)(2,1)S(1)}, bf16[4,2,64,256]{3,2,1,0:T(8,128)(2,1)S(1)}, u32[]{:S(2)}, u32[]{:S(2)}) collective-permute-start(bf16[4,2,64,256]{3,2,1,0:T(8,128)(2,1)S(1)} %pad_maximum_fusion.6.refs_5_), channel_id=1, source_target_pairs={{0,8},{8,16},{16,24},{24,0},{32,40},{40,48},{48,56},{56,32},{64,72... | collective-permute-start | bytes 786440 | tf_op jit(solution)/shard_map/ppermute | solution.py:217
  186.8 16.9 %collective-permute-start.30 = (bf16[4,2,64,256]{3,2,1,0:T(8,128)(2,1)S(1)}, bf16[4,2,64,256]{3,2,1,0:T(8,128)(2,1)S(1)}, u32[]{:S(2)}, u32[]{:S(2)}) collective-permute-start(bf16[4,2,64,256]{3,2,1,0:T(8,128)(2,1)S(1)} %pad_maximum_fusion.6.refs_5_), channel_id=1, source_target_pairs={{0,16},{8,24},{16,0},{24,8},{32,48},{40,56},{48,32},{56,40},{64,80... | collective-permute-start | bytes 786440 | tf_op jit(solution)/shard_map/ppermute | solution.py:217
  189.1 14.6 %collective-permute-start.31 = (bf16[4,2,64,256]{3,2,1,0:T(8,128)(2,1)S(1)}, bf16[4,2,64,256]{3,2,1,0:T(8,128)(2,1)S(1)}, u32[]{:S(2)}, u32[]{:S(2)}) collective-permute-start(bf16[4,2,64,256]{3,2,1,0:T(8,128)(2,1)S(1)} %pad_maximum_fusion.6.refs_5_), channel_id=1, source_target_pairs={{0,24},{8,0},{16,8},{24,16},{32,56},{40,32},{48,40},{56,48},{64,88... | collective-permute-start | bytes 786440 | tf_op jit(solution)/shard_map/ppermute | solution.py:217
  191.2 12.5 %collective-permute-start.23 = (bf16[4,2,64,256]{3,2,1,0:T(8,128)(2,1)S(1)}, bf16[4,2,64,256]{3,2,1,0:T(8,128)(2,1)}, u32[]{:S(2)}, u32[]{:S(2)}) collective-permute-start(bf16[4,2,64,256]{3,2,1,0:T(8,128)(2,1)S(1)} %pad_maximum_fusion.5.refs_1_), channel_id=1, source_target_pairs={{0,32},{8,40},{16,48},{24,56},{32,64},{40,72},{48,80},{56,88},{64,... | collective-permute-start | bytes 786440 | tf_op jit(solution)/shard_map/ppermute | solution.py:214
  192.4 13.0 %collective-permute-start.24 = (bf16[4,2,64,256]{3,2,1,0:T(8,128)(2,1)S(1)}, bf16[4,2,64,256]{3,2,1,0:T(8,128)(2,1)}, u32[]{:S(2)}, u32[]{:S(2)}) collective-permute-start(bf16[4,2,64,256]{3,2,1,0:T(8,128)(2,1)S(1)} %pad_maximum_fusion.5.refs_1_), channel_id=1, source_target_pairs={{0,64},{8,72},{16,80},{24,88},{32,96},{40,104},{48,112},{56,120},{... | collective-permute-start | bytes 786440 | tf_op jit(solution)/shard_map/ppermute | solution.py:214
  (19 other events, 130.2 us)
Sparse Core Ops, SparseCore 0:
  9.7 87.3 all-gather.1

commit v3 on v2

--- a/solution.py
+++ b/solution.py
@@ -20,52 +20,75 @@
     return lax.optimization_barrier((value, others))[0]
 
 
-def pick_body(width, owner_ref, listed_ref, logit_ref, head_ref, out_ref, onehot_ref):
-    step = pl.program_id(0)
-    columns = head_ref.shape[1]
+def pick_body(owner_ref, listed_ref, logit_ref, head_ref, out_ref, onehot_ref, head, picked, in_sems, out_sems):
     rows, count = onehot_ref.shape
     blocks = owner_ref.shape[0]
     block = rows // blocks
-
-    @pl.when(step == 0)
-    def _():
-        lane = lax.broadcasted_iota(jnp.int32, (block, EXTRA), 1)
-        tokens = lax.broadcasted_iota(jnp.int32, (block, count), 1)
-        for peer in range(rows // block):
-            found = jnp.int32(blocks)
-            for b in range(blocks):
-                found = jnp.where(owner_ref[b] == peer, b, found)
-            there = found < blocks
-            start = pl.multiple_of(jnp.minimum(found, blocks - 1) * block, block)
-            listed = jnp.where(there, listed_ref[pl.ds(start, block), :], -1)
-            hit = listed == tokens
-            span = slice(peer * block, (peer + 1) * block)
-            onehot_ref[span, :] = hit.astype(jnp.bfloat16)
-            logit = jnp.sum(jnp.where(hit, logit_ref[...], 0.0), axis=1, keepdims=True)
-            mark = jnp.where(there, 1.0, 0.0)
-            out_ref[span, width:] = jnp.where(lane == 0, jax.nn.sigmoid(logit), mark).astype(jnp.bfloat16)
-
-    out_ref[:, pl.ds(pl.multiple_of(step * columns, columns), columns)] = jnp.dot(
-        onehot_ref[...], head_ref[...], preferred_element_type=jnp.float32
-    ).astype(jnp.bfloat16)
+    steps = in_sems.shape[0]
+    width = head.shape[1]
+    columns = width // steps
+
+    def fetch(step):
+        span = pl.ds(step * columns, columns)
+        return pltpu.make_async_copy(head_ref.at[:, span], head.at[:, span], in_sems.at[step])
+
+    def hand_over(step):
+        span = pl.ds(step * columns, columns if step < steps else EXTRA)
+        return pltpu.make_async_copy(picked.at[:, span], out_ref.at[:, span], out_sems.at[step])
+
+    for step in range(steps):
+        fetch(step).start()
+
+    lane = lax.broadcasted_iota(jnp.int32, (block, EXTRA), 1)
+    tokens = lax.broadcasted_iota(jnp.int32, (block, count), 1)
+    for peer in range(rows // block):
+        found = jnp.int32(blocks)
+        for b in range(blocks):
+            found = jnp.where(owner_ref[b] == peer, b, found)
+        there = found < blocks
+        start = pl.multiple_of(jnp.minimum(found, blocks - 1) * block, block)
+        listed = jnp.where(there, listed_ref[pl.ds(start, block), :], -1)
+        hit = listed == tokens
+        span = slice(peer * block, (peer + 1) * block)
+        onehot_ref[span, :] = hit.astype(jnp.bfloat16)
+        logit = jnp.sum(jnp.where(hit, logit_ref[...], 0.0), axis=1, keepdims=True)
+        mark = jnp.where(there, 1.0, 0.0)
+        picked[span, width:] = jnp.where(lane == 0, jax.nn.sigmoid(logit), mark).astype(jnp.bfloat16)
+    hand_over(steps).start()
+
+    for step in range(steps):
+        fetch(step).wait()
+        span = slice(step * columns, (step + 1) * columns)
+        picked[:, span] = jnp.dot(
+            onehot_ref[...], head[:, span], preferred_element_type=jnp.float32
+        ).astype(jnp.bfloat16)
+        hand_over(step).start()
+    for step in range(steps + 1):
+        hand_over(step).wait()
 
 
 def pick_rows(owner, listed, logits, head):
     rows = listed.shape[0]
     count, width = head.shape
-    columns = 512
-    return pl.pallas_call(
-        lambda *refs: pick_body(width, *refs),
+    steps = width // 512
+    vmem = pl.BlockSpec(memory_space=pltpu.VMEM)
+    return pl.pallas_call(
+        pick_body,
         out_shape=jax.ShapeDtypeStruct((rows, width + EXTRA), jnp.bfloat16),
-        grid=(width // columns,),
         in_specs=[
             pl.BlockSpec(memory_space=pltpu.SMEM),
-            pl.BlockSpec((rows, 1), lambda n: (0, 0)),
-            pl.BlockSpec((1, count), lambda n: (0, 0)),
-            pl.BlockSpec((count, columns), lambda n: (0, n)),
-        ],
-        out_specs=pl.BlockSpec((rows, width + EXTRA), lambda n: (0, 0)),
-        scratch_shapes=[pltpu.VMEM((rows, count), jnp.bfloat16)],
+            vmem,
+            vmem,
+            pl.BlockSpec(memory_space=pl.ANY),
+        ],
+        out_specs=pl.BlockSpec(memory_space=pl.ANY),
+        scratch_shapes=[
+            pltpu.VMEM((rows, count), jnp.bfloat16),
+            pltpu.VMEM((count, width), jnp.bfloat16),
+            pltpu.VMEM((rows, width + EXTRA), jnp.bfloat16),
+            pltpu.SemaphoreType.DMA((steps,)),
+            pltpu.SemaphoreType.DMA((steps + 1,)),
+        ],
         compiler_params=params(56),
         cost_estimate=NO_COST,
         name="pick_rows",
@@ -103,46 +126,37 @@
     )(index, source)
 
 
-def project_body(width, slot_ref, rows_ref, weight_ref, cot_ref, update_ref, back_ref, total_ref, inner_ref):
-    step, steps = pl.program_id(0), pl.num_programs(0)
+def answer_body(width, slot_ref, rows_ref, weight_ref, cot_ref, back_ref, total_ref, logit_ref):
+    step = pl.program_id(0)
 
     @pl.when(step == 0)
     def _():
         total_ref[...] = jnp.zeros_like(total_ref)
-        inner_ref[...] = jnp.zeros_like(inner_ref)
-
-    weight = weight_ref[...]
-    gate = rows_ref[:, width : width + 1].astype(jnp.float32)
-    projected = jnp.dot(rows_ref[:, :width], weight, preferred_element_type=jnp.float32)
-    update_ref[...] = (gate * projected).astype(jnp.bfloat16)
-    cot = cot_ref[...].astype(jnp.float32)
-    inner_ref[...] += cot * projected
-    weighted = (gate * cot).astype(jnp.bfloat16)
+
     total_ref[...] += lax.dot_general(
-        weighted, weight, (((1,), (1,)), ((), ())), preferred_element_type=jnp.float32
-    )
-
-    @pl.when(step == steps - 1)
+        cot_ref[...], weight_ref[...], (((1,), (1,)), ((), ())), preferred_element_type=jnp.float32
+    )
+
+    @pl.when(step == pl.num_programs(0) - 1)
     def _():
-        inner = jnp.sum(inner_ref[...], axis=1, keepdims=True)
-        inner_ref[:, :EXTRA] = jnp.broadcast_to(gate * (1.0 - gate) * inner, (gate.shape[0], EXTRA))
+        gate = rows_ref[:, width : width + 1].astype(jnp.float32)
+        inner = jnp.sum(rows_ref[:, :width].astype(jnp.float32) * total_ref[...], axis=1, keepdims=True)
+        logit_ref[...] = jnp.broadcast_to(gate * (1.0 - gate) * inner, logit_ref.shape)
+        total_ref[...] *= gate
         block = back_ref.shape[1]
         for peer in range(back_ref.shape[0]):
-            start = pl.multiple_of(slot_ref[peer] * block, block)
-            back_ref[peer, :, :width] = total_ref[pl.ds(start, block), :].astype(jnp.bfloat16)
-            back_ref[peer, :, width:] = inner_ref[pl.ds(start, block), :EXTRA].astype(jnp.bfloat16)
-
-
-def project(rows, weight, cotangent, slots, block):
+            here = pl.ds(pl.multiple_of(slot_ref[peer] * block, block), block)
+            back_ref[peer, :, :width] = total_ref[here, :].astype(jnp.bfloat16)
+            back_ref[peer, :, width:] = logit_ref[here, :].astype(jnp.bfloat16)
+
+
+def answer(rows, weight, cotangent, slots, block):
     count, wide = rows.shape
     width, model = weight.shape
-    columns = 512
-    return pl.pallas_call(
-        lambda *refs: project_body(width, *refs),
-        out_shape=(
-            jax.ShapeDtypeStruct((count, model), jnp.bfloat16),
-            jax.ShapeDtypeStruct((slots.shape[0], block, wide), jnp.bfloat16),
-        ),
+    columns = 1024
+    return pl.pallas_call(
+        lambda *refs: answer_body(width, *refs),
+        out_shape=jax.ShapeDtypeStruct((slots.shape[0], block, wide), jnp.bfloat16),
         grid=(model // columns,),
         in_specs=[
             pl.BlockSpec(memory_space=pltpu.SMEM),
@@ -150,46 +164,63 @@
             pl.BlockSpec((width, columns), lambda n: (0, n)),
             pl.BlockSpec((count, columns), lambda n: (0, n)),
         ],
-        out_specs=(
-            pl.BlockSpec((count, columns), lambda n: (0, n)),
-            pl.BlockSpec((slots.shape[0], block, wide), lambda n: (0, 0, 0)),
-        ),
+        out_specs=pl.BlockSpec((slots.shape[0], block, wide), lambda n: (0, 0, 0)),
         scratch_shapes=[
             pltpu.VMEM((count, width), jnp.float32),
-            pltpu.VMEM((count, columns), jnp.float32),
+            pltpu.VMEM((count, EXTRA), jnp.float32),
         ],
         compiler_params=params(56),
         cost_estimate=NO_COST,
+        name="answer",
+    )(slots, rows, weight, cotangent)
+
+
+def project_body(width, rows_ref, weight_ref, update_ref):
+    gate = rows_ref[:, width : width + 1].astype(jnp.float32)
+    projected = jnp.dot(rows_ref[:, :width], weight_ref[...], preferred_element_type=jnp.float32)
+    update_ref[...] = (gate * projected).astype(jnp.bfloat16)
+
+
+def project(rows, weight):
+    count, wide = rows.shape
+    width, model = weight.shape
+    columns = 1024
+    return pl.pallas_call(
+        lambda *refs: project_body(width, *refs),
+        out_shape=jax.ShapeDtypeStruct((count, model), jnp.bfloat16),
+        grid=(model // columns,),
+        in_specs=[
+            pl.BlockSpec((count, wide), lambda n: (0, 0)),
+            pl.BlockSpec((width, columns), lambda n: (0, n)),
+        ],
+        out_specs=pl.BlockSpec((count, columns), lambda n: (0, n)),
+        compiler_params=params(56),
+        cost_estimate=NO_COST,
         name="project",
-    )(slots, rows, weight, cotangent)
+    )(rows, weight)
 
 
 def place_body(side, spot_ref, *refs):
     out_ref = refs[-1]
-    rows, columns = refs[0].shape[2:]
-    across = out_ref.shape[1] // 2
+    columns = refs[0].shape[2]
     for which in range(2):
-        line, cross = spot_ref[1 - which], spot_ref[which]
-        for j in range(side):
-            array = refs[which * side + j]
-            place = (cross - j + side) % side * columns + which * across
-            for k in range(side):
-                top = (line - k + side) % side * rows
-                out_ref[pl.ds(pl.multiple_of(top, rows), rows), pl.ds(pl.multiple_of(place, columns), columns)] = array[
-                    k, 0
-                ].astype(jnp.float32)
+        for ahead in range(side):
+            left = (spot_ref[which] - ahead + side) % side * columns + which * side * columns
+            array = refs[which * side + ahead]
+            out_ref[:, pl.ds(pl.multiple_of(left, columns), columns)] = array[0].astype(jnp.float32)
 
 
 def place_blocks(spot, first, second):
-    side, halves, rows, columns = first[0].shape
+    side = len(first)
+    halves, rows, columns = first[0].shape
     model = halves * 2 * side * columns
-    block = pl.BlockSpec((side, 1, rows, columns), lambda h: (0, h, 0, 0))
+    block = pl.BlockSpec((1, rows, columns), lambda h: (h, 0, 0))
     return pl.pallas_call(
         lambda *refs: place_body(side, *refs),
-        out_shape=jax.ShapeDtypeStruct((side * rows, model), jnp.float32),
+        out_shape=jax.ShapeDtypeStruct((rows, model), jnp.float32),
         grid=(halves,),
         in_specs=[pl.BlockSpec(memory_space=pltpu.SMEM)] + [block] * (2 * side),
-        out_specs=pl.BlockSpec((side * rows, model // halves), lambda h: (0, h)),
+        out_specs=pl.BlockSpec((rows, model // halves), lambda h: (0, h)),
         compiler_params=params(),
         cost_estimate=NO_COST,
         name="place_blocks",
@@ -280,7 +311,8 @@
     )
     ahead_y, ahead_z = term(0, y + 1), term(half // 2, z + 1)
     behind_y, behind_z = term(0, y + side - 1), term(half // 2, z + side - 1)
-    got_parts = after(got_parts, ahead_y, ahead_z, behind_y, behind_z)
+    own_y, own_z = term(0, y), term(half // 2, z)
+    got_parts = after(got_parts, ahead_y, ahead_z, behind_y, behind_z, own_y, own_z)
     low_y, low_z, high_y, high_z = [wide(part_sum) for part_sum in got_parts]
     sent = (
         narrow(jnp.concatenate([ahead_y[:cut] + low_y, ahead_y[cut:]], axis=0)),
@@ -292,12 +324,12 @@
     to_y, to_z = along_y(sent[2], -1), along_z(sent[3], -1)
 
     slot = after(jnp.clip(position, 0, receive - 1), sent)
-    update, back = project(held, weight, cotangent, slot, block)
+    back = answer(held, weight, cotangent, slot, block)
     returned = lax.all_to_all(back, "dp", split_axis=0, concat_axis=0, tiled=True)
     from_y, to_y, from_z, to_z = after((from_y, to_y, from_z, to_z), back)
 
-    sum_y = narrow(term(0, y) + wide(from_y) + wide(to_y))
-    sum_z = narrow(term(half // 2, z) + wide(from_z) + wide(to_z))
+    sum_y = narrow(own_y + wide(from_y) + wide(to_y))
+    sum_z = narrow(own_z + wide(from_z) + wide(to_z))
 
     share = shard // side
 
@@ -308,21 +340,24 @@
             total += wide(along(at(value, (place + ahead) % count, axis), ahead))
         return narrow(total)
 
-    sum_y = exchange(sum_y.reshape(n_fsdp, side, share, part), 1, z, along_z)
-    sum_z = exchange(sum_z.reshape(n_fsdp, side, share, part), 1, y, along_y)
-    sums = jnp.stack([sum_y, sum_z]).reshape(2, chips, 2, share, part)
-    sums = exchange(after(sums, returned), 1, chip, along_x)
+    sums = jnp.stack([sum_y, sum_z]).reshape(2, chips, 2 * shard, part)
+    update = project(after(held, sums), weight)
+    sums = exchange(sums, 1, chip, along_x)
+    sums = after(sums, returned, update).reshape(2, 2, shard, part)
     keep, take = at(sums, core, 1), to_partner(at(sums, 1 - core, 1))
     first = core == 0
-    piece = jnp.stack([jnp.where(first, keep, take), jnp.where(first, take, keep)])
+    piece = jnp.stack([jnp.where(first, keep, take), jnp.where(first, take, keep)], axis=1)
 
     def around(value, along):
         return [value] + [along(value, ahead) for ahead in range(1, side)]
 
-    line_z = jnp.stack(around(piece[:, 0], along_z))
-    line_y = jnp.stack(around(piece[:, 1], along_y))
+    def whole(value, along):
+        terms = [wide(term) for term in around(value, along)]
+        return narrow((terms[0] + terms[2]) + (terms[1] + terms[3]))
+
+    sum_y, sum_z = whole(piece[0], along_z), whole(piece[1], along_y)
     spot = jnp.stack([y, z]).astype(jnp.int32)
-    grad_weight = place_blocks(spot, around(line_z, along_y), around(line_y, along_z))
+    grad_weight = place_blocks(spot, around(sum_y, along_y), around(sum_z, along_z))
 
     grad_context = move_blocks(returned, owner, width).reshape(slots, width)
     logit_blocks = returned[:, :, width]

time: 218 us -> 204 us (0.936)
  starting transfers between devices: 64.8 us -> 51.3 us
  waiting for transfers between devices: 76 us -> 65.6 us
  other arithmetic: 10.2 us -> 17.3 us
  Pallas kernels: 32.8 us -> 37.7 us
    ppermute x13 -> x10, waiting for transfers between devices: 29.4 us -> 7.23 us  [along_z(): lax.ppermute(value, 'dp', [(d, d // side * side + (d + ahead) % side) for...]
    ppermute x13 -> x10, starting transfers between devices: 23.1 us -> 15 us  [along_y(): lax.ppermute(value, 'dp', [(d, (d + side * ahead) % n_dp) for d in range(...]
    ppermute x13 -> x10, waiting for transfers between devices: 8.48 us -> 16.3 us  [along_y(): lax.ppermute(value, 'dp', [(d, (d + side * ahead) % n_dp) for d in range(...]
    ppermute x13 -> x10, starting transfers between devices: 21.4 us -> 14.9 us  [along_z(): lax.ppermute(value, 'dp', [(d, d // side * side + (d + ahead) % side) for...]
    pallas_call x2 -> x3, Pallas kernels: 26.7 us -> 31.6 us  [the longest x1 11.4 us: answer(): pl.pallas_call(lambda *refs: answer_body(width, *refs), out_shape=jax.Sha...]
    convert_element_type x3 -> x4, other arithmetic: 2.64 us -> 6.7 us  [narrow(): return value.astype(jnp.bfloat16)]
    ppermute x3, waiting for transfers between devices: 3.73 us -> 7.68 us  [along_x(): lax.ppermute(value, 'fsdp', [(f, (f + 2 * ahead) % n_fsdp) for f in range...]
  transfers between devices with their start and end apart: 35 -> 29, of which waited for: 18 -> 17; matrix products, arithmetic and copies ran while one was open for 12% -> 15% of each run, Pallas kernels for 14% -> 17%
where the time goes in v3:
time: 204 us; the launch traced here: 203 us
  waiting for transfers between devices  65.6 us (32%)
  starting transfers between devices  51.3 us (25%)
  Pallas kernels  37.7 us (18%)
  other arithmetic  17.3 us (8%)
  between operations  14.7 us (7%)
  matrix products  8.8 us (4%)
  local copies, waits for them, and re-layouts  7.74 us (4%)
    all_to_all x1, waiting for transfers between devices, on_device(): got = lax.all_to_all(send, 'dp', split_axis=0, concat_axis=0, tiled=True)  26.4 us
    ppermute x10, waiting for transfers between devices, along_y(): lax.ppermute(value, 'dp', [(d, (d + side * ahead) % n_dp) for d in range(...  16.3 us
    ppermute x10, starting transfers between devices, along_y(): lax.ppermute(value, 'dp', [(d, (d + side * ahead) % n_dp) for d in range(...  15 us
    ppermute x10, starting transfers between devices, along_z(): lax.ppermute(value, 'dp', [(d, d // side * side + (d + ahead) % side) for...  14.9 us
    pallas_call x1, Pallas kernels, answer(): pl.pallas_call(lambda *refs: answer_body(width, *refs), out_shape=jax.Sha...  11.4 us
    pallas_call x1, Pallas kernels, pick_rows(): pl.pallas_call(pick_body, out_shape=jax.ShapeDtypeStruct((rows, width + E...  10.3 us
    pallas_call x1, Pallas kernels, project(): pl.pallas_call(lambda *refs: project_body(width, *refs), out_shape=jax.Sh...  9.93 us
    dot_general x8, matrix products, term(): lax.dot_general(both_rows, columns, (((0,), (0,)), ((), ())), preferred_e...  8.8 us
  transfers between devices with their start and end apart: 29, of which 17 were waited for; matrix products, arithmetic and copies ran while one was open for 15% of the time, Pallas kernels for 17%

profile of v3, /device:TPU:0, one launch (start us, length us, event | category | flops | bytes accessed | tf_op | source)
XLA Modules:
  0.0 203.1 jit_solution(17542602771304224702)
XLA Ops:
  8.8 10.3 %pick_rows.1 = bf16[512,2176]{1,0:T(8,128)(2,1)} custom-call(s32[16]{0:T(128)} %bitcast.59, s32[512,1]{1,0:T(8,128)} %copy.17.listed_ref, f32[1,2048]{1,0:T(1,128)} %bitcast.71, bf16[2048,2048]{1,0:T(8,128)(2,1)} %head_ref.1), custom_call_target="tpu_custom_call" | custom-call | tf_op jit(solution)/shard_map/pick_rows/pallas_call | solution.py:75
  19.1 8.1 %all-to-all-start = ((bf16[16,32,2176]{2,1,0:T(8,128)(2,1)}), bf16[16,32,2176]{2,1,0:T(8,128)(2,1)S(1)}, u32[]{:S(2)}, u32[]{:S(2)}) async-start(bf16[16,32,2176]{2,1,0:T(8,128)(2,1)} %bitcast.66), calls=%async_computation | async-start | bytes 4456448 | tf_op jit(solution)/shard_map/all_to_all | solution.py:275
  27.3 2.8 %constant_dynamic-slice_fusion = (bf16[256,2048]{1,0:T(8,128)(2,1)}, bf16[256,2048]{1,0:T(8,128)(2,1)S(1)}) fusion(bf16[256,4096]{1,0:T(8,128)(2,1)} %refs_3_.1, s32[]{:T(128)S(6)} %select_n.135, s32[]{:T(128)S(6)} %select_n.133), kind=kLoop, calls=%fused_computation.90 | loop fusion | bytes 4194312 | tf_op jit(solution)/shard_map/dynamic_slice | solution.py:268
  30.1 2.8 %collective-permute-done = bf16[256,2048]{1,0:T(8,128)(2,1)} collective-permute-done((bf16[256,2048]{1,0:T(8,128)(2,1)S(1)}, bf16[256,2048]{1,0:T(8,128)(2,1)}, u32[]{:S(2)}, u32[]{:S(2)}) %collective-permute-start) | collective-permute-done | bytes 1048608 | tf_op jit(solution)/shard_map/ppermute | solution.py:253
  32.9 26.4 %all-to-all-done.refs_1_ = bf16[16,32,2176]{2,1,0:T(8,128)(2,1)S(1)} async-done(((bf16[16,32,2176]{2,1,0:T(8,128)(2,1)}), bf16[16,32,2176]{2,1,0:T(8,128)(2,1)S(1)}, u32[]{:S(2)}, u32[]{:S(2)}) %all-to-all-start) | async-done | bytes 2228256 | tf_op jit(solution)/shard_map/all_to_all | solution.py:275
  61.0 3.0 %collective-permute-done.1 = bf16[256,2176]{1,0:T(8,128)(2,1)S(1)} collective-permute-done((bf16[256,2176]{1,0:T(8,128)(2,1)S(1)}, bf16[256,2176]{1,0:T(8,128)(2,1)S(1)}, u32[]{:S(2)}, u32[]{:S(2)}) %collective-permute-start.1) | collective-permute-done | bytes 1114144 | tf_op jit(solution)/shard_map/ppermute | solution.py:253
  68.1 3.1 %collective-permute-start.5 = (bf16[1024,256]{1,0:T(8,128)(2,1)S(1)}, bf16[1024,256]{1,0:T(8,128)(2,1)S(1)}, u32[]{:S(2)}, u32[]{:S(2)}) collective-permute-start(bf16[1024,256]{1,0:T(8,128)(2,1)S(1)} %get-tuple-element.35), channel_id=1, source_target_pairs={{0,24},{8,0},{16,8},{24,16},{32,56},{40,32},{48,40},{56,48},{64,88... | collective-permute-start | bytes 1572872 | tf_op jit(solution)/shard_map/ppermute | solution.py:248
  72.1 3.2 %collective-permute-start.4 = (bf16[1024,256]{1,0:T(8,128)(2,1)S(1)}, bf16[1024,256]{1,0:T(8,128)(2,1)S(1)}, u32[]{:S(2)}, u32[]{:S(2)}) collective-permute-start(bf16[1024,256]{1,0:T(8,128)(2,1)S(1)} %get-tuple-element.37), channel_id=1, source_target_pairs={{0,96},{8,104},{16,112},{24,120},{32,0},{40,8},{48,16},{56,24},{64... | collective-permute-start | bytes 1572872 | tf_op jit(solution)/shard_map/ppermute | solution.py:245
  83.1 3.6 %collective-permute-done.2 = bf16[1024,256]{1,0:T(8,128)(2,1)S(1)} collective-permute-done((bf16[1024,256]{1,0:T(8,128)(2,1)S(1)}, bf16[1024,256]{1,0:T(8,128)(2,1)S(1)}, u32[]{:S(2)}, u32[]{:S(2)}) %collective-permute-start.2) | collective-permute-done | bytes 524320 | tf_op jit(solution)/shard_map/ppermute | solution.py:245
  89.4 3.0 %collective-permute-start.7 = (bf16[2048,256]{1,0:T(8,128)(2,1)}, bf16[2048,256]{1,0:T(8,128)(2,1)}, u32[]{:S(2)}, u32[]{:S(2)}) collective-permute-start(bf16[2048,256]{1,0:T(8,128)(2,1)} %pad_maximum_fusion.2), channel_id=1, source_target_pairs={{0,96},{8,104},{16,112},{24,120},{32,0},{40,8},{48,16},{56,24},{64... | collective-permute-start | bytes 3145736 | tf_op jit(solution)/shard_map/ppermute | solution.py:245
  97.1 11.4 %answer.1 = bf16[16,32,2176]{2,1,0:T(8,128)(2,1)} custom-call(s32[16]{0:T(128)} %broadcast_clamp_fusion.refs_0_, bf16[256,2176]{1,0:T(8,128)(2,1)} %bitcast.57, bf16[2048,4096]{1,0:T(8,128)(2,1)} %all-gather.2.cloned.1.call-done.refs_2_.refs_1_, bf16[256,4096]{1,0:T(8,128)(2,1)} %refs_3_.1), custom_call_target="tpu_custom_call" | custom-call | tf_op jit(solution)/shard_map/answer/pallas_call | solution.py:157
  108.5 7.0 %all-to-all-start.1 = ((bf16[16,32,2176]{2,1,0:T(8,128)(2,1)}), bf16[16,32,2176]{2,1,0:T(8,128)(2,1)S(1)}, u32[]{:S(2)}, u32[]{:S(2)}) async-start(bf16[16,32,2176]{2,1,0:T(8,128)(2,1)} %answer.1), calls=%async_computation.1 | async-start | bytes 4456448 | tf_op jit(solution)/shard_map/all_to_all | solution.py:328
  115.6 2.7 %collective-permute-done.8 = bf16[2048,256]{1,0:T(8,128)(2,1)} collective-permute-done((bf16[2048,256]{1,0:T(8,128)(2,1)}, bf16[2048,256]{1,0:T(8,128)(2,1)}, u32[]{:S(2)}, u32[]{:S(2)}) %collective-permute-start.8) | collective-permute-done | bytes 1048608 | tf_op jit(solution)/shard_map/ppermute | solution.py:248
  118.3 3.7 %collective-permute-done.6 = bf16[2048,256]{1,0:T(8,128)(2,1)} collective-permute-done((bf16[2048,256]{1,0:T(8,128)(2,1)}, bf16[2048,256]{1,0:T(8,128)(2,1)}, u32[]{:S(2)}, u32[]{:S(2)}) %collective-permute-start.6) | collective-permute-done | bytes 1048608 | tf_op jit(solution)/shard_map/ppermute | solution.py:245
  122.1 4.0 %add_convert_fusion = (bf16[2048,256]{1,0:T(8,128)(2,1)S(1)}, bf16[2048,256]{1,0:T(8,128)(2,1)S(1)}) fusion(bf16[2048,256]{1,0:T(8,128)(2,1)} %copy-done.5, f32[2048,256]{1,0:T(8,128)} %convolution_multiply_fusion, bf16[2048,256]{1,0:T(8,128)(2,1)} %collective-permute-done.8, bf16[2048,256]{1,0:T(8,128)(2,1)} %collective-permute-done.7, ...), kind=kLoop, calls=%fused_computation.23 | loop fusion | flops 5242880 | bytes 10485760 | tf_op jit(solution)/shard_map/convert_element_type | solution.py:306
  129.2 5.1 %collective-permute-start.11 = (bf16[2,512,256]{2,1,0:T(8,128)(2,1)}, bf16[2,512,256]{2,1,0:T(8,128)(2,1)}, u32[]{:S(2)}, u32[]{:S(2)}) collective-permute-start(bf16[2,512,256]{2,1,0:T(8,128)(2,1)} %get-tuple-element.31), channel_id=1, source_target_pairs={{0,4},{1,5},{2,6},{3,7},{4,0},{5,1},{6,2},{7,3},{8,12},{9,13},{10,... | collective-permute-start | bytes 1572872 | tf_op jit(solution)/shard_map/ppermute | solution.py:242
  134.4 9.9 %project.1 = bf16[256,4096]{1,0:T(8,128)(2,1)} custom-call(bf16[256,2176]{1,0:T(8,128)(2,1)} %bitcast.58, bf16[2048,4096]{1,0:T(8,128)(2,1)} %all-gather.2.cloned.1.call-done.refs_2_.refs_1_), custom_call_target="tpu_custom_call" | custom-call | tf_op jit(solution)/shard_map/project/pallas_call | solution.py:188
  146.0 6.0 %collective-permute-done.11 = bf16[2,512,256]{2,1,0:T(8,128)(2,1)} collective-permute-done((bf16[2,512,256]{2,1,0:T(8,128)(2,1)}, bf16[2,512,256]{2,1,0:T(8,128)(2,1)}, u32[]{:S(2)}, u32[]{:S(2)}) %collective-permute-start.11) | collective-permute-done | bytes 524320 | tf_op jit(solution)/shard_map/ppermute | solution.py:242
  162.5 3.0 %collective-permute-start.14 = (bf16[2,256,256]{2,1,0:T(8,128)(2,1)S(1)}, bf16[2,256,256]{2,1,0:T(8,128)(2,1)S(1)}, u32[]{:S(2)}, u32[]{:S(2)}) collective-permute-start(bf16[2,256,256]{2,1,0:T(8,128)(2,1)S(1)} %get-tuple-element.42), channel_id=1, source_target_pairs={{0,16},{8,24},{16,0},{24,8},{32,48},{40,56},{48,32},{56,40},{64,80... | collective-permute-start | bytes 786440 | tf_op jit(solution)/shard_map/ppermute | solution.py:248
  166.0 2.8 %collective-permute-done.20 = bf16[2,256,256]{2,1,0:T(8,128)(2,1)S(1)} collective-permute-done((bf16[2,256,256]{2,1,0:T(8,128)(2,1)S(1)}, bf16[2,256,256]{2,1,0:T(8,128)(2,1)S(1)}, u32[]{:S(2)}, u32[]{:S(2)}) %collective-permute-start.20) | collective-permute-done | bytes 262176 | tf_op jit(solution)/shard_map/ppermute | solution.py:245
  170.9 2.7 %collective-permute-done.21 = bf16[2,256,256]{2,1,0:T(8,128)(2,1)S(1)} collective-permute-done((bf16[2,256,256]{2,1,0:T(8,128)(2,1)S(1)}, bf16[2,256,256]{2,1,0:T(8,128)(2,1)S(1)}, u32[]{:S(2)}, u32[]{:S(2)}) %collective-permute-start.21) | collective-permute-done | bytes 262176 | tf_op jit(solution)/shard_map/ppermute | solution.py:245
  174.3 3.1 %collective-permute-start.24 = (bf16[2,256,256]{2,1,0:T(8,128)(2,1)S(1)}, bf16[2,256,256]{2,1,0:T(8,128)(2,1)S(1)}, u32[]{:S(2)}, u32[]{:S(2)}) collective-permute-start(bf16[2,256,256]{2,1,0:T(8,128)(2,1)S(1)} %add_convert_fusion.2.refs_5_), channel_id=1, source_target_pairs={{0,16},{8,24},{16,0},{24,8},{32,48},{40,56},{48,32},{56,40},{64,80... | collective-permute-start | bytes 786440 | tf_op jit(solution)/shard_map/ppermute | solution.py:248
  189.6 3.5 %collective-permute-done.18.refs_3_ = bf16[2,256,256]{2,1,0:T(8,128)(2,1)} collective-permute-done((bf16[2,256,256]{2,1,0:T(8,128)(2,1)S(1)}, bf16[2,256,256]{2,1,0:T(8,128)(2,1)}, u32[]{:S(2)}, u32[]{:S(2)}) %collective-permute-start.18) | collective-permute-done | bytes 262176 | tf_op jit(solution)/shard_map/ppermute | solution.py:245
  193.1 3.2 %place_blocks.1 = f32[256,4096]{1,0:T(8,128)} custom-call(s32[2]{0:T(128)S(1)} %pad_add_fusion.refs_0_, bf16[2,256,256]{2,1,0:T(8,128)(2,1)S(1)} %add_convert_fusion.3.refs_1_, bf16[2,256,256]{2,1,0:T(8,128)(2,1)} %collective-permute-done.17.refs_2_, bf16[2,256,256]{2,1,0:T(8,128)(2,1)} %collective-permute-done.18.refs_3_, ...), custom_call_target="tpu_custom_call" | custom-call | tf_op jit(solution)/shard_map/place_blocks/pallas_call | solution.py:218
  (100 shorter events, 54.1 us)
Async XLA Ops:
  7.2 90.0 %all-gather.2.cloned.1.call-start = ((), (), s32[]{:S(2)}) async-start(), calls=%async_computation.2 | async-start | bytes 18874368 | tf_op jit(solution)/shard_map/all_gather | solution.py:266
  19.1 40.1 %all-to-all-start = ((bf16[16,32,2176]{2,1,0:T(8,128)(2,1)}), bf16[16,32,2176]{2,1,0:T(8,128)(2,1)S(1)}, u32[]{:S(2)}, u32[]{:S(2)}) async-start(bf16[16,32,2176]{2,1,0:T(8,128)(2,1)} %bitcast.66), calls=%async_computation | async-start | bytes 4456448 | tf_op jit(solution)/shard_map/all_to_all | solution.py:275
  67.9 15.2 %collective-permute-start.3 = (bf16[1024,256]{1,0:T(8,128)(2,1)S(1)}, bf16[1024,256]{1,0:T(8,128)(2,1)S(1)}, u32[]{:S(2)}, u32[]{:S(2)}) collective-permute-start(bf16[1024,256]{1,0:T(8,128)(2,1)S(1)} %get-tuple-element.36), channel_id=1, source_target_pairs={{0,8},{8,16},{16,24},{24,0},{32,40},{40,48},{48,56},{56,32},{64,72... | collective-permute-start | bytes 1572872 | tf_op jit(solution)/shard_map/ppermute | solution.py:248
  68.1 15.0 %collective-permute-start.5 = (bf16[1024,256]{1,0:T(8,128)(2,1)S(1)}, bf16[1024,256]{1,0:T(8,128)(2,1)S(1)}, u32[]{:S(2)}, u32[]{:S(2)}) collective-permute-start(bf16[1024,256]{1,0:T(8,128)(2,1)S(1)} %get-tuple-element.35), channel_id=1, source_target_pairs={{0,24},{8,0},{16,8},{24,16},{32,56},{40,32},{48,40},{56,48},{64,88... | collective-permute-start | bytes 1572872 | tf_op jit(solution)/shard_map/ppermute | solution.py:248
  72.0 14.7 %collective-permute-start.2 = (bf16[1024,256]{1,0:T(8,128)(2,1)S(1)}, bf16[1024,256]{1,0:T(8,128)(2,1)S(1)}, u32[]{:S(2)}, u32[]{:S(2)}) collective-permute-start(bf16[1024,256]{1,0:T(8,128)(2,1)S(1)} %get-tuple-element.38), channel_id=1, source_target_pairs={{0,32},{8,40},{16,48},{24,56},{32,64},{40,72},{48,80},{56,88},{64,... | collective-permute-start | bytes 1572872 | tf_op jit(solution)/shard_map/ppermute | solution.py:245
  72.1 14.6 %collective-permute-start.4 = (bf16[1024,256]{1,0:T(8,128)(2,1)S(1)}, bf16[1024,256]{1,0:T(8,128)(2,1)S(1)}, u32[]{:S(2)}, u32[]{:S(2)}) collective-permute-start(bf16[1024,256]{1,0:T(8,128)(2,1)S(1)} %get-tuple-element.37), channel_id=1, source_target_pairs={{0,96},{8,104},{16,112},{24,120},{32,0},{40,8},{48,16},{56,24},{64... | collective-permute-start | bytes 1572872 | tf_op jit(solution)/shard_map/ppermute | solution.py:245
  87.9 27.6 %collective-permute-start.9 = (bf16[2048,256]{1,0:T(8,128)(2,1)}, bf16[2048,256]{1,0:T(8,128)(2,1)S(1)}, u32[]{:S(2)}, u32[]{:S(2)}) collective-permute-start(bf16[2048,256]{1,0:T(8,128)(2,1)} %pad_maximum_fusion.4), channel_id=1, source_target_pairs={{0,24},{8,0},{16,8},{24,16},{32,56},{40,32},{48,40},{56,48},{64,88... | collective-permute-start | bytes 3145736 | tf_op jit(solution)/shard_map/ppermute | solution.py:248
  89.4 26.2 %collective-permute-start.7 = (bf16[2048,256]{1,0:T(8,128)(2,1)}, bf16[2048,256]{1,0:T(8,128)(2,1)}, u32[]{:S(2)}, u32[]{:S(2)}) collective-permute-start(bf16[2048,256]{1,0:T(8,128)(2,1)} %pad_maximum_fusion.2), channel_id=1, source_target_pairs={{0,96},{8,104},{16,112},{24,120},{32,0},{40,8},{48,16},{56,24},{64... | collective-permute-start | bytes 3145736 | tf_op jit(solution)/shard_map/ppermute | solution.py:245
  93.5 24.8 %collective-permute-start.8 = (bf16[2048,256]{1,0:T(8,128)(2,1)}, bf16[2048,256]{1,0:T(8,128)(2,1)}, u32[]{:S(2)}, u32[]{:S(2)}) collective-permute-start(bf16[2048,256]{1,0:T(8,128)(2,1)} %pad_maximum_fusion.3), channel_id=1, source_target_pairs={{0,8},{8,16},{16,24},{24,0},{32,40},{40,48},{48,56},{56,32},{64,72... | collective-permute-start | bytes 3145736 | tf_op jit(solution)/shard_map/ppermute | solution.py:248
  96.6 25.5 %collective-permute-start.6 = (bf16[2048,256]{1,0:T(8,128)(2,1)}, bf16[2048,256]{1,0:T(8,128)(2,1)}, u32[]{:S(2)}, u32[]{:S(2)}) collective-permute-start(bf16[2048,256]{1,0:T(8,128)(2,1)} %pad_maximum_fusion.1), channel_id=1, source_target_pairs={{0,32},{8,40},{16,48},{24,56},{32,64},{40,72},{48,80},{56,88},{64,... | collective-permute-start | bytes 3145736 | tf_op jit(solution)/shard_map/ppermute | solution.py:245
  108.5 45.9 %all-to-all-start.1 = ((bf16[16,32,2176]{2,1,0:T(8,128)(2,1)}), bf16[16,32,2176]{2,1,0:T(8,128)(2,1)S(1)}, u32[]{:S(2)}, u32[]{:S(2)}) async-start(bf16[16,32,2176]{2,1,0:T(8,128)(2,1)} %answer.1), calls=%async_computation.1 | async-start | bytes 4456448 | tf_op jit(solution)/shard_map/all_to_all | solution.py:328
  128.3 17.7 %collective-permute-start.10 = (bf16[2,512,256]{2,1,0:T(8,128)(2,1)}, bf16[2,512,256]{2,1,0:T(8,128)(2,1)}, u32[]{:S(2)}, u32[]{:S(2)}) collective-permute-start(bf16[2,512,256]{2,1,0:T(8,128)(2,1)} %get-tuple-element.30), channel_id=1, source_target_pairs={{0,2},{1,3},{2,4},{3,5},{4,6},{5,7},{6,0},{7,1},{8,10},{9,11},{10,... | collective-permute-start | bytes 1572872 | tf_op jit(solution)/shard_map/ppermute | solution.py:242
  129.2 22.7 %collective-permute-start.11 = (bf16[2,512,256]{2,1,0:T(8,128)(2,1)}, bf16[2,512,256]{2,1,0:T(8,128)(2,1)}, u32[]{:S(2)}, u32[]{:S(2)}) collective-permute-start(bf16[2,512,256]{2,1,0:T(8,128)(2,1)} %get-tuple-element.31), channel_id=1, source_target_pairs={{0,4},{1,5},{2,6},{3,7},{4,0},{5,1},{6,2},{7,3},{8,12},{9,13},{10,... | collective-permute-start | bytes 1572872 | tf_op jit(solution)/shard_map/ppermute | solution.py:242
  134.4 17.6 %collective-permute-start.12 = (bf16[2,512,256]{2,1,0:T(8,128)(2,1)}, bf16[2,512,256]{2,1,0:T(8,128)(2,1)}, u32[]{:S(2)}, u32[]{:S(2)}) collective-permute-start(bf16[2,512,256]{2,1,0:T(8,128)(2,1)} %get-tuple-element.32), channel_id=1, source_target_pairs={{0,6},{1,7},{2,0},{3,1},{4,2},{5,3},{6,4},{7,5},{8,14},{9,15},{10,... | collective-permute-start | bytes 1572872 | tf_op jit(solution)/shard_map/ppermute | solution.py:242
  158.1 10.8 %collective-permute-start.20 = (bf16[2,256,256]{2,1,0:T(8,128)(2,1)S(1)}, bf16[2,256,256]{2,1,0:T(8,128)(2,1)S(1)}, u32[]{:S(2)}, u32[]{:S(2)}) collective-permute-start(bf16[2,256,256]{2,1,0:T(8,128)(2,1)S(1)} %get-tuple-element.41), channel_id=1, source_target_pairs={{0,64},{8,72},{16,80},{24,88},{32,96},{40,104},{48,112},{56,120},{... | collective-permute-start | bytes 786440 | tf_op jit(solution)/shard_map/ppermute | solution.py:245
  159.2 14.4 %collective-permute-start.21 = (bf16[2,256,256]{2,1,0:T(8,128)(2,1)S(1)}, bf16[2,256,256]{2,1,0:T(8,128)(2,1)S(1)}, u32[]{:S(2)}, u32[]{:S(2)}) collective-permute-start(bf16[2,256,256]{2,1,0:T(8,128)(2,1)S(1)} %get-tuple-element.41), channel_id=1, source_target_pairs={{0,32},{8,40},{16,48},{24,56},{32,64},{40,72},{48,80},{56,88},{64,... | collective-permute-start | bytes 786440 | tf_op jit(solution)/shard_map/ppermute | solution.py:245
  159.8 13.8 %collective-permute-start.22 = (bf16[2,256,256]{2,1,0:T(8,128)(2,1)S(1)}, bf16[2,256,256]{2,1,0:T(8,128)(2,1)S(1)}, u32[]{:S(2)}, u32[]{:S(2)}) collective-permute-start(bf16[2,256,256]{2,1,0:T(8,128)(2,1)S(1)} %get-tuple-element.41), channel_id=1, source_target_pairs={{0,96},{8,104},{16,112},{24,120},{32,0},{40,8},{48,16},{56,24},{64... | collective-permute-start | bytes 786440 | tf_op jit(solution)/shard_map/ppermute | solution.py:245
  162.5 15.0 %collective-permute-start.14 = (bf16[2,256,256]{2,1,0:T(8,128)(2,1)S(1)}, bf16[2,256,256]{2,1,0:T(8,128)(2,1)S(1)}, u32[]{:S(2)}, u32[]{:S(2)}) collective-permute-start(bf16[2,256,256]{2,1,0:T(8,128)(2,1)S(1)} %get-tuple-element.42), channel_id=1, source_target_pairs={{0,16},{8,24},{16,0},{24,8},{32,48},{40,56},{48,32},{56,40},{64,80... | collective-permute-start | bytes 786440 | tf_op jit(solution)/shard_map/ppermute | solution.py:248
  165.4 12.3 %collective-permute-start.15 = (bf16[2,256,256]{2,1,0:T(8,128)(2,1)S(1)}, bf16[2,256,256]{2,1,0:T(8,128)(2,1)S(1)}, u32[]{:S(2)}, u32[]{:S(2)}) collective-permute-start(bf16[2,256,256]{2,1,0:T(8,128)(2,1)S(1)} %get-tuple-element.42), channel_id=1, source_target_pairs={{0,8},{8,16},{16,24},{24,0},{32,40},{40,48},{48,56},{56,32},{64,72... | collective-permute-start | bytes 786440 | tf_op jit(solution)/shard_map/ppermute | solution.py:248
  173.7 10.1 %collective-permute-start.23 = (bf16[2,256,256]{2,1,0:T(8,128)(2,1)S(1)}, bf16[2,256,256]{2,1,0:T(8,128)(2,1)S(1)}, u32[]{:S(2)}, u32[]{:S(2)}) collective-permute-start(bf16[2,256,256]{2,1,0:T(8,128)(2,1)S(1)} %add_convert_fusion.2.refs_5_), channel_id=1, source_target_pairs={{0,8},{8,16},{16,24},{24,0},{32,40},{40,48},{48,56},{56,32},{64,72... | collective-permute-start | bytes 786440 | tf_op jit(solution)/shard_map/ppermute | solution.py:248
  174.3 14.8 %collective-permute-start.24 = (bf16[2,256,256]{2,1,0:T(8,128)(2,1)S(1)}, bf16[2,256,256]{2,1,0:T(8,128)(2,1)S(1)}, u32[]{:S(2)}, u32[]{:S(2)}) collective-permute-start(bf16[2,256,256]{2,1,0:T(8,128)(2,1)S(1)} %add_convert_fusion.2.refs_5_), channel_id=1, source_target_pairs={{0,16},{8,24},{16,0},{24,8},{32,48},{40,56},{48,32},{56,40},{64,80... | collective-permute-start | bytes 786440 | tf_op jit(solution)/shard_map/ppermute | solution.py:248
  177.5 12.1 %collective-permute-start.25 = (bf16[2,256,256]{2,1,0:T(8,128)(2,1)S(1)}, bf16[2,256,256]{2,1,0:T(8,128)(2,1)S(1)}, u32[]{:S(2)}, u32[]{:S(2)}) collective-permute-start(bf16[2,256,256]{2,1,0:T(8,128)(2,1)S(1)} %add_convert_fusion.2.refs_5_), channel_id=1, source_target_pairs={{0,24},{8,0},{16,8},{24,16},{32,56},{40,32},{48,40},{56,48},{64,88... | collective-permute-start | bytes 786440 | tf_op jit(solution)/shard_map/ppermute | solution.py:248
  177.9 11.7 %collective-permute-start.17 = (bf16[2,256,256]{2,1,0:T(8,128)(2,1)S(1)}, bf16[2,256,256]{2,1,0:T(8,128)(2,1)}, u32[]{:S(2)}, u32[]{:S(2)}) collective-permute-start(bf16[2,256,256]{2,1,0:T(8,128)(2,1)S(1)} %add_convert_fusion.3.refs_1_), channel_id=1, source_target_pairs={{0,32},{8,40},{16,48},{24,56},{32,64},{40,72},{48,80},{56,88},{64,... | collective-permute-start | bytes 786440 | tf_op jit(solution)/shard_map/ppermute | solution.py:245
  179.4 13.7 %collective-permute-start.18 = (bf16[2,256,256]{2,1,0:T(8,128)(2,1)S(1)}, bf16[2,256,256]{2,1,0:T(8,128)(2,1)}, u32[]{:S(2)}, u32[]{:S(2)}) collective-permute-start(bf16[2,256,256]{2,1,0:T(8,128)(2,1)S(1)} %add_convert_fusion.3.refs_1_), channel_id=1, source_target_pairs={{0,64},{8,72},{16,80},{24,88},{32,96},{40,104},{48,112},{56,120},{... | collective-permute-start | bytes 786440 | tf_op jit(solution)/shard_map/ppermute | solution.py:245
  (12 other events, 72.8 us)
Sparse Core Ops, SparseCore 0:
  9.7 87.3 all-gather.1

commit v4 on v3

--- a/solution.py
+++ b/solution.py
@@ -39,21 +39,19 @@
     for step in range(steps):
         fetch(step).start()
 
-    lane = lax.broadcasted_iota(jnp.int32, (block, EXTRA), 1)
     tokens = lax.broadcasted_iota(jnp.int32, (block, count), 1)
     for peer in range(rows // block):
         found = jnp.int32(blocks)
         for b in range(blocks):
             found = jnp.where(owner_ref[b] == peer, b, found)
-        there = found < blocks
         start = pl.multiple_of(jnp.minimum(found, blocks - 1) * block, block)
-        listed = jnp.where(there, listed_ref[pl.ds(start, block), :], -1)
-        hit = listed == tokens
-        span = slice(peer * block, (peer + 1) * block)
-        onehot_ref[span, :] = hit.astype(jnp.bfloat16)
-        logit = jnp.sum(jnp.where(hit, logit_ref[...], 0.0), axis=1, keepdims=True)
-        mark = jnp.where(there, 1.0, 0.0)
-        picked[span, width:] = jnp.where(lane == 0, jax.nn.sigmoid(logit), mark).astype(jnp.bfloat16)
+        listed = jnp.where(found < blocks, listed_ref[pl.ds(start, block), :], -1)
+        onehot_ref[peer * block : (peer + 1) * block, :] = (listed == tokens).astype(jnp.bfloat16)
+    first = lax.broadcasted_iota(jnp.int32, (EXTRA, count), 0) == 0
+    extra = jnp.where(first, jax.nn.sigmoid(logit_ref[...]), 1.0).astype(jnp.bfloat16)
+    picked[:, width:] = lax.dot_general(
+        onehot_ref[...], extra, (((1,), (1,)), ((), ())), preferred_element_type=jnp.float32
+    ).astype(jnp.bfloat16)
     hand_over(steps).start()
 
     for step in range(steps):
@@ -214,13 +212,16 @@
     side = len(first)
     halves, rows, columns = first[0].shape
     model = halves * 2 * side * columns
-    block = pl.BlockSpec((1, rows, columns), lambda h: (h, 0, 0))
+    block = pl.BlockSpec((1, rows, columns), lambda h, spot_ref: (h, 0, 0))
     return pl.pallas_call(
         lambda *refs: place_body(side, *refs),
         out_shape=jax.ShapeDtypeStruct((rows, model), jnp.float32),
-        grid=(halves,),
-        in_specs=[pl.BlockSpec(memory_space=pltpu.SMEM)] + [block] * (2 * side),
-        out_specs=pl.BlockSpec((rows, model // halves), lambda h: (0, h)),
+        grid_spec=pltpu.PrefetchScalarGridSpec(
+            num_scalar_prefetch=1,
+            grid=(halves,),
+            in_specs=[block] * (2 * side),
+            out_specs=pl.BlockSpec((rows, model // halves), lambda h, spot_ref: (0, (h + spot_ref[2]) % halves)),
+        ),
         compiler_params=params(),
         cost_estimate=NO_COST,
         name="place_blocks",
@@ -290,7 +291,6 @@
     weighted = (gate[:, None] * both_cot.astype(jnp.float32)).astype(jnp.bfloat16)
     both_rows = both[:, :width]
     part = half // (2 * side)
-    cut = width // 2
 
     def term(first, index):
         columns = lax.dynamic_slice(weighted, (0, first + index % side * part), (2 * rows, part))
@@ -305,13 +305,14 @@
     def narrow(value):
         return value.astype(jnp.bfloat16)
 
+    cut = width // 2
     far_y, far_z = narrow(term(0, y + 2)), narrow(term(half // 2, z + 2))
     got_parts = (
         along_y(far_y[:cut], 1), along_z(far_z[:cut], 1), along_y(far_y[cut:], -1), along_z(far_z[cut:], -1)
     )
     ahead_y, ahead_z = term(0, y + 1), term(half // 2, z + 1)
     behind_y, behind_z = term(0, y + side - 1), term(half // 2, z + side - 1)
-    own_y, own_z = term(0, y), term(half // 2, z)
+    own_y, own_z = narrow(term(0, y)), narrow(term(half // 2, z))
     got_parts = after(got_parts, ahead_y, ahead_z, behind_y, behind_z, own_y, own_z)
     low_y, low_z, high_y, high_z = [wide(part_sum) for part_sum in got_parts]
     sent = (
@@ -328,35 +329,42 @@
     returned = lax.all_to_all(back, "dp", split_axis=0, concat_axis=0, tiled=True)
     from_y, to_y, from_z, to_z = after((from_y, to_y, from_z, to_z), back)
 
-    sum_y = narrow(own_y + wide(from_y) + wide(to_y))
-    sum_z = narrow(own_z + wide(from_z) + wide(to_z))
-
-    share = shard // side
-
-    def exchange(value, axis, place, along):
-        count = value.shape[axis]
-        total = wide(at(value, place, axis))
-        for ahead in range(1, count):
-            total += wide(along(at(value, (place + ahead) % count, axis), ahead))
+    def rows_of(ahead):
+        start = (chip + ahead) % chips * (2 * shard)
+
+        def cut_out(value):
+            return wide(lax.dynamic_slice(value, (start, 0), (2 * shard, part)))
+
+        return jnp.stack(
+            [
+                cut_out(own) + cut_out(up) + cut_out(down)
+                for own, up, down in ((own_y, from_y, to_y), (own_z, from_z, to_z))
+            ]
+        )
+
+    order = [2, 1] + list(range(3, chips))
+    chunks = [narrow(rows_of(ahead)) for ahead in order]
+    terms = [rows_of(0)] + [along_x(chunk, ahead) for chunk, ahead in zip(chunks, order)]
+    update = project(after(held, *chunks), weight)
+    terms = after(terms, returned, update)
+
+    def rows_for(which):
+        total = sum(wide(at(term_x.reshape(2, 2, shard, part), which, 1)) for term_x in terms)
         return narrow(total)
 
-    sums = jnp.stack([sum_y, sum_z]).reshape(2, chips, 2 * shard, part)
-    update = project(after(held, sums), weight)
-    sums = exchange(sums, 1, chip, along_x)
-    sums = after(sums, returned, update).reshape(2, 2, shard, part)
-    keep, take = at(sums, core, 1), to_partner(at(sums, 1 - core, 1))
-    first = core == 0
-    piece = jnp.stack([jnp.where(first, keep, take), jnp.where(first, take, keep)], axis=1)
+    take = to_partner(rows_for(1 - core))
+    keep = rows_for(core)
 
     def around(value, along):
         return [value] + [along(value, ahead) for ahead in range(1, side)]
 
     def whole(value, along):
-        terms = [wide(term) for term in around(value, along)]
-        return narrow((terms[0] + terms[2]) + (terms[1] + terms[3]))
-
-    sum_y, sum_z = whole(piece[0], along_z), whole(piece[1], along_y)
-    spot = jnp.stack([y, z]).astype(jnp.int32)
+        values = [wide(one) for one in around(value, along)]
+        return narrow((values[0] + values[2]) + (values[1] + values[3]))
+
+    sum_y = whole(jnp.stack([keep[0], take[0]]), along_z)
+    sum_z = whole(jnp.stack([keep[1], take[1]]), along_y)
+    spot = jnp.stack([y, z, core]).astype(jnp.int32)
     grad_weight = place_blocks(spot, around(sum_y, along_y), around(sum_z, along_z))
 
     grad_context = move_blocks(returned, owner, width).reshape(slots, width)

time: 204 us -> 201 us (0.985)
    another operation x7 -> x14, other arithmetic: 1.75 us -> 9.18 us  [the longest x5 6.8 us: rows_of(): jnp.stack([cut_out(own) + cut_out(up) + cut_out(down) for own, up, down i...]
    convert_element_type x4 -> x2, other arithmetic: 6.7 us -> 0.26 us  [narrow(): return value.astype(jnp.bfloat16)]
    all_gather x1, waiting for transfers between devices: 0.04 us -> 2.09 us  [on_device(): weight = lax.all_gather(out_weight, 'fsdp', axis=0, tiled=True)]
  transfers between devices with their start and end apart: 29 -> 29, of which waited for: 17 -> 17; matrix products, arithmetic and copies ran while one was open for 15% -> 14% of each run, Pallas kernels for 17% -> 16%
where the time goes in v4:
time: 201 us; the launch traced here: 200 us
  waiting for transfers between devices  66.8 us (33%)
  starting transfers between devices  51.6 us (26%)
  Pallas kernels  36.6 us (18%)
  other arithmetic  17 us (8%)
  between operations  14.7 us (7%)
  matrix products  7.15 us (4%)
  local copies, waits for them, and re-layouts  6.2 us (3%)
    all_to_all x1, waiting for transfers between devices, on_device(): got = lax.all_to_all(send, 'dp', split_axis=0, concat_axis=0, tiled=True)  26.1 us
    ppermute x10, waiting for transfers between devices, along_y(): lax.ppermute(value, 'dp', [(d, (d + side * ahead) % n_dp) for d in range(...  15.6 us
    ppermute x10, starting transfers between devices, along_z(): lax.ppermute(value, 'dp', [(d, d // side * side + (d + ahead) % side) for...  15.1 us
    ppermute x10, starting transfers between devices, along_y(): lax.ppermute(value, 'dp', [(d, (d + side * ahead) % n_dp) for d in range(...  15 us
    pallas_call x1, Pallas kernels, answer(): pl.pallas_call(lambda *refs: answer_body(width, *refs), out_shape=jax.Sha...  11.4 us
    pallas_call x1, Pallas kernels, project(): pl.pallas_call(lambda *refs: project_body(width, *refs), out_shape=jax.Sh...  9.92 us
    ppermute x3, waiting for transfers between devices, along_x(): lax.ppermute(value, 'fsdp', [(f, (f + 2 * ahead) % n_fsdp) for f in range...  9.52 us
    pallas_call x1, Pallas kernels, pick_rows(): pl.pallas_call(pick_body, out_shape=jax.ShapeDtypeStruct((rows, width + E...  8.64 us
  transfers between devices with their start and end apart: 29, of which 17 were waited for; matrix products, arithmetic and copies ran while one was open for 14% of the time, Pallas kernels for 16%

profile of v4, /device:TPU:0, one launch (start us, length us, event | category | flops | bytes accessed | tf_op | source)
XLA Modules:
  0.0 200.1 jit_solution(15707393349622792970)
XLA Ops:
  8.8 8.6 %pick_rows.1 = bf16[512,2176]{1,0:T(8,128)(2,1)} custom-call(s32[16]{0:T(128)} %bitcast.49, s32[512,1]{1,0:T(8,128)} %copy.13.listed_ref, f32[1,2048]{1,0:T(1,128)} %bitcast.56, bf16[2048,2048]{1,0:T(8,128)(2,1)} %head_ref.1), custom_call_target="tpu_custom_call" | custom-call | tf_op jit(solution)/shard_map/pick_rows/pallas_call | solution.py:73
  17.4 8.1 %all-to-all-start = ((bf16[16,32,2176]{2,1,0:T(8,128)(2,1)}), bf16[16,32,2176]{2,1,0:T(8,128)(2,1)S(1)}, u32[]{:S(2)}, u32[]{:S(2)}) async-start(bf16[16,32,2176]{2,1,0:T(8,128)(2,1)} %bitcast.52), calls=%async_computation | async-start | bytes 4456448 | tf_op jit(solution)/shard_map/all_to_all | solution.py:276
  25.6 3.0 %constant_dynamic-slice_fusion = (bf16[256,2048]{1,0:T(8,128)(2,1)}, bf16[256,2048]{1,0:T(8,128)(2,1)S(1)}) fusion(bf16[256,4096]{1,0:T(8,128)(2,1)} %refs_3_.1, s32[]{:T(128)S(6)} %select_n.153, s32[]{:T(128)S(6)} %select_n.151), kind=kLoop, calls=%fused_computation.81 | loop fusion | bytes 4194312 | tf_op jit(solution)/shard_map/dynamic_slice | solution.py:269
  28.7 2.8 %collective-permute-done = bf16[256,2048]{1,0:T(8,128)(2,1)} collective-permute-done((bf16[256,2048]{1,0:T(8,128)(2,1)S(1)}, bf16[256,2048]{1,0:T(8,128)(2,1)}, u32[]{:S(2)}, u32[]{:S(2)}) %collective-permute-start) | collective-permute-done | bytes 1048608 | tf_op jit(solution)/shard_map/ppermute | solution.py:254
  31.4 26.1 %all-to-all-done.refs_1_ = bf16[16,32,2176]{2,1,0:T(8,128)(2,1)S(1)} async-done(((bf16[16,32,2176]{2,1,0:T(8,128)(2,1)}), bf16[16,32,2176]{2,1,0:T(8,128)(2,1)S(1)}, u32[]{:S(2)}, u32[]{:S(2)}) %all-to-all-start) | async-done | bytes 2228256 | tf_op jit(solution)/shard_map/all_to_all | solution.py:276
  66.4 2.8 %collective-permute-start.5 = (bf16[1024,256]{1,0:T(8,128)(2,1)S(1)}, bf16[1024,256]{1,0:T(8,128)(2,1)S(1)}, u32[]{:S(2)}, u32[]{:S(2)}) collective-permute-start(bf16[1024,256]{1,0:T(8,128)(2,1)S(1)} %get-tuple-element.48), channel_id=1, source_target_pairs={{0,24},{8,0},{16,8},{24,16},{32,56},{40,32},{48,40},{56,48},{64,88... | collective-permute-start | bytes 1572872 | tf_op jit(solution)/shard_map/ppermute | solution.py:249
  70.2 3.2 %collective-permute-start.4 = (bf16[1024,256]{1,0:T(8,128)(2,1)S(1)}, bf16[1024,256]{1,0:T(8,128)(2,1)S(1)}, u32[]{:S(2)}, u32[]{:S(2)}) collective-permute-start(bf16[1024,256]{1,0:T(8,128)(2,1)S(1)} %get-tuple-element.50), channel_id=1, source_target_pairs={{0,96},{8,104},{16,112},{24,120},{32,0},{40,8},{48,16},{56,24},{64... | collective-permute-start | bytes 1572872 | tf_op jit(solution)/shard_map/ppermute | solution.py:246
  81.0 3.6 %collective-permute-done.2 = bf16[1024,256]{1,0:T(8,128)(2,1)S(1)} collective-permute-done((bf16[1024,256]{1,0:T(8,128)(2,1)S(1)}, bf16[1024,256]{1,0:T(8,128)(2,1)S(1)}, u32[]{:S(2)}, u32[]{:S(2)}) %collective-permute-start.2) | collective-permute-done | bytes 524320 | tf_op jit(solution)/shard_map/ppermute | solution.py:246
  90.3 3.0 %collective-permute-start.7 = (bf16[2048,256]{1,0:T(8,128)(2,1)}, bf16[2048,256]{1,0:T(8,128)(2,1)}, u32[]{:S(2)}, u32[]{:S(2)}) collective-permute-start(bf16[2048,256]{1,0:T(8,128)(2,1)} %pad_maximum_fusion.1), channel_id=1, source_target_pairs={{0,96},{8,104},{16,112},{24,120},{32,0},{40,8},{48,16},{56,24},{64... | collective-permute-start | bytes 3145736 | tf_op jit(solution)/shard_map/ppermute | solution.py:246
  97.1 11.4 %answer.1 = bf16[16,32,2176]{2,1,0:T(8,128)(2,1)} custom-call(s32[16]{0:T(128)} %broadcast_clamp_fusion.refs_0_, bf16[256,2176]{1,0:T(8,128)(2,1)} %bitcast.47, bf16[2048,4096]{1,0:T(8,128)(2,1)} %all-gather.2.cloned.1.call-done.refs_2_.refs_1_, bf16[256,4096]{1,0:T(8,128)(2,1)} %refs_3_.1), custom_call_target="tpu_custom_call" | custom-call | tf_op jit(solution)/shard_map/answer/pallas_call | solution.py:155
  108.5 7.0 %all-to-all-start.1 = ((bf16[16,32,2176]{2,1,0:T(8,128)(2,1)}), bf16[16,32,2176]{2,1,0:T(8,128)(2,1)S(1)}, u32[]{:S(2)}, u32[]{:S(2)}) async-start(bf16[16,32,2176]{2,1,0:T(8,128)(2,1)} %answer.1), calls=%async_computation.1 | async-start | bytes 4456448 | tf_op jit(solution)/shard_map/all_to_all | solution.py:329
  115.6 3.0 %collective-permute-done.6 = bf16[2048,256]{1,0:T(8,128)(2,1)} collective-permute-done((bf16[2048,256]{1,0:T(8,128)(2,1)}, bf16[2048,256]{1,0:T(8,128)(2,1)}, u32[]{:S(2)}, u32[]{:S(2)}) %collective-permute-start.6) | collective-permute-done | bytes 1048608 | tf_op jit(solution)/shard_map/ppermute | solution.py:246
  118.6 4.2 %add_bitcast_fusion = (f32[1,512,256]{2,1,0:T(8,128)}, bf16[1,512,256]{2,1,0:T(8,128)(2,1)S(1)}, bf16[1,512,256]{2,1,0:T(8,128)(2,1)S(1)}, bf16[1,512,256]{2,1,0...) fusion(bf16[2048,256]{1,0:T(8,128)(2,1)} %collective-permute-do, ...), kind=kLoop, calls=%fused_computation.40 | loop fusion | flops 6029312 | bytes 8912912 | tf_op jit(solution)/shard_map/stack | solution.py:338
  123.7 4.7 %collective-permute-start.12 = (bf16[2,512,256]{2,1,0:T(8,128)(2,1)}, bf16[2,512,256]{2,1,0:T(8,128)(2,1)}, u32[]{:S(2)}, u32[]{:S(2)}) collective-permute-start(bf16[2,512,256]{2,1,0:T(8,128)(2,1)} %pad_maximum_fusion.7), channel_id=1, source_target_pairs={{0,6},{1,7},{2,0},{3,1},{4,2},{5,3},{6,4},{7,5},{8,14},{9,15},{10,... | collective-permute-start | bytes 1572872 | tf_op jit(solution)/shard_map/ppermute | solution.py:243
  131.5 9.9 %project.1 = bf16[256,4096]{1,0:T(8,128)(2,1)} custom-call(bf16[256,2176]{1,0:T(8,128)(2,1)} %bitcast.48, bf16[2048,4096]{1,0:T(8,128)(2,1)} %all-gather.2.cloned.1.call-done.refs_2_.refs_1_), custom_call_target="tpu_custom_call" | custom-call | tf_op jit(solution)/shard_map/project/pallas_call | solution.py:186
  141.5 5.3 %collective-permute-done.12 = bf16[2,512,256]{2,1,0:T(8,128)(2,1)} collective-permute-done((bf16[2,512,256]{2,1,0:T(8,128)(2,1)}, bf16[2,512,256]{2,1,0:T(8,128)(2,1)}, u32[]{:S(2)}, u32[]{:S(2)}) %collective-permute-start.12) | collective-permute-done | bytes 524320 | tf_op jit(solution)/shard_map/ppermute | solution.py:243
  146.8 4.3 %collective-permute-done.11 = bf16[2,512,256]{2,1,0:T(8,128)(2,1)} collective-permute-done((bf16[2,512,256]{2,1,0:T(8,128)(2,1)}, bf16[2,512,256]{2,1,0:T(8,128)(2,1)}, u32[]{:S(2)}, u32[]{:S(2)}) %collective-permute-start.11) | collective-permute-done | bytes 524320 | tf_op jit(solution)/shard_map/ppermute | solution.py:243
  156.2 2.7 %collective-permute-start.22 = (bf16[2,256,256]{2,1,0:T(8,128)(2,1)S(1)}, bf16[2,256,256]{2,1,0:T(8,128)(2,1)S(1)}, u32[]{:S(2)}, u32[]{:S(2)}) collective-permute-start(bf16[2,256,256]{2,1,0:T(8,128)(2,1)S(1)} %pad_maximum_fusion.9), channel_id=1, source_target_pairs={{0,96},{8,104},{16,112},{24,120},{32,0},{40,8},{48,16},{56,24},{64... | collective-permute-start | bytes 786440 | tf_op jit(solution)/shard_map/ppermute | solution.py:246
  158.9 3.0 %collective-permute-start.14 = (bf16[2,256,256]{2,1,0:T(8,128)(2,1)S(1)}, bf16[2,256,256]{2,1,0:T(8,128)(2,1)S(1)}, u32[]{:S(2)}, u32[]{:S(2)}) collective-permute-start(bf16[2,256,256]{2,1,0:T(8,128)(2,1)S(1)} %pad_maximum_fusion.8), channel_id=1, source_target_pairs={{0,16},{8,24},{16,0},{24,8},{32,48},{40,56},{48,32},{56,40},{64,80... | collective-permute-start | bytes 786440 | tf_op jit(solution)/shard_map/ppermute | solution.py:249
  167.2 2.7 %collective-permute-done.21 = bf16[2,256,256]{2,1,0:T(8,128)(2,1)S(1)} collective-permute-done((bf16[2,256,256]{2,1,0:T(8,128)(2,1)S(1)}, bf16[2,256,256]{2,1,0:T(8,128)(2,1)S(1)}, u32[]{:S(2)}, u32[]{:S(2)}) %collective-permute-start.21) | collective-permute-done | bytes 262176 | tf_op jit(solution)/shard_map/ppermute | solution.py:246
  170.7 3.0 %collective-permute-start.24 = (bf16[2,256,256]{2,1,0:T(8,128)(2,1)S(1)}, bf16[2,256,256]{2,1,0:T(8,128)(2,1)S(1)}, u32[]{:S(2)}, u32[]{:S(2)}) collective-permute-start(bf16[2,256,256]{2,1,0:T(8,128)(2,1)S(1)} %add_convert_fusion.refs_5_), channel_id=1, source_target_pairs={{0,16},{8,24},{16,0},{24,8},{32,48},{40,56},{48,32},{56,40},{64,80... | collective-permute-start | bytes 786440 | tf_op jit(solution)/shard_map/ppermute | solution.py:249
  175.8 2.6 %collective-permute-start.18 = (bf16[2,256,256]{2,1,0:T(8,128)(2,1)S(1)}, bf16[2,256,256]{2,1,0:T(8,128)(2,1)}, u32[]{:S(2)}, u32[]{:S(2)}) collective-permute-start(bf16[2,256,256]{2,1,0:T(8,128)(2,1)S(1)} %add_convert_fusion.1.refs_1_), channel_id=1, source_target_pairs={{0,64},{8,72},{16,80},{24,88},{32,96},{40,104},{48,112},{56,120},{... | collective-permute-start | bytes 786440 | tf_op jit(solution)/shard_map/ppermute | solution.py:246
  185.9 3.6 %collective-permute-done.18.refs_3_ = bf16[2,256,256]{2,1,0:T(8,128)(2,1)} collective-permute-done((bf16[2,256,256]{2,1,0:T(8,128)(2,1)S(1)}, bf16[2,256,256]{2,1,0:T(8,128)(2,1)}, u32[]{:S(2)}, u32[]{:S(2)}) %collective-permute-start.18) | collective-permute-done | bytes 262176 | tf_op jit(solution)/shard_map/ppermute | solution.py:246
  189.5 3.7 %place_blocks.1 = f32[256,4096]{1,0:T(8,128)} custom-call(s32[3]{0:T(128)S(1)} %pad_add_fusion.refs_0_, bf16[2,256,256]{2,1,0:T(8,128)(2,1)S(1)} %add_convert_fusion.1.refs_1_, bf16[2,256,256]{2,1,0:T(8,128)(2,1)} %collective-permute-done.17.refs_2_, bf16[2,256,256]{2,1,0:T(8,128)(2,1)} %collective-permute-done.18.refs_3_, ...), custom_call_target="tpu_custom_call" | custom-call | tf_op jit(solution)/shard_map/place_blocks/pallas_call | solution.py:216
  (102 shorter events, 52.9 us)
Async XLA Ops:
  7.2 90.0 %all-gather.2.cloned.1.call-start = ((), (), s32[]{:S(2)}) async-start(), calls=%async_computation.2 | async-start | bytes 18874368 | tf_op jit(solution)/shard_map/all_gather | solution.py:267
  17.4 40.2 %all-to-all-start = ((bf16[16,32,2176]{2,1,0:T(8,128)(2,1)}), bf16[16,32,2176]{2,1,0:T(8,128)(2,1)S(1)}, u32[]{:S(2)}, u32[]{:S(2)}) async-start(bf16[16,32,2176]{2,1,0:T(8,128)(2,1)} %bitcast.52), calls=%async_computation | async-start | bytes 4456448 | tf_op jit(solution)/shard_map/all_to_all | solution.py:276
  65.9 15.1 %collective-permute-start.3 = (bf16[1024,256]{1,0:T(8,128)(2,1)S(1)}, bf16[1024,256]{1,0:T(8,128)(2,1)S(1)}, u32[]{:S(2)}, u32[]{:S(2)}) collective-permute-start(bf16[1024,256]{1,0:T(8,128)(2,1)S(1)} %get-tuple-element.49), channel_id=1, source_target_pairs={{0,8},{8,16},{16,24},{24,0},{32,40},{40,48},{48,56},{56,32},{64,72... | collective-permute-start | bytes 1572872 | tf_op jit(solution)/shard_map/ppermute | solution.py:249
  66.4 14.6 %collective-permute-start.5 = (bf16[1024,256]{1,0:T(8,128)(2,1)S(1)}, bf16[1024,256]{1,0:T(8,128)(2,1)S(1)}, u32[]{:S(2)}, u32[]{:S(2)}) collective-permute-start(bf16[1024,256]{1,0:T(8,128)(2,1)S(1)} %get-tuple-element.48), channel_id=1, source_target_pairs={{0,24},{8,0},{16,8},{24,16},{32,56},{40,32},{48,40},{56,48},{64,88... | collective-permute-start | bytes 1572872 | tf_op jit(solution)/shard_map/ppermute | solution.py:249
  70.1 14.6 %collective-permute-start.2 = (bf16[1024,256]{1,0:T(8,128)(2,1)S(1)}, bf16[1024,256]{1,0:T(8,128)(2,1)S(1)}, u32[]{:S(2)}, u32[]{:S(2)}) collective-permute-start(bf16[1024,256]{1,0:T(8,128)(2,1)S(1)} %get-tuple-element.51), channel_id=1, source_target_pairs={{0,32},{8,40},{16,48},{24,56},{32,64},{40,72},{48,80},{56,88},{64,... | collective-permute-start | bytes 1572872 | tf_op jit(solution)/shard_map/ppermute | solution.py:246
  70.2 14.5 %collective-permute-start.4 = (bf16[1024,256]{1,0:T(8,128)(2,1)S(1)}, bf16[1024,256]{1,0:T(8,128)(2,1)S(1)}, u32[]{:S(2)}, u32[]{:S(2)}) collective-permute-start(bf16[1024,256]{1,0:T(8,128)(2,1)S(1)} %get-tuple-element.50), channel_id=1, source_target_pairs={{0,96},{8,104},{16,112},{24,120},{32,0},{40,8},{48,16},{56,24},{64... | collective-permute-start | bytes 1572872 | tf_op jit(solution)/shard_map/ppermute | solution.py:246
  85.8 29.7 %collective-permute-start.9 = (bf16[2048,256]{1,0:T(8,128)(2,1)}, bf16[2048,256]{1,0:T(8,128)(2,1)}, u32[]{:S(2)}, u32[]{:S(2)}) collective-permute-start(bf16[2048,256]{1,0:T(8,128)(2,1)} %pad_maximum_fusion.3), channel_id=1, source_target_pairs={{0,24},{8,0},{16,8},{24,16},{32,56},{40,32},{48,40},{56,48},{64,88... | collective-permute-start | bytes 3145736 | tf_op jit(solution)/shard_map/ppermute | solution.py:249
  87.3 28.3 %collective-permute-start.8 = (bf16[2048,256]{1,0:T(8,128)(2,1)}, bf16[2048,256]{1,0:T(8,128)(2,1)}, u32[]{:S(2)}, u32[]{:S(2)}) collective-permute-start(bf16[2048,256]{1,0:T(8,128)(2,1)} %pad_maximum_fusion.2), channel_id=1, source_target_pairs={{0,8},{8,16},{16,24},{24,0},{32,40},{40,48},{48,56},{56,32},{64,72... | collective-permute-start | bytes 3145736 | tf_op jit(solution)/shard_map/ppermute | solution.py:249
  90.3 25.3 %collective-permute-start.7 = (bf16[2048,256]{1,0:T(8,128)(2,1)}, bf16[2048,256]{1,0:T(8,128)(2,1)}, u32[]{:S(2)}, u32[]{:S(2)}) collective-permute-start(bf16[2048,256]{1,0:T(8,128)(2,1)} %pad_maximum_fusion.1), channel_id=1, source_target_pairs={{0,96},{8,104},{16,112},{24,120},{32,0},{40,8},{48,16},{56,24},{64... | collective-permute-start | bytes 3145736 | tf_op jit(solution)/shard_map/ppermute | solution.py:246
  94.5 24.1 %collective-permute-start.6 = (bf16[2048,256]{1,0:T(8,128)(2,1)}, bf16[2048,256]{1,0:T(8,128)(2,1)}, u32[]{:S(2)}, u32[]{:S(2)}) collective-permute-start(bf16[2048,256]{1,0:T(8,128)(2,1)} %pad_maximum_fusion), channel_id=1, source_target_pairs={{0,32},{8,40},{16,48},{24,56},{32,64},{40,72},{48,80},{56,88},{64,... | collective-permute-start | bytes 3145736 | tf_op jit(solution)/shard_map/ppermute | solution.py:246
  108.5 42.6 %all-to-all-start.1 = ((bf16[16,32,2176]{2,1,0:T(8,128)(2,1)}), bf16[16,32,2176]{2,1,0:T(8,128)(2,1)S(1)}, u32[]{:S(2)}, u32[]{:S(2)}) async-start(bf16[16,32,2176]{2,1,0:T(8,128)(2,1)} %answer.1), calls=%async_computation.1 | async-start | bytes 4456448 | tf_op jit(solution)/shard_map/all_to_all | solution.py:329
  123.7 23.1 %collective-permute-start.12 = (bf16[2,512,256]{2,1,0:T(8,128)(2,1)}, bf16[2,512,256]{2,1,0:T(8,128)(2,1)}, u32[]{:S(2)}, u32[]{:S(2)}) collective-permute-start(bf16[2,512,256]{2,1,0:T(8,128)(2,1)} %pad_maximum_fusion.7), channel_id=1, source_target_pairs={{0,6},{1,7},{2,0},{3,1},{4,2},{5,3},{6,4},{7,5},{8,14},{9,15},{10,... | collective-permute-start | bytes 1572872 | tf_op jit(solution)/shard_map/ppermute | solution.py:243
  129.2 21.8 %collective-permute-start.11 = (bf16[2,512,256]{2,1,0:T(8,128)(2,1)}, bf16[2,512,256]{2,1,0:T(8,128)(2,1)}, u32[]{:S(2)}, u32[]{:S(2)}) collective-permute-start(bf16[2,512,256]{2,1,0:T(8,128)(2,1)} %pad_maximum_fusion.6), channel_id=1, source_target_pairs={{0,2},{1,3},{2,4},{3,5},{4,6},{5,7},{6,0},{7,1},{8,10},{9,11},{10,... | collective-permute-start | bytes 1572872 | tf_op jit(solution)/shard_map/ppermute | solution.py:243
  130.1 21.0 %collective-permute-start.10 = (bf16[2,512,256]{2,1,0:T(8,128)(2,1)}, bf16[2,512,256]{2,1,0:T(8,128)(2,1)}, u32[]{:S(2)}, u32[]{:S(2)}) collective-permute-start(bf16[2,512,256]{2,1,0:T(8,128)(2,1)} %pad_maximum_fusion.5), channel_id=1, source_target_pairs={{0,4},{1,5},{2,6},{3,7},{4,0},{5,1},{6,2},{7,3},{8,12},{9,13},{10,... | collective-permute-start | bytes 1572872 | tf_op jit(solution)/shard_map/ppermute | solution.py:243
  154.3 10.8 %collective-permute-start.20 = (bf16[2,256,256]{2,1,0:T(8,128)(2,1)S(1)}, bf16[2,256,256]{2,1,0:T(8,128)(2,1)S(1)}, u32[]{:S(2)}, u32[]{:S(2)}) collective-permute-start(bf16[2,256,256]{2,1,0:T(8,128)(2,1)S(1)} %pad_maximum_fusion.9), channel_id=1, source_target_pairs={{0,64},{8,72},{16,80},{24,88},{32,96},{40,104},{48,112},{56,120},{... | collective-permute-start | bytes 786440 | tf_op jit(solution)/shard_map/ppermute | solution.py:246
  155.7 14.2 %collective-permute-start.21 = (bf16[2,256,256]{2,1,0:T(8,128)(2,1)S(1)}, bf16[2,256,256]{2,1,0:T(8,128)(2,1)S(1)}, u32[]{:S(2)}, u32[]{:S(2)}) collective-permute-start(bf16[2,256,256]{2,1,0:T(8,128)(2,1)S(1)} %pad_maximum_fusion.9), channel_id=1, source_target_pairs={{0,32},{8,40},{16,48},{24,56},{32,64},{40,72},{48,80},{56,88},{64,... | collective-permute-start | bytes 786440 | tf_op jit(solution)/shard_map/ppermute | solution.py:246
  156.2 13.7 %collective-permute-start.22 = (bf16[2,256,256]{2,1,0:T(8,128)(2,1)S(1)}, bf16[2,256,256]{2,1,0:T(8,128)(2,1)S(1)}, u32[]{:S(2)}, u32[]{:S(2)}) collective-permute-start(bf16[2,256,256]{2,1,0:T(8,128)(2,1)S(1)} %pad_maximum_fusion.9), channel_id=1, source_target_pairs={{0,96},{8,104},{16,112},{24,120},{32,0},{40,8},{48,16},{56,24},{64... | collective-permute-start | bytes 786440 | tf_op jit(solution)/shard_map/ppermute | solution.py:246
  158.9 14.8 %collective-permute-start.14 = (bf16[2,256,256]{2,1,0:T(8,128)(2,1)S(1)}, bf16[2,256,256]{2,1,0:T(8,128)(2,1)S(1)}, u32[]{:S(2)}, u32[]{:S(2)}) collective-permute-start(bf16[2,256,256]{2,1,0:T(8,128)(2,1)S(1)} %pad_maximum_fusion.8), channel_id=1, source_target_pairs={{0,16},{8,24},{16,0},{24,8},{32,48},{40,56},{48,32},{56,40},{64,80... | collective-permute-start | bytes 786440 | tf_op jit(solution)/shard_map/ppermute | solution.py:249
  162.0 12.4 %collective-permute-start.15 = (bf16[2,256,256]{2,1,0:T(8,128)(2,1)S(1)}, bf16[2,256,256]{2,1,0:T(8,128)(2,1)S(1)}, u32[]{:S(2)}, u32[]{:S(2)}) collective-permute-start(bf16[2,256,256]{2,1,0:T(8,128)(2,1)S(1)} %pad_maximum_fusion.8), channel_id=1, source_target_pairs={{0,8},{8,16},{16,24},{24,0},{32,40},{40,48},{48,56},{56,32},{64,72... | collective-permute-start | bytes 786440 | tf_op jit(solution)/shard_map/ppermute | solution.py:249
  170.0 10.2 %collective-permute-start.23 = (bf16[2,256,256]{2,1,0:T(8,128)(2,1)S(1)}, bf16[2,256,256]{2,1,0:T(8,128)(2,1)S(1)}, u32[]{:S(2)}, u32[]{:S(2)}) collective-permute-start(bf16[2,256,256]{2,1,0:T(8,128)(2,1)S(1)} %add_convert_fusion.refs_5_), channel_id=1, source_target_pairs={{0,8},{8,16},{16,24},{24,0},{32,40},{40,48},{48,56},{56,32},{64,72... | collective-permute-start | bytes 786440 | tf_op jit(solution)/shard_map/ppermute | solution.py:249
  170.7 14.8 %collective-permute-start.24 = (bf16[2,256,256]{2,1,0:T(8,128)(2,1)S(1)}, bf16[2,256,256]{2,1,0:T(8,128)(2,1)S(1)}, u32[]{:S(2)}, u32[]{:S(2)}) collective-permute-start(bf16[2,256,256]{2,1,0:T(8,128)(2,1)S(1)} %add_convert_fusion.refs_5_), channel_id=1, source_target_pairs={{0,16},{8,24},{16,0},{24,8},{32,48},{40,56},{48,32},{56,40},{64,80... | collective-permute-start | bytes 786440 | tf_op jit(solution)/shard_map/ppermute | solution.py:249
  173.7 12.1 %collective-permute-start.25 = (bf16[2,256,256]{2,1,0:T(8,128)(2,1)S(1)}, bf16[2,256,256]{2,1,0:T(8,128)(2,1)S(1)}, u32[]{:S(2)}, u32[]{:S(2)}) collective-permute-start(bf16[2,256,256]{2,1,0:T(8,128)(2,1)S(1)} %add_convert_fusion.refs_5_), channel_id=1, source_target_pairs={{0,24},{8,0},{16,8},{24,16},{32,56},{40,32},{48,40},{56,48},{64,88... | collective-permute-start | bytes 786440 | tf_op jit(solution)/shard_map/ppermute | solution.py:249
  174.5 11.4 %collective-permute-start.17 = (bf16[2,256,256]{2,1,0:T(8,128)(2,1)S(1)}, bf16[2,256,256]{2,1,0:T(8,128)(2,1)}, u32[]{:S(2)}, u32[]{:S(2)}) collective-permute-start(bf16[2,256,256]{2,1,0:T(8,128)(2,1)S(1)} %add_convert_fusion.1.refs_1_), channel_id=1, source_target_pairs={{0,32},{8,40},{16,48},{24,56},{32,64},{40,72},{48,80},{56,88},{64,... | collective-permute-start | bytes 786440 | tf_op jit(solution)/shard_map/ppermute | solution.py:246
  175.8 13.7 %collective-permute-start.18 = (bf16[2,256,256]{2,1,0:T(8,128)(2,1)S(1)}, bf16[2,256,256]{2,1,0:T(8,128)(2,1)}, u32[]{:S(2)}, u32[]{:S(2)}) collective-permute-start(bf16[2,256,256]{2,1,0:T(8,128)(2,1)S(1)} %add_convert_fusion.1.refs_1_), channel_id=1, source_target_pairs={{0,64},{8,72},{16,80},{24,88},{32,96},{40,104},{48,112},{56,120},{... | collective-permute-start | bytes 786440 | tf_op jit(solution)/shard_map/ppermute | solution.py:246
  (11 other events, 69.0 us)
Sparse Core Ops, SparseCore 0:
  9.7 87.3 all-gather.1

commit v5 on v4

--- a/solution.py
+++ b/solution.py
@@ -53,13 +53,13 @@
         onehot_ref[...], extra, (((1,), (1,)), ((), ())), preferred_element_type=jnp.float32
     ).astype(jnp.bfloat16)
     hand_over(steps).start()
+    gate = picked[:, width : width + 1].astype(jnp.float32)
 
     for step in range(steps):
         fetch(step).wait()
         span = slice(step * columns, (step + 1) * columns)
-        picked[:, span] = jnp.dot(
-            onehot_ref[...], head[:, span], preferred_element_type=jnp.float32
-        ).astype(jnp.bfloat16)
+        rows_of_step = jnp.dot(onehot_ref[...], head[:, span], preferred_element_type=jnp.float32)
+        picked[:, span] = (gate * rows_of_step).astype(jnp.bfloat16)
         hand_over(step).start()
     for step in range(steps + 1):
         hand_over(step).wait()
@@ -139,7 +139,7 @@
     def _():
         gate = rows_ref[:, width : width + 1].astype(jnp.float32)
         inner = jnp.sum(rows_ref[:, :width].astype(jnp.float32) * total_ref[...], axis=1, keepdims=True)
-        logit_ref[...] = jnp.broadcast_to(gate * (1.0 - gate) * inner, logit_ref.shape)
+        logit_ref[...] = jnp.broadcast_to((1.0 - gate) * inner, logit_ref.shape)
         total_ref[...] *= gate
         block = back_ref.shape[1]
         for peer in range(back_ref.shape[0]):
@@ -174,9 +174,8 @@
 
 
 def project_body(width, rows_ref, weight_ref, update_ref):
-    gate = rows_ref[:, width : width + 1].astype(jnp.float32)
-    projected = jnp.dot(rows_ref[:, :width], weight_ref[...], preferred_element_type=jnp.float32)
-    update_ref[...] = (gate * projected).astype(jnp.bfloat16)
+    gated = jnp.dot(rows_ref[:, :width], weight_ref[...], preferred_element_type=jnp.float32)
+    update_ref[...] = gated.astype(jnp.bfloat16)
 
 
 def project(rows, weight):
@@ -198,34 +197,35 @@
     )(rows, weight)
 
 
-def place_body(side, spot_ref, *refs):
+def place_body(side, which, spot_ref, *refs):
     out_ref = refs[-1]
     columns = refs[0].shape[2]
-    for which in range(2):
-        for ahead in range(side):
-            left = (spot_ref[which] - ahead + side) % side * columns + which * side * columns
-            array = refs[which * side + ahead]
-            out_ref[:, pl.ds(pl.multiple_of(left, columns), columns)] = array[0].astype(jnp.float32)
-
-
-def place_blocks(spot, first, second):
-    side = len(first)
-    halves, rows, columns = first[0].shape
-    model = halves * 2 * side * columns
+    for ahead in range(side):
+        left = (spot_ref[which] - ahead + side) % side * columns
+        out_ref[:, pl.ds(pl.multiple_of(left, columns), columns)] = refs[ahead][0].astype(jnp.float32)
+
+
+def place_blocks(which, spot, pieces, whole=None):
+    side = len(pieces)
+    halves, rows, columns = pieces[0].shape
     block = pl.BlockSpec((1, rows, columns), lambda h, spot_ref: (h, 0, 0))
-    return pl.pallas_call(
-        lambda *refs: place_body(side, *refs),
-        out_shape=jax.ShapeDtypeStruct((rows, model), jnp.float32),
+    rest = () if whole is None else (whole,)
+    return pl.pallas_call(
+        lambda *refs: place_body(side, which, *refs),
+        out_shape=jax.ShapeDtypeStruct((rows, halves * 2 * side * columns), jnp.float32),
         grid_spec=pltpu.PrefetchScalarGridSpec(
             num_scalar_prefetch=1,
             grid=(halves,),
-            in_specs=[block] * (2 * side),
-            out_specs=pl.BlockSpec((rows, model // halves), lambda h, spot_ref: (0, (h + spot_ref[2]) % halves)),
+            in_specs=[block] * side + [pl.BlockSpec(memory_space=pl.ANY)] * len(rest),
+            out_specs=pl.BlockSpec(
+                (rows, side * columns), lambda h, spot_ref: (0, (h + spot_ref[2]) % halves * 2 + which)
+            ),
         ),
+        input_output_aliases={1 + side: 0} if rest else {},
         compiler_params=params(),
         cost_estimate=NO_COST,
         name="place_blocks",
-    )(spot, *first, *second)
+    )(spot, *pieces, *rest)
 
 
 def at(array, index, axis=0):
@@ -275,7 +275,8 @@
     send = send.reshape(n_dp, block, width + EXTRA)
     got = lax.all_to_all(send, "dp", split_axis=0, concat_axis=0, tiled=True)
 
-    got = after(got, partner_cot)
+    both_cot = jnp.concatenate([own_cot, partner_cot], axis=0)
+    got, both_cot = lax.optimization_barrier((got, both_cot))
     incoming = (got[:, 0, width + 1] > 0.5).astype(jnp.int32)
     position = jnp.cumsum(incoming) - 1
     ids = jnp.arange(receive, dtype=jnp.int32)
@@ -286,14 +287,11 @@
     held = move_blocks(got, source, width + EXTRA).reshape(rows, width + EXTRA)
 
     both = jnp.concatenate([held, to_partner(held)], axis=0)
-    both_cot = jnp.concatenate([own_cot, partner_cot], axis=0)
-    gate = both[:, width].astype(jnp.float32)
-    weighted = (gate[:, None] * both_cot.astype(jnp.float32)).astype(jnp.bfloat16)
     both_rows = both[:, :width]
     part = half // (2 * side)
 
     def term(first, index):
-        columns = lax.dynamic_slice(weighted, (0, first + index % side * part), (2 * rows, part))
+        columns = lax.dynamic_slice(both_cot, (0, first + index % side * part), (2 * rows, part))
         product = lax.dot_general(
             both_rows, columns, (((0,), (0,)), ((), ())), preferred_element_type=jnp.float32
         )
@@ -310,16 +308,16 @@
     got_parts = (
         along_y(far_y[:cut], 1), along_z(far_z[:cut], 1), along_y(far_y[cut:], -1), along_z(far_z[cut:], -1)
     )
-    ahead_y, ahead_z = term(0, y + 1), term(half // 2, z + 1)
-    behind_y, behind_z = term(0, y + side - 1), term(half // 2, z + side - 1)
+    ahead_y, ahead_z = narrow(term(0, y + 1)), narrow(term(half // 2, z + 1))
+    behind_y, behind_z = narrow(term(0, y + side - 1)), narrow(term(half // 2, z + side - 1))
     own_y, own_z = narrow(term(0, y)), narrow(term(half // 2, z))
     got_parts = after(got_parts, ahead_y, ahead_z, behind_y, behind_z, own_y, own_z)
     low_y, low_z, high_y, high_z = [wide(part_sum) for part_sum in got_parts]
     sent = (
-        narrow(jnp.concatenate([ahead_y[:cut] + low_y, ahead_y[cut:]], axis=0)),
-        narrow(jnp.concatenate([ahead_z[:cut] + low_z, ahead_z[cut:]], axis=0)),
-        narrow(jnp.concatenate([behind_y[:cut], behind_y[cut:] + high_y], axis=0)),
-        narrow(jnp.concatenate([behind_z[:cut], behind_z[cut:] + high_z], axis=0)),
+        narrow(jnp.concatenate([wide(ahead_y[:cut]) + low_y, wide(ahead_y[cut:])], axis=0)),
+        narrow(jnp.concatenate([wide(ahead_z[:cut]) + low_z, wide(ahead_z[cut:])], axis=0)),
+        narrow(jnp.concatenate([wide(behind_y[:cut]), wide(behind_y[cut:]) + high_y], axis=0)),
+        narrow(jnp.concatenate([wide(behind_z[:cut]), wide(behind_z[cut:]) + high_z], axis=0)),
     )
     from_y, from_z = along_y(sent[0], 1), along_z(sent[1], 1)
     to_y, to_z = along_y(sent[2], -1), along_z(sent[3], -1)
@@ -365,7 +363,8 @@
     sum_y = whole(jnp.stack([keep[0], take[0]]), along_z)
     sum_z = whole(jnp.stack([keep[1], take[1]]), along_y)
     spot = jnp.stack([y, z, core]).astype(jnp.int32)
-    grad_weight = place_blocks(spot, around(sum_y, along_y), around(sum_z, along_z))
+    grad_weight = place_blocks(0, spot, around(sum_y, along_y))
+    grad_weight = place_blocks(1, spot, around(sum_z, along_z), grad_weight)
 
     grad_context = move_blocks(returned, owner, width).reshape(slots, width)
     logit_blocks = returned[:, :, width]

time: 201 us -> 200 us (level)
  waiting for transfers between devices: 66.8 us -> 60 us
  starting transfers between devices: 51.6 us -> 54.9 us
  matrix products: 7.15 us -> 9.6 us
    ppermute x10, waiting for transfers between devices: 15.6 us -> 7.16 us  [along_y(): lax.ppermute(value, 'dp', [(d, (d + side * ahead) % n_dp) for d in range(...]
    ppermute x10, starting transfers between devices: 15 us -> 18.4 us  [along_y(): lax.ppermute(value, 'dp', [(d, (d + side * ahead) % n_dp) for d in range(...]
    dot_general x8, matrix products: 7.15 us -> 9.6 us  [term(): lax.dot_general(both_rows, columns, (((0,), (0,)), ((), ())), preferred_e...]
    all_gather x1, waiting for transfers between devices: 2.09 us -> 4.15 us  [on_device(): weight = lax.all_gather(out_weight, 'fsdp', axis=0, tiled=True)]
    pallas_call x1 -> x2, Pallas kernels: 3.74 us -> 4.88 us  [place_blocks(): pl.pallas_call(lambda *refs: place_body(side, which, *refs), out_shape=ja...]
  transfers between devices with their start and end apart: 29 -> 29, of which waited for: 17 -> 17; matrix products, arithmetic and copies ran while one was open for 14% -> 14% of each run, Pallas kernels for 16% -> 18%
where the time goes in v5:
time: 200 us; the launch traced here: 198 us
  waiting for transfers between devices  60 us (30%)
  starting transfers between devices  54.9 us (27%)
  Pallas kernels  37.7 us (19%)
  other arithmetic  16.5 us (8%)
  between operations  14.7 us (7%)
  matrix products  9.6 us (5%)
  local copies, waits for them, and re-layouts  4.81 us (2%)
    all_to_all x1, waiting for transfers between devices, on_device(): got = lax.all_to_all(send, 'dp', split_axis=0, concat_axis=0, tiled=True)  25.6 us
    ppermute x10, starting transfers between devices, along_y(): lax.ppermute(value, 'dp', [(d, (d + side * ahead) % n_dp) for d in range(...  18.4 us
    ppermute x10, starting transfers between devices, along_z(): lax.ppermute(value, 'dp', [(d, d // side * side + (d + ahead) % side) for...  16.1 us
    pallas_call x1, Pallas kernels, answer(): pl.pallas_call(lambda *refs: answer_body(width, *refs), out_shape=jax.Sha...  11.4 us
    ppermute x3, waiting for transfers between devices, along_x(): lax.ppermute(value, 'fsdp', [(f, (f + 2 * ahead) % n_fsdp) for f in range...  10.8 us
    pallas_call x1, Pallas kernels, project(): pl.pallas_call(lambda *refs: project_body(width, *refs), out_shape=jax.Sh...  9.91 us
    dot_general x8, matrix products, term(): lax.dot_general(both_rows, columns, (((0,), (0,)), ((), ())), preferred_e...  9.6 us
    pallas_call x1, Pallas kernels, pick_rows(): pl.pallas_call(pick_body, out_shape=jax.ShapeDtypeStruct((rows, width + E...  8.62 us
  transfers between devices with their start and end apart: 29, of which 17 were waited for; matrix products, arithmetic and copies ran while one was open for 14% of the time, Pallas kernels for 18%

profile of v5, /device:TPU:0, one launch (start us, length us, event | category | flops | bytes accessed | tf_op | source)
XLA Modules:
  0.0 198.2 jit_solution(9784626142612087040)
XLA Ops:
  8.8 8.6 %pick_rows.1 = bf16[512,2176]{1,0:T(8,128)(2,1)} custom-call(s32[16]{0:T(128)} %bitcast.47, s32[512,1]{1,0:T(8,128)} %copy.14.listed_ref, f32[1,2048]{1,0:T(1,128)} %bitcast.54, bf16[2048,2048]{1,0:T(8,128)(2,1)} %head_ref.1), custom_call_target="tpu_custom_call" | custom-call | tf_op jit(solution)/shard_map/pick_rows/pallas_call | solution.py:73
  17.4 8.1 %all-to-all-start = ((bf16[16,32,2176]{2,1,0:T(8,128)(2,1)}), bf16[16,32,2176]{2,1,0:T(8,128)(2,1)S(1)}, u32[]{:S(2)}, u32[]{:S(2)}) async-start(bf16[16,32,2176]{2,1,0:T(8,128)(2,1)} %bitcast.50), calls=%async_computation | async-start | bytes 4456448 | tf_op jit(solution)/shard_map/all_to_all | solution.py:276
  27.8 2.6 %collective-permute-done = bf16[256,2048]{1,0:T(8,128)(2,1)S(1)} collective-permute-done((bf16[256,2048]{1,0:T(8,128)(2,1)S(1)}, bf16[256,2048]{1,0:T(8,128)(2,1)S(1)}, u32[]{:S(2)}, u32[]{:S(2)}) %collective-permute-start) | collective-permute-done | bytes 1048608 | tf_op jit(solution)/shard_map/ppermute | solution.py:254
  32.0 25.6 %all-to-all-done.refs_1_ = bf16[16,32,2176]{2,1,0:T(8,128)(2,1)S(1)} async-done(((bf16[16,32,2176]{2,1,0:T(8,128)(2,1)}), bf16[16,32,2176]{2,1,0:T(8,128)(2,1)S(1)}, u32[]{:S(2)}, u32[]{:S(2)}) %all-to-all-start) | async-done | bytes 2228256 | tf_op jit(solution)/shard_map/all_to_all | solution.py:276
  59.3 2.5 %collective-permute-done.1 = bf16[256,2176]{1,0:T(8,128)(2,1)S(1)} collective-permute-done((bf16[256,2176]{1,0:T(8,128)(2,1)S(1)}, bf16[256,2176]{1,0:T(8,128)(2,1)S(1)}, u32[]{:S(2)}, u32[]{:S(2)}) %collective-permute-start.1) | collective-permute-done | bytes 1114144 | tf_op jit(solution)/shard_map/ppermute | solution.py:254
  64.5 2.7 %collective-permute-start.5 = (bf16[1024,256]{1,0:T(8,128)(2,1)S(1)}, bf16[1024,256]{1,0:T(8,128)(2,1)S(1)}, u32[]{:S(2)}, u32[]{:S(2)}) collective-permute-start(bf16[1024,256]{1,0:T(8,128)(2,1)S(1)} %get-tuple-element.50), channel_id=1, source_target_pairs={{0,24},{8,0},{16,8},{24,16},{32,56},{40,32},{48,40},{56,48},{64,88... | collective-permute-start | bytes 1572872 | tf_op jit(solution)/shard_map/ppermute | solution.py:249
  68.1 3.2 %collective-permute-start.4 = (bf16[1024,256]{1,0:T(8,128)(2,1)S(1)}, bf16[1024,256]{1,0:T(8,128)(2,1)S(1)}, u32[]{:S(2)}, u32[]{:S(2)}) collective-permute-start(bf16[1024,256]{1,0:T(8,128)(2,1)S(1)} %get-tuple-element.52), channel_id=1, source_target_pairs={{0,96},{8,104},{16,112},{24,120},{32,0},{40,8},{48,16},{56,24},{64... | collective-permute-start | bytes 1572872 | tf_op jit(solution)/shard_map/ppermute | solution.py:246
  79.1 3.6 %collective-permute-done.2 = bf16[1024,256]{1,0:T(8,128)(2,1)S(1)} collective-permute-done((bf16[1024,256]{1,0:T(8,128)(2,1)S(1)}, bf16[1024,256]{1,0:T(8,128)(2,1)S(1)}, u32[]{:S(2)}, u32[]{:S(2)}) %collective-permute-start.2) | collective-permute-done | bytes 524320 | tf_op jit(solution)/shard_map/ppermute | solution.py:246
  88.2 3.0 %collective-permute-start.7 = (bf16[2048,256]{1,0:T(8,128)(2,1)}, bf16[2048,256]{1,0:T(8,128)(2,1)}, u32[]{:S(2)}, u32[]{:S(2)}) collective-permute-start(bf16[2048,256]{1,0:T(8,128)(2,1)} %pad_maximum_fusion.3), channel_id=1, source_target_pairs={{0,96},{8,104},{16,112},{24,120},{32,0},{40,8},{48,16},{56,24},{64... | collective-permute-start | bytes 3145736 | tf_op jit(solution)/shard_map/ppermute | solution.py:246
  93.0 4.2 %all-gather.2.cloned.1.call-done.refs_2_.refs_1_ = bf16[2048,4096]{1,0:T(8,128)(2,1)} async-done(((bf16[256,4096]{1,0:T(8,128)(2,1)}), bf16[2048,4096]{1,0:T(8,128)(2,1)}) %all-gather.2.cloned.1.call-update) | async-done | bytes 16777232 | tf_op jit(solution)/shard_map/all_gather | solution.py:267
  97.1 11.4 %answer.1 = bf16[16,32,2176]{2,1,0:T(8,128)(2,1)} custom-call(s32[16]{0:T(128)} %broadcast_clamp_fusion.refs_0_, bf16[256,2176]{1,0:T(8,128)(2,1)} %bitcast.45, bf16[2048,4096]{1,0:T(8,128)(2,1)} %all-gather.2.cloned.1.call-done.refs_2_.refs_1_, bf16[256,4096]{1,0:T(8,128)(2,1)} %refs_3_.1), custom_call_target="tpu_custom_call" | custom-call | tf_op jit(solution)/shard_map/answer/pallas_call | solution.py:155
  108.5 7.0 %all-to-all-start.1 = ((bf16[16,32,2176]{2,1,0:T(8,128)(2,1)}), bf16[16,32,2176]{2,1,0:T(8,128)(2,1)S(1)}, u32[]{:S(2)}, u32[]{:S(2)}) async-start(bf16[16,32,2176]{2,1,0:T(8,128)(2,1)} %answer.1), calls=%async_computation.1 | async-start | bytes 4456448 | tf_op jit(solution)/shard_map/all_to_all | solution.py:327
  116.7 4.2 %add_bitcast_fusion = (f32[1,512,256]{2,1,0:T(8,128)}, bf16[1,512,256]{2,1,0:T(8,128)(2,1)S(1)}, bf16[1,512,256]{2,1,0:T(8,128)(2,1)S(1)}, bf16[1,512,256]{2,1,0...) fusion(bf16[2048,256]{1,0:T(8,128)(2,1)} %collective-permute-do, ...), kind=kLoop, calls=%fused_computation.34 | loop fusion | flops 6029312 | bytes 8912912 | tf_op jit(solution)/shard_map/stack | solution.py:336
  121.7 3.5 %collective-permute-start.12 = (bf16[2,512,256]{2,1,0:T(8,128)(2,1)}, bf16[2,512,256]{2,1,0:T(8,128)(2,1)}, u32[]{:S(2)}, u32[]{:S(2)}) collective-permute-start(bf16[2,512,256]{2,1,0:T(8,128)(2,1)} %pad_maximum_fusion.9), channel_id=1, source_target_pairs={{0,6},{1,7},{2,0},{3,1},{4,2},{5,3},{6,4},{7,5},{8,14},{9,15},{10,... | collective-permute-start | bytes 1572872 | tf_op jit(solution)/shard_map/ppermute | solution.py:243
  128.4 9.9 %project.1 = bf16[256,4096]{1,0:T(8,128)(2,1)} custom-call(bf16[256,2176]{1,0:T(8,128)(2,1)} %bitcast.46, bf16[2048,4096]{1,0:T(8,128)(2,1)} %all-gather.2.cloned.1.call-done.refs_2_.refs_1_), custom_call_target="tpu_custom_call" | custom-call | tf_op jit(solution)/shard_map/project/pallas_call | solution.py:185
  138.4 10.8 %collective-permute-done.11 = bf16[2,512,256]{2,1,0:T(8,128)(2,1)} collective-permute-done((bf16[2,512,256]{2,1,0:T(8,128)(2,1)}, bf16[2,512,256]{2,1,0:T(8,128)(2,1)}, u32[]{:S(2)}, u32[]{:S(2)}) %collective-permute-start.11) | collective-permute-done | bytes 524320 | tf_op jit(solution)/shard_map/ppermute | solution.py:243
  152.5 3.1 %collective-permute-start.20 = (bf16[2,256,256]{2,1,0:T(8,128)(2,1)S(1)}, bf16[2,256,256]{2,1,0:T(8,128)(2,1)S(1)}, u32[]{:S(2)}, u32[]{:S(2)}) collective-permute-start(bf16[2,256,256]{2,1,0:T(8,128)(2,1)S(1)} %pad_maximum_fusion.11), channel_id=1, source_target_pairs={{0,16},{8,24},{16,0},{24,8},{32,48},{40,56},{48,32},{56,40},{64,80... | collective-permute-start | bytes 786440 | tf_op jit(solution)/shard_map/ppermute | solution.py:249
  156.2 2.7 %collective-permute-start.22 = (bf16[2,256,256]{2,1,0:T(8,128)(2,1)S(1)}, bf16[2,256,256]{2,1,0:T(8,128)(2,1)S(1)}, u32[]{:S(2)}, u32[]{:S(2)}) collective-permute-start(bf16[2,256,256]{2,1,0:T(8,128)(2,1)S(1)} %pad_maximum_fusion.11), channel_id=1, source_target_pairs={{0,24},{8,0},{16,8},{24,16},{32,56},{40,32},{48,40},{56,48},{64,88... | collective-permute-start | bytes 786440 | tf_op jit(solution)/shard_map/ppermute | solution.py:249
  158.9 3.1 %collective-permute-start.14 = (bf16[2,256,256]{2,1,0:T(8,128)(2,1)S(1)}, bf16[2,256,256]{2,1,0:T(8,128)(2,1)S(1)}, u32[]{:S(2)}, u32[]{:S(2)}) collective-permute-start(bf16[2,256,256]{2,1,0:T(8,128)(2,1)S(1)} %pad_maximum_fusion.10), channel_id=1, source_target_pairs={{0,64},{8,72},{16,80},{24,88},{32,96},{40,104},{48,112},{56,120},{... | collective-permute-start | bytes 786440 | tf_op jit(solution)/shard_map/ppermute | solution.py:246
  163.3 2.8 %collective-permute-start.16 = (bf16[2,256,256]{2,1,0:T(8,128)(2,1)S(1)}, bf16[2,256,256]{2,1,0:T(8,128)(2,1)S(1)}, u32[]{:S(2)}, u32[]{:S(2)}) collective-permute-start(bf16[2,256,256]{2,1,0:T(8,128)(2,1)S(1)} %pad_maximum_fusion.10), channel_id=1, source_target_pairs={{0,96},{8,104},{16,112},{24,120},{32,0},{40,8},{48,16},{56,24},{64... | collective-permute-start | bytes 786440 | tf_op jit(solution)/shard_map/ppermute | solution.py:246
  169.8 2.8 %collective-permute-start.24 = (bf16[2,256,256]{2,1,0:T(8,128)(2,1)S(1)}, bf16[2,256,256]{2,1,0:T(8,128)(2,1)}, u32[]{:S(2)}, u32[]{:S(2)}) collective-permute-start(bf16[2,256,256]{2,1,0:T(8,128)(2,1)S(1)} %add_convert_fusion.4.refs_1_), channel_id=1, source_target_pairs={{0,64},{8,72},{16,80},{24,88},{32,96},{40,104},{48,112},{56,120},{... | collective-permute-start | bytes 786440 | tf_op jit(solution)/shard_map/ppermute | solution.py:246
  175.8 2.6 %collective-permute-start.18 = (bf16[2,256,256]{2,1,0:T(8,128)(2,1)S(1)}, bf16[2,256,256]{2,1,0:T(8,128)(2,1)S(1)}, u32[]{:S(2)}, u32[]{:S(2)}) collective-permute-start(bf16[2,256,256]{2,1,0:T(8,128)(2,1)S(1)} %add_convert_fusion.5.refs_1_), channel_id=1, source_target_pairs={{0,16},{8,24},{16,0},{24,8},{32,48},{40,56},{48,32},{56,40},{64,80... | collective-permute-start | bytes 786440 | tf_op jit(solution)/shard_map/ppermute | solution.py:249
  182.2 2.2 %move_blocks.3 = bf16[16,32,2048]{2,1,0:T(8,128)(2,1)} custom-call(s32[16]{0:T(128)S(1)} %bitcast.49, bf16[16,32,2176]{2,1,0:T(8,128)(2,1)S(1)} %all-to-all-done.1.refs_1_), custom_call_target="tpu_custom_call" | custom-call | tf_op jit(solution)/shard_map/move_blocks/pallas_call | solution.py:113
  185.0 2.9 %place_blocks.2.refs_5_ = f32[256,4096]{1,0:T(8,128)} custom-call(s32[3]{0:T(128)S(1)} %pad_add_fusion.refs_0_, bf16[2,256,256]{2,1,0:T(8,128)(2,1)S(1)} %add_convert_fusion.4.refs_1_, bf16[2,256,256]{2,1,0:T(8,128)(2,1)S(1)} %copy-done.2, bf16[2,256,256]{2,1,0:T(8,128)(2,1)} %collective-permute-done.24.refs_3_, ...), custom_call_target="tpu_custom_call" | custom-call | tf_op jit(solution)/shard_map/place_blocks/pallas_call | solution.py:213
  (109 shorter events, 50.5 us)
Async XLA Ops:
  7.2 90.0 %all-gather.2.cloned.1.call-start = ((), (), s32[]{:S(2)}) async-start(), calls=%async_computation.2 | async-start | bytes 18874368 | tf_op jit(solution)/shard_map/all_gather | solution.py:267
  17.4 40.2 %all-to-all-start = ((bf16[16,32,2176]{2,1,0:T(8,128)(2,1)}), bf16[16,32,2176]{2,1,0:T(8,128)(2,1)S(1)}, u32[]{:S(2)}, u32[]{:S(2)}) async-start(bf16[16,32,2176]{2,1,0:T(8,128)(2,1)} %bitcast.50), calls=%async_computation | async-start | bytes 4456448 | tf_op jit(solution)/shard_map/all_to_all | solution.py:276
  63.9 15.2 %collective-permute-start.3 = (bf16[1024,256]{1,0:T(8,128)(2,1)S(1)}, bf16[1024,256]{1,0:T(8,128)(2,1)S(1)}, u32[]{:S(2)}, u32[]{:S(2)}) collective-permute-start(bf16[1024,256]{1,0:T(8,128)(2,1)S(1)} %get-tuple-element.51), channel_id=1, source_target_pairs={{0,8},{8,16},{16,24},{24,0},{32,40},{40,48},{48,56},{56,32},{64,72... | collective-permute-start | bytes 1572872 | tf_op jit(solution)/shard_map/ppermute | solution.py:249
  64.5 14.6 %collective-permute-start.5 = (bf16[1024,256]{1,0:T(8,128)(2,1)S(1)}, bf16[1024,256]{1,0:T(8,128)(2,1)S(1)}, u32[]{:S(2)}, u32[]{:S(2)}) collective-permute-start(bf16[1024,256]{1,0:T(8,128)(2,1)S(1)} %get-tuple-element.50), channel_id=1, source_target_pairs={{0,24},{8,0},{16,8},{24,16},{32,56},{40,32},{48,40},{56,48},{64,88... | collective-permute-start | bytes 1572872 | tf_op jit(solution)/shard_map/ppermute | solution.py:249
  68.0 14.6 %collective-permute-start.2 = (bf16[1024,256]{1,0:T(8,128)(2,1)S(1)}, bf16[1024,256]{1,0:T(8,128)(2,1)S(1)}, u32[]{:S(2)}, u32[]{:S(2)}) collective-permute-start(bf16[1024,256]{1,0:T(8,128)(2,1)S(1)} %get-tuple-element.53), channel_id=1, source_target_pairs={{0,32},{8,40},{16,48},{24,56},{32,64},{40,72},{48,80},{56,88},{64,... | collective-permute-start | bytes 1572872 | tf_op jit(solution)/shard_map/ppermute | solution.py:246
  68.1 14.6 %collective-permute-start.4 = (bf16[1024,256]{1,0:T(8,128)(2,1)S(1)}, bf16[1024,256]{1,0:T(8,128)(2,1)S(1)}, u32[]{:S(2)}, u32[]{:S(2)}) collective-permute-start(bf16[1024,256]{1,0:T(8,128)(2,1)S(1)} %get-tuple-element.52), channel_id=1, source_target_pairs={{0,96},{8,104},{16,112},{24,120},{32,0},{40,8},{48,16},{56,24},{64... | collective-permute-start | bytes 1572872 | tf_op jit(solution)/shard_map/ppermute | solution.py:246
  83.9 31.7 %collective-permute-start.9 = (bf16[2048,256]{1,0:T(8,128)(2,1)}, bf16[2048,256]{1,0:T(8,128)(2,1)}, u32[]{:S(2)}, u32[]{:S(2)}) collective-permute-start(bf16[2048,256]{1,0:T(8,128)(2,1)} %pad_maximum_fusion.5), channel_id=1, source_target_pairs={{0,24},{8,0},{16,8},{24,16},{32,56},{40,32},{48,40},{56,48},{64,88... | collective-permute-start | bytes 3145736 | tf_op jit(solution)/shard_map/ppermute | solution.py:249
  85.3 30.3 %collective-permute-start.8 = (bf16[2048,256]{1,0:T(8,128)(2,1)}, bf16[2048,256]{1,0:T(8,128)(2,1)}, u32[]{:S(2)}, u32[]{:S(2)}) collective-permute-start(bf16[2048,256]{1,0:T(8,128)(2,1)} %pad_maximum_fusion.4), channel_id=1, source_target_pairs={{0,8},{8,16},{16,24},{24,0},{32,40},{40,48},{48,56},{56,32},{64,72... | collective-permute-start | bytes 3145736 | tf_op jit(solution)/shard_map/ppermute | solution.py:249
  88.2 27.4 %collective-permute-start.7 = (bf16[2048,256]{1,0:T(8,128)(2,1)}, bf16[2048,256]{1,0:T(8,128)(2,1)}, u32[]{:S(2)}, u32[]{:S(2)}) collective-permute-start(bf16[2048,256]{1,0:T(8,128)(2,1)} %pad_maximum_fusion.3), channel_id=1, source_target_pairs={{0,96},{8,104},{16,112},{24,120},{32,0},{40,8},{48,16},{56,24},{64... | collective-permute-start | bytes 3145736 | tf_op jit(solution)/shard_map/ppermute | solution.py:246
  92.5 24.2 %collective-permute-start.6 = (bf16[2048,256]{1,0:T(8,128)(2,1)}, bf16[2048,256]{1,0:T(8,128)(2,1)}, u32[]{:S(2)}, u32[]{:S(2)}) collective-permute-start(bf16[2048,256]{1,0:T(8,128)(2,1)} %pad_maximum_fusion.2), channel_id=1, source_target_pairs={{0,32},{8,40},{16,48},{24,56},{32,64},{40,72},{48,80},{56,88},{64,... | collective-permute-start | bytes 3145736 | tf_op jit(solution)/shard_map/ppermute | solution.py:246
  108.5 40.7 %all-to-all-start.1 = ((bf16[16,32,2176]{2,1,0:T(8,128)(2,1)}), bf16[16,32,2176]{2,1,0:T(8,128)(2,1)S(1)}, u32[]{:S(2)}, u32[]{:S(2)}) async-start(bf16[16,32,2176]{2,1,0:T(8,128)(2,1)} %answer.1), calls=%async_computation.1 | async-start | bytes 4456448 | tf_op jit(solution)/shard_map/all_to_all | solution.py:327
  121.7 16.7 %collective-permute-start.12 = (bf16[2,512,256]{2,1,0:T(8,128)(2,1)}, bf16[2,512,256]{2,1,0:T(8,128)(2,1)}, u32[]{:S(2)}, u32[]{:S(2)}) collective-permute-start(bf16[2,512,256]{2,1,0:T(8,128)(2,1)} %pad_maximum_fusion.9), channel_id=1, source_target_pairs={{0,6},{1,7},{2,0},{3,1},{4,2},{5,3},{6,4},{7,5},{8,14},{9,15},{10,... | collective-permute-start | bytes 1572872 | tf_op jit(solution)/shard_map/ppermute | solution.py:243
  126.0 23.2 %collective-permute-start.11 = (bf16[2,512,256]{2,1,0:T(8,128)(2,1)}, bf16[2,512,256]{2,1,0:T(8,128)(2,1)}, u32[]{:S(2)}, u32[]{:S(2)}) collective-permute-start(bf16[2,512,256]{2,1,0:T(8,128)(2,1)} %pad_maximum_fusion.8), channel_id=1, source_target_pairs={{0,2},{1,3},{2,4},{3,5},{4,6},{5,7},{6,0},{7,1},{8,10},{9,11},{10,... | collective-permute-start | bytes 1572872 | tf_op jit(solution)/shard_map/ppermute | solution.py:243
  126.9 22.3 %collective-permute-start.10 = (bf16[2,512,256]{2,1,0:T(8,128)(2,1)}, bf16[2,512,256]{2,1,0:T(8,128)(2,1)}, u32[]{:S(2)}, u32[]{:S(2)}) collective-permute-start(bf16[2,512,256]{2,1,0:T(8,128)(2,1)} %pad_maximum_fusion.7), channel_id=1, source_target_pairs={{0,4},{1,5},{2,6},{3,7},{4,0},{5,1},{6,2},{7,3},{8,12},{9,13},{10,... | collective-permute-start | bytes 1572872 | tf_op jit(solution)/shard_map/ppermute | solution.py:243
  155.6 12.4 %collective-permute-start.21 = (bf16[2,256,256]{2,1,0:T(8,128)(2,1)S(1)}, bf16[2,256,256]{2,1,0:T(8,128)(2,1)S(1)}, u32[]{:S(2)}, u32[]{:S(2)}) collective-permute-start(bf16[2,256,256]{2,1,0:T(8,128)(2,1)S(1)} %pad_maximum_fusion.11), channel_id=1, source_target_pairs={{0,8},{8,16},{16,24},{24,0},{32,40},{40,48},{48,56},{56,32},{64,72... | collective-permute-start | bytes 786440 | tf_op jit(solution)/shard_map/ppermute | solution.py:249
  156.2 12.0 %collective-permute-start.22 = (bf16[2,256,256]{2,1,0:T(8,128)(2,1)S(1)}, bf16[2,256,256]{2,1,0:T(8,128)(2,1)S(1)}, u32[]{:S(2)}, u32[]{:S(2)}) collective-permute-start(bf16[2,256,256]{2,1,0:T(8,128)(2,1)S(1)} %pad_maximum_fusion.11), channel_id=1, source_target_pairs={{0,24},{8,0},{16,8},{24,16},{32,56},{40,32},{48,40},{56,48},{64,88... | collective-permute-start | bytes 786440 | tf_op jit(solution)/shard_map/ppermute | solution.py:249
  158.9 13.7 %collective-permute-start.14 = (bf16[2,256,256]{2,1,0:T(8,128)(2,1)S(1)}, bf16[2,256,256]{2,1,0:T(8,128)(2,1)S(1)}, u32[]{:S(2)}, u32[]{:S(2)}) collective-permute-start(bf16[2,256,256]{2,1,0:T(8,128)(2,1)S(1)} %pad_maximum_fusion.10), channel_id=1, source_target_pairs={{0,64},{8,72},{16,80},{24,88},{32,96},{40,104},{48,112},{56,120},{... | collective-permute-start | bytes 786440 | tf_op jit(solution)/shard_map/ppermute | solution.py:246
  161.9 12.4 %collective-permute-start.15 = (bf16[2,256,256]{2,1,0:T(8,128)(2,1)S(1)}, bf16[2,256,256]{2,1,0:T(8,128)(2,1)S(1)}, u32[]{:S(2)}, u32[]{:S(2)}) collective-permute-start(bf16[2,256,256]{2,1,0:T(8,128)(2,1)S(1)} %pad_maximum_fusion.10), channel_id=1, source_target_pairs={{0,32},{8,40},{16,48},{24,56},{32,64},{40,72},{48,80},{56,88},{64,... | collective-permute-start | bytes 786440 | tf_op jit(solution)/shard_map/ppermute | solution.py:246
  163.3 11.1 %collective-permute-start.16 = (bf16[2,256,256]{2,1,0:T(8,128)(2,1)S(1)}, bf16[2,256,256]{2,1,0:T(8,128)(2,1)S(1)}, u32[]{:S(2)}, u32[]{:S(2)}) collective-permute-start(bf16[2,256,256]{2,1,0:T(8,128)(2,1)S(1)} %pad_maximum_fusion.10), channel_id=1, source_target_pairs={{0,96},{8,104},{16,112},{24,120},{32,0},{40,8},{48,16},{56,24},{64... | collective-permute-start | bytes 786440 | tf_op jit(solution)/shard_map/ppermute | solution.py:246
  168.3 11.6 %collective-permute-start.23 = (bf16[2,256,256]{2,1,0:T(8,128)(2,1)S(1)}, bf16[2,256,256]{2,1,0:T(8,128)(2,1)S(1)}, u32[]{:S(2)}, u32[]{:S(2)}) collective-permute-start(bf16[2,256,256]{2,1,0:T(8,128)(2,1)S(1)} %add_convert_fusion.4.refs_1_), channel_id=1, source_target_pairs={{0,32},{8,40},{16,48},{24,56},{32,64},{40,72},{48,80},{56,88},{64,... | collective-permute-start | bytes 786440 | tf_op jit(solution)/shard_map/ppermute | solution.py:246
  169.8 15.1 %collective-permute-start.24 = (bf16[2,256,256]{2,1,0:T(8,128)(2,1)S(1)}, bf16[2,256,256]{2,1,0:T(8,128)(2,1)}, u32[]{:S(2)}, u32[]{:S(2)}) collective-permute-start(bf16[2,256,256]{2,1,0:T(8,128)(2,1)S(1)} %add_convert_fusion.4.refs_1_), channel_id=1, source_target_pairs={{0,64},{8,72},{16,80},{24,88},{32,96},{40,104},{48,112},{56,120},{... | collective-permute-start | bytes 786440 | tf_op jit(solution)/shard_map/ppermute | solution.py:246
  172.6 12.4 %collective-permute-start.25 = (bf16[2,256,256]{2,1,0:T(8,128)(2,1)S(1)}, bf16[2,256,256]{2,1,0:T(8,128)(2,1)}, u32[]{:S(2)}, u32[]{:S(2)}) collective-permute-start(bf16[2,256,256]{2,1,0:T(8,128)(2,1)S(1)} %add_convert_fusion.4.refs_1_), channel_id=1, source_target_pairs={{0,96},{8,104},{16,112},{24,120},{32,0},{40,8},{48,16},{56,24},{64... | collective-permute-start | bytes 786440 | tf_op jit(solution)/shard_map/ppermute | solution.py:246
  174.5 13.4 %collective-permute-start.17 = (bf16[2,256,256]{2,1,0:T(8,128)(2,1)S(1)}, bf16[2,256,256]{2,1,0:T(8,128)(2,1)S(1)}, u32[]{:S(2)}, u32[]{:S(2)}) collective-permute-start(bf16[2,256,256]{2,1,0:T(8,128)(2,1)S(1)} %add_convert_fusion.5.refs_1_), channel_id=1, source_target_pairs={{0,8},{8,16},{16,24},{24,0},{32,40},{40,48},{48,56},{56,32},{64,72... | collective-permute-start | bytes 786440 | tf_op jit(solution)/shard_map/ppermute | solution.py:249
  175.8 13.6 %collective-permute-start.18 = (bf16[2,256,256]{2,1,0:T(8,128)(2,1)S(1)}, bf16[2,256,256]{2,1,0:T(8,128)(2,1)S(1)}, u32[]{:S(2)}, u32[]{:S(2)}) collective-permute-start(bf16[2,256,256]{2,1,0:T(8,128)(2,1)S(1)} %add_convert_fusion.5.refs_1_), channel_id=1, source_target_pairs={{0,16},{8,24},{16,0},{24,8},{32,48},{40,56},{48,32},{56,40},{64,80... | collective-permute-start | bytes 786440 | tf_op jit(solution)/shard_map/ppermute | solution.py:249
  (15 other events, 105.0 us)
Sparse Core Ops, SparseCore 0:
  9.7 87.3 all-gather.1

commit v6 on v5

--- a/solution.py
+++ b/solution.py
@@ -356,12 +356,18 @@
     def around(value, along):
         return [value] + [along(value, ahead) for ahead in range(1, side)]
 
-    def whole(value, along):
-        values = [wide(one) for one in around(value, along)]
-        return narrow((values[0] + values[2]) + (values[1] + values[3]))
-
-    sum_y = whole(jnp.stack([keep[0], take[0]]), along_z)
-    sum_z = whole(jnp.stack([keep[1], take[1]]), along_y)
+    def whole(value, beside, along):
+        pair = narrow(wide(value) + wide(beside(value)))
+        return narrow(wide(pair) + wide(along(pair, 2)))
+
+    def beside_y(value):
+        return lax.ppermute(value, "dp", [(d, d ^ side) for d in range(n_dp)])
+
+    def beside_z(value):
+        return lax.ppermute(value, "dp", [(d, d ^ 1) for d in range(n_dp)])
+
+    sum_y = whole(jnp.stack([keep[0], take[0]]), beside_z, along_z)
+    sum_z = whole(jnp.stack([keep[1], take[1]]), beside_y, along_y)
     spot = jnp.stack([y, z, core]).astype(jnp.int32)
     grad_weight = place_blocks(0, spot, around(sum_y, along_y))
     grad_weight = place_blocks(1, spot, around(sum_z, along_z), grad_weight)

time: 200 us -> 199 us (level)
  waiting for transfers between devices: 60 us -> 62.1 us
    ppermute x0 -> x2, waiting for transfers between devices: none -> 5.23 us  [the longest x1 5.23 us: beside_z(): return lax.ppermute(value, 'dp', [(d, d ^ 1) for d in range(n_dp)])]
    ppermute x10 -> x8, starting transfers between devices: 18.4 us -> 15.1 us  [along_y(): lax.ppermute(value, 'dp', [(d, (d + side * ahead) % n_dp) for d in range(...]
    ppermute x0 -> x2, starting transfers between devices: none -> 3.17 us  [the longest x1 1.63 us: beside_z(): return lax.ppermute(value, 'dp', [(d, d ^ 1) for d in range(n_dp)])]
    ppermute x10 -> x8, waiting for transfers between devices: 7.16 us -> 5.15 us  [along_y(): lax.ppermute(value, 'dp', [(d, (d + side * ahead) % n_dp) for d in range(...]
    ppermute x10 -> x8, starting transfers between devices: 16.1 us -> 14.4 us  [along_z(): lax.ppermute(value, 'dp', [(d, d // side * side + (d + ahead) % side) for...]
    ppermute x10 -> x8, waiting for transfers between devices: 4.92 us -> 3.78 us  [along_z(): lax.ppermute(value, 'dp', [(d, d // side * side + (d + ahead) % side) for...]
  transfers between devices with their start and end apart: 29 -> 27, of which waited for: 17 -> 13; matrix products, arithmetic and copies ran while one was open for 14% -> 14% of each run, Pallas kernels for 18% -> 18%
where the time goes in v6:
time: 199 us
  waiting for transfers between devices  62.1 us (31%)
  starting transfers between devices  53.1 us (27%)
  Pallas kernels  37.7 us (19%)
  other arithmetic  16.5 us (8%)
  between operations  14.7 us (7%)
  matrix products  9.59 us (5%)
  local copies, waits for them, and re-layouts  4.81 us (2%)
    all_to_all x1, waiting for transfers between devices, on_device(): got = lax.all_to_all(send, 'dp', split_axis=0, concat_axis=0, tiled=True)  25.6 us
    ppermute x8, starting transfers between devices, along_y(): lax.ppermute(value, 'dp', [(d, (d + side * ahead) % n_dp) for d in range(...  15.1 us
    ppermute x8, starting transfers between devices, along_z(): lax.ppermute(value, 'dp', [(d, d // side * side + (d + ahead) % side) for...  14.4 us
    pallas_call x1, Pallas kernels, answer(): pl.pallas_call(lambda *refs: answer_body(width, *refs), out_shape=jax.Sha...  11.4 us
    ppermute x3, waiting for transfers between devices, along_x(): lax.ppermute(value, 'fsdp', [(f, (f + 2 * ahead) % n_fsdp) for f in range...  10.8 us
    pallas_call x1, Pallas kernels, project(): pl.pallas_call(lambda *refs: project_body(width, *refs), out_shape=jax.Sh...  9.91 us
    dot_general x8, matrix products, term(): lax.dot_general(both_rows, columns, (((0,), (0,)), ((), ())), preferred_e...  9.59 us
    pallas_call x1, Pallas kernels, pick_rows(): pl.pallas_call(pick_body, out_shape=jax.ShapeDtypeStruct((rows, width + E...  8.62 us
  transfers between devices with their start and end apart: 27, of which 13 were waited for; matrix products, arithmetic and copies ran while one was open for 14% of the time, Pallas kernels for 18%

profile of v6, /device:TPU:0, one launch (start us, length us, event | category | flops | bytes accessed | tf_op | source)
XLA Modules:
  0.0 198.5 jit_solution(14247575139721245504)
XLA Ops:
  8.8 8.6 %pick_rows.1 = bf16[512,2176]{1,0:T(8,128)(2,1)} custom-call(s32[16]{0:T(128)} %bitcast.47, s32[512,1]{1,0:T(8,128)} %copy.14.listed_ref, f32[1,2048]{1,0:T(1,128)} %bitcast.54, bf16[2048,2048]{1,0:T(8,128)(2,1)} %head_ref.1), custom_call_target="tpu_custom_call" | custom-call | tf_op jit(solution)/shard_map/pick_rows/pallas_call | solution.py:73
  17.4 8.1 %all-to-all-start = ((bf16[16,32,2176]{2,1,0:T(8,128)(2,1)}), bf16[16,32,2176]{2,1,0:T(8,128)(2,1)S(1)}, u32[]{:S(2)}, u32[]{:S(2)}) async-start(bf16[16,32,2176]{2,1,0:T(8,128)(2,1)} %bitcast.50), calls=%async_computation | async-start | bytes 4456448 | tf_op jit(solution)/shard_map/all_to_all | solution.py:276
  27.8 2.6 %collective-permute-done = bf16[256,2048]{1,0:T(8,128)(2,1)S(1)} collective-permute-done((bf16[256,2048]{1,0:T(8,128)(2,1)S(1)}, bf16[256,2048]{1,0:T(8,128)(2,1)S(1)}, u32[]{:S(2)}, u32[]{:S(2)}) %collective-permute-start) | collective-permute-done | bytes 1048608 | tf_op jit(solution)/shard_map/ppermute | solution.py:254
  32.0 25.6 %all-to-all-done.refs_1_ = bf16[16,32,2176]{2,1,0:T(8,128)(2,1)S(1)} async-done(((bf16[16,32,2176]{2,1,0:T(8,128)(2,1)}), bf16[16,32,2176]{2,1,0:T(8,128)(2,1)S(1)}, u32[]{:S(2)}, u32[]{:S(2)}) %all-to-all-start) | async-done | bytes 2228256 | tf_op jit(solution)/shard_map/all_to_all | solution.py:276
  59.3 2.5 %collective-permute-done.1 = bf16[256,2176]{1,0:T(8,128)(2,1)S(1)} collective-permute-done((bf16[256,2176]{1,0:T(8,128)(2,1)S(1)}, bf16[256,2176]{1,0:T(8,128)(2,1)S(1)}, u32[]{:S(2)}, u32[]{:S(2)}) %collective-permute-start.1) | collective-permute-done | bytes 1114144 | tf_op jit(solution)/shard_map/ppermute | solution.py:254
  64.5 2.7 %collective-permute-start.5 = (bf16[1024,256]{1,0:T(8,128)(2,1)S(1)}, bf16[1024,256]{1,0:T(8,128)(2,1)S(1)}, u32[]{:S(2)}, u32[]{:S(2)}) collective-permute-start(bf16[1024,256]{1,0:T(8,128)(2,1)S(1)} %get-tuple-element.50), channel_id=1, source_target_pairs={{0,24},{8,0},{16,8},{24,16},{32,56},{40,32},{48,40},{56,48},{64,88... | collective-permute-start | bytes 1572872 | tf_op jit(solution)/shard_map/ppermute | solution.py:249
  68.1 3.2 %collective-permute-start.4 = (bf16[1024,256]{1,0:T(8,128)(2,1)S(1)}, bf16[1024,256]{1,0:T(8,128)(2,1)S(1)}, u32[]{:S(2)}, u32[]{:S(2)}) collective-permute-start(bf16[1024,256]{1,0:T(8,128)(2,1)S(1)} %get-tuple-element.52), channel_id=1, source_target_pairs={{0,96},{8,104},{16,112},{24,120},{32,0},{40,8},{48,16},{56,24},{64... | collective-permute-start | bytes 1572872 | tf_op jit(solution)/shard_map/ppermute | solution.py:246
  79.1 3.6 %collective-permute-done.2 = bf16[1024,256]{1,0:T(8,128)(2,1)S(1)} collective-permute-done((bf16[1024,256]{1,0:T(8,128)(2,1)S(1)}, bf16[1024,256]{1,0:T(8,128)(2,1)S(1)}, u32[]{:S(2)}, u32[]{:S(2)}) %collective-permute-start.2) | collective-permute-done | bytes 524320 | tf_op jit(solution)/shard_map/ppermute | solution.py:246
  88.2 3.0 %collective-permute-start.7 = (bf16[2048,256]{1,0:T(8,128)(2,1)}, bf16[2048,256]{1,0:T(8,128)(2,1)}, u32[]{:S(2)}, u32[]{:S(2)}) collective-permute-start(bf16[2048,256]{1,0:T(8,128)(2,1)} %pad_maximum_fusion.3), channel_id=1, source_target_pairs={{0,96},{8,104},{16,112},{24,120},{32,0},{40,8},{48,16},{56,24},{64... | collective-permute-start | bytes 3145736 | tf_op jit(solution)/shard_map/ppermute | solution.py:246
  93.0 4.1 %all-gather.2.cloned.1.call-done.refs_2_.refs_1_ = bf16[2048,4096]{1,0:T(8,128)(2,1)} async-done(((bf16[256,4096]{1,0:T(8,128)(2,1)}), bf16[2048,4096]{1,0:T(8,128)(2,1)}) %all-gather.2.cloned.1.call-update) | async-done | bytes 16777232 | tf_op jit(solution)/shard_map/all_gather | solution.py:267
  97.1 11.4 %answer.1 = bf16[16,32,2176]{2,1,0:T(8,128)(2,1)} custom-call(s32[16]{0:T(128)} %broadcast_clamp_fusion.refs_0_, bf16[256,2176]{1,0:T(8,128)(2,1)} %bitcast.45, bf16[2048,4096]{1,0:T(8,128)(2,1)} %all-gather.2.cloned.1.call-done.refs_2_.refs_1_, bf16[256,4096]{1,0:T(8,128)(2,1)} %refs_3_.1), custom_call_target="tpu_custom_call" | custom-call | tf_op jit(solution)/shard_map/answer/pallas_call | solution.py:155
  108.5 7.0 %all-to-all-start.1 = ((bf16[16,32,2176]{2,1,0:T(8,128)(2,1)}), bf16[16,32,2176]{2,1,0:T(8,128)(2,1)S(1)}, u32[]{:S(2)}, u32[]{:S(2)}) async-start(bf16[16,32,2176]{2,1,0:T(8,128)(2,1)} %answer.1), calls=%async_computation.1 | async-start | bytes 4456448 | tf_op jit(solution)/shard_map/all_to_all | solution.py:327
  116.7 4.2 %add_bitcast_fusion = (f32[1,512,256]{2,1,0:T(8,128)}, bf16[1,512,256]{2,1,0:T(8,128)(2,1)S(1)}, bf16[1,512,256]{2,1,0:T(8,128)(2,1)S(1)}, bf16[1,512,256]{2,1,0...) fusion(bf16[2048,256]{1,0:T(8,128)(2,1)} %collective-permute-do, ...), kind=kLoop, calls=%fused_computation.36 | loop fusion | flops 6029312 | bytes 8912912 | tf_op jit(solution)/shard_map/stack | solution.py:336
  121.7 3.5 %collective-permute-start.12 = (bf16[2,512,256]{2,1,0:T(8,128)(2,1)}, bf16[2,512,256]{2,1,0:T(8,128)(2,1)}, u32[]{:S(2)}, u32[]{:S(2)}) collective-permute-start(bf16[2,512,256]{2,1,0:T(8,128)(2,1)} %pad_maximum_fusion.9), channel_id=1, source_target_pairs={{0,6},{1,7},{2,0},{3,1},{4,2},{5,3},{6,4},{7,5},{8,14},{9,15},{10,... | collective-permute-start | bytes 1572872 | tf_op jit(solution)/shard_map/ppermute | solution.py:243
  128.4 9.9 %project.1 = bf16[256,4096]{1,0:T(8,128)(2,1)} custom-call(bf16[256,2176]{1,0:T(8,128)(2,1)} %bitcast.46, bf16[2048,4096]{1,0:T(8,128)(2,1)} %all-gather.2.cloned.1.call-done.refs_2_.refs_1_), custom_call_target="tpu_custom_call" | custom-call | tf_op jit(solution)/shard_map/project/pallas_call | solution.py:185
  138.4 10.8 %collective-permute-done.11 = bf16[2,512,256]{2,1,0:T(8,128)(2,1)} collective-permute-done((bf16[2,512,256]{2,1,0:T(8,128)(2,1)}, bf16[2,512,256]{2,1,0:T(8,128)(2,1)}, u32[]{:S(2)}, u32[]{:S(2)}) %collective-permute-start.11) | collective-permute-done | bytes 524320 | tf_op jit(solution)/shard_map/ppermute | solution.py:243
  155.7 5.2 %collective-permute-done.19 = bf16[2,256,256]{2,1,0:T(8,128)(2,1)S(1)} collective-permute-done((bf16[2,256,256]{2,1,0:T(8,128)(2,1)S(1)}, bf16[2,256,256]{2,1,0:T(8,128)(2,1)S(1)}, u32[]{:S(2)}, u32[]{:S(2)}) %collective-permute-start.19) | collective-permute-done | bytes 262176 | tf_op jit(solution)/shard_map/ppermute | solution.py:367
  161.0 3.1 %collective-permute-start.20 = (bf16[2,256,256]{2,1,0:T(8,128)(2,1)S(1)}, bf16[2,256,256]{2,1,0:T(8,128)(2,1)S(1)}, u32[]{:S(2)}, u32[]{:S(2)}) collective-permute-start(bf16[2,256,256]{2,1,0:T(8,128)(2,1)S(1)} %add_convert_fusion.5), channel_id=1, source_target_pairs={{0,16},{8,24},{16,0},{24,8},{32,48},{40,56},{48,32},{56,40},{64,80... | collective-permute-start | bytes 786440 | tf_op jit(solution)/shard_map/ppermute | solution.py:249
  164.2 3.1 %collective-permute-start.15 = (bf16[2,256,256]{2,1,0:T(8,128)(2,1)S(1)}, bf16[2,256,256]{2,1,0:T(8,128)(2,1)S(1)}, u32[]{:S(2)}, u32[]{:S(2)}) collective-permute-start(bf16[2,256,256]{2,1,0:T(8,128)(2,1)S(1)} %add_convert_fusion.7), channel_id=1, source_target_pairs={{0,64},{8,72},{16,80},{24,88},{32,96},{40,104},{48,112},{56,120},{... | collective-permute-start | bytes 786440 | tf_op jit(solution)/shard_map/ppermute | solution.py:246
  167.2 2.9 %collective-permute-done.20 = bf16[2,256,256]{2,1,0:T(8,128)(2,1)S(1)} collective-permute-done((bf16[2,256,256]{2,1,0:T(8,128)(2,1)S(1)}, bf16[2,256,256]{2,1,0:T(8,128)(2,1)S(1)}, u32[]{:S(2)}, u32[]{:S(2)}) %collective-permute-start.20) | collective-permute-done | bytes 262176 | tf_op jit(solution)/shard_map/ppermute | solution.py:249
  171.8 2.8 %collective-permute-start.22 = (bf16[2,256,256]{2,1,0:T(8,128)(2,1)S(1)}, bf16[2,256,256]{2,1,0:T(8,128)(2,1)}, u32[]{:S(2)}, u32[]{:S(2)}) collective-permute-start(bf16[2,256,256]{2,1,0:T(8,128)(2,1)S(1)} %add_convert_fusion.4.refs_1_), channel_id=1, source_target_pairs={{0,64},{8,72},{16,80},{24,88},{32,96},{40,104},{48,112},{56,120},{... | collective-permute-start | bytes 786440 | tf_op jit(solution)/shard_map/ppermute | solution.py:246
  177.7 2.7 %collective-permute-start.17 = (bf16[2,256,256]{2,1,0:T(8,128)(2,1)S(1)}, bf16[2,256,256]{2,1,0:T(8,128)(2,1)S(1)}, u32[]{:S(2)}, u32[]{:S(2)}) collective-permute-start(bf16[2,256,256]{2,1,0:T(8,128)(2,1)S(1)} %add_convert_fusion.6.refs_1_), channel_id=1, source_target_pairs={{0,16},{8,24},{16,0},{24,8},{32,48},{40,56},{48,32},{56,40},{64,80... | collective-permute-start | bytes 786440 | tf_op jit(solution)/shard_map/ppermute | solution.py:249
  184.3 2.2 %move_blocks.3 = bf16[16,32,2048]{2,1,0:T(8,128)(2,1)} custom-call(s32[16]{0:T(128)S(1)} %bitcast.49, bf16[16,32,2176]{2,1,0:T(8,128)(2,1)S(1)} %all-to-all-done.1.refs_1_), custom_call_target="tpu_custom_call" | custom-call | tf_op jit(solution)/shard_map/move_blocks/pallas_call | solution.py:113
  186.4 2.9 %place_blocks.2.refs_5_ = f32[256,4096]{1,0:T(8,128)} custom-call(s32[3]{0:T(128)S(1)} %pad_add_fusion.refs_0_, bf16[2,256,256]{2,1,0:T(8,128)(2,1)S(1)} %add_convert_fusion.4.refs_1_, bf16[2,256,256]{2,1,0:T(8,128)(2,1)S(1)} %copy-done.2, bf16[2,256,256]{2,1,0:T(8,128)(2,1)} %collective-permute-done.22.refs_3_, ...), custom_call_target="tpu_custom_call" | custom-call | tf_op jit(solution)/shard_map/place_blocks/pallas_call | solution.py:213
  (107 shorter events, 48.1 us)
Async XLA Ops:
  7.2 90.0 %all-gather.2.cloned.1.call-start = ((), (), s32[]{:S(2)}) async-start(), calls=%async_computation.2 | async-start | bytes 18874368 | tf_op jit(solution)/shard_map/all_gather | solution.py:267
  17.4 40.2 %all-to-all-start = ((bf16[16,32,2176]{2,1,0:T(8,128)(2,1)}), bf16[16,32,2176]{2,1,0:T(8,128)(2,1)S(1)}, u32[]{:S(2)}, u32[]{:S(2)}) async-start(bf16[16,32,2176]{2,1,0:T(8,128)(2,1)} %bitcast.50), calls=%async_computation | async-start | bytes 4456448 | tf_op jit(solution)/shard_map/all_to_all | solution.py:276
  63.9 15.2 %collective-permute-start.3 = (bf16[1024,256]{1,0:T(8,128)(2,1)S(1)}, bf16[1024,256]{1,0:T(8,128)(2,1)S(1)}, u32[]{:S(2)}, u32[]{:S(2)}) collective-permute-start(bf16[1024,256]{1,0:T(8,128)(2,1)S(1)} %get-tuple-element.51), channel_id=1, source_target_pairs={{0,8},{8,16},{16,24},{24,0},{32,40},{40,48},{48,56},{56,32},{64,72... | collective-permute-start | bytes 1572872 | tf_op jit(solution)/shard_map/ppermute | solution.py:249
  64.5 14.6 %collective-permute-start.5 = (bf16[1024,256]{1,0:T(8,128)(2,1)S(1)}, bf16[1024,256]{1,0:T(8,128)(2,1)S(1)}, u32[]{:S(2)}, u32[]{:S(2)}) collective-permute-start(bf16[1024,256]{1,0:T(8,128)(2,1)S(1)} %get-tuple-element.50), channel_id=1, source_target_pairs={{0,24},{8,0},{16,8},{24,16},{32,56},{40,32},{48,40},{56,48},{64,88... | collective-permute-start | bytes 1572872 | tf_op jit(solution)/shard_map/ppermute | solution.py:249
  68.0 14.6 %collective-permute-start.2 = (bf16[1024,256]{1,0:T(8,128)(2,1)S(1)}, bf16[1024,256]{1,0:T(8,128)(2,1)S(1)}, u32[]{:S(2)}, u32[]{:S(2)}) collective-permute-start(bf16[1024,256]{1,0:T(8,128)(2,1)S(1)} %get-tuple-element.53), channel_id=1, source_target_pairs={{0,32},{8,40},{16,48},{24,56},{32,64},{40,72},{48,80},{56,88},{64,... | collective-permute-start | bytes 1572872 | tf_op jit(solution)/shard_map/ppermute | solution.py:246
  68.1 14.6 %collective-permute-start.4 = (bf16[1024,256]{1,0:T(8,128)(2,1)S(1)}, bf16[1024,256]{1,0:T(8,128)(2,1)S(1)}, u32[]{:S(2)}, u32[]{:S(2)}) collective-permute-start(bf16[1024,256]{1,0:T(8,128)(2,1)S(1)} %get-tuple-element.52), channel_id=1, source_target_pairs={{0,96},{8,104},{16,112},{24,120},{32,0},{40,8},{48,16},{56,24},{64... | collective-permute-start | bytes 1572872 | tf_op jit(solution)/shard_map/ppermute | solution.py:246
  83.9 31.7 %collective-permute-start.9 = (bf16[2048,256]{1,0:T(8,128)(2,1)}, bf16[2048,256]{1,0:T(8,128)(2,1)}, u32[]{:S(2)}, u32[]{:S(2)}) collective-permute-start(bf16[2048,256]{1,0:T(8,128)(2,1)} %pad_maximum_fusion.5), channel_id=1, source_target_pairs={{0,24},{8,0},{16,8},{24,16},{32,56},{40,32},{48,40},{56,48},{64,88... | collective-permute-start | bytes 3145736 | tf_op jit(solution)/shard_map/ppermute | solution.py:249
  85.3 30.3 %collective-permute-start.8 = (bf16[2048,256]{1,0:T(8,128)(2,1)}, bf16[2048,256]{1,0:T(8,128)(2,1)}, u32[]{:S(2)}, u32[]{:S(2)}) collective-permute-start(bf16[2048,256]{1,0:T(8,128)(2,1)} %pad_maximum_fusion.4), channel_id=1, source_target_pairs={{0,8},{8,16},{16,24},{24,0},{32,40},{40,48},{48,56},{56,32},{64,72... | collective-permute-start | bytes 3145736 | tf_op jit(solution)/shard_map/ppermute | solution.py:249
  88.2 27.4 %collective-permute-start.7 = (bf16[2048,256]{1,0:T(8,128)(2,1)}, bf16[2048,256]{1,0:T(8,128)(2,1)}, u32[]{:S(2)}, u32[]{:S(2)}) collective-permute-start(bf16[2048,256]{1,0:T(8,128)(2,1)} %pad_maximum_fusion.3), channel_id=1, source_target_pairs={{0,96},{8,104},{16,112},{24,120},{32,0},{40,8},{48,16},{56,24},{64... | collective-permute-start | bytes 3145736 | tf_op jit(solution)/shard_map/ppermute | solution.py:246
  92.5 24.2 %collective-permute-start.6 = (bf16[2048,256]{1,0:T(8,128)(2,1)}, bf16[2048,256]{1,0:T(8,128)(2,1)}, u32[]{:S(2)}, u32[]{:S(2)}) collective-permute-start(bf16[2048,256]{1,0:T(8,128)(2,1)} %pad_maximum_fusion.2), channel_id=1, source_target_pairs={{0,32},{8,40},{16,48},{24,56},{32,64},{40,72},{48,80},{56,88},{64,... | collective-permute-start | bytes 3145736 | tf_op jit(solution)/shard_map/ppermute | solution.py:246
  108.5 40.7 %all-to-all-start.1 = ((bf16[16,32,2176]{2,1,0:T(8,128)(2,1)}), bf16[16,32,2176]{2,1,0:T(8,128)(2,1)S(1)}, u32[]{:S(2)}, u32[]{:S(2)}) async-start(bf16[16,32,2176]{2,1,0:T(8,128)(2,1)} %answer.1), calls=%async_computation.1 | async-start | bytes 4456448 | tf_op jit(solution)/shard_map/all_to_all | solution.py:327
  121.7 16.7 %collective-permute-start.12 = (bf16[2,512,256]{2,1,0:T(8,128)(2,1)}, bf16[2,512,256]{2,1,0:T(8,128)(2,1)}, u32[]{:S(2)}, u32[]{:S(2)}) collective-permute-start(bf16[2,512,256]{2,1,0:T(8,128)(2,1)} %pad_maximum_fusion.9), channel_id=1, source_target_pairs={{0,6},{1,7},{2,0},{3,1},{4,2},{5,3},{6,4},{7,5},{8,14},{9,15},{10,... | collective-permute-start | bytes 1572872 | tf_op jit(solution)/shard_map/ppermute | solution.py:243
  126.0 23.2 %collective-permute-start.11 = (bf16[2,512,256]{2,1,0:T(8,128)(2,1)}, bf16[2,512,256]{2,1,0:T(8,128)(2,1)}, u32[]{:S(2)}, u32[]{:S(2)}) collective-permute-start(bf16[2,512,256]{2,1,0:T(8,128)(2,1)} %pad_maximum_fusion.8), channel_id=1, source_target_pairs={{0,2},{1,3},{2,4},{3,5},{4,6},{5,7},{6,0},{7,1},{8,10},{9,11},{10,... | collective-permute-start | bytes 1572872 | tf_op jit(solution)/shard_map/ppermute | solution.py:243
  126.9 22.3 %collective-permute-start.10 = (bf16[2,512,256]{2,1,0:T(8,128)(2,1)}, bf16[2,512,256]{2,1,0:T(8,128)(2,1)}, u32[]{:S(2)}, u32[]{:S(2)}) collective-permute-start(bf16[2,512,256]{2,1,0:T(8,128)(2,1)} %pad_maximum_fusion.7), channel_id=1, source_target_pairs={{0,4},{1,5},{2,6},{3,7},{4,0},{5,1},{6,2},{7,3},{8,12},{9,13},{10,... | collective-permute-start | bytes 1572872 | tf_op jit(solution)/shard_map/ppermute | solution.py:243
  152.5 8.4 %collective-permute-start.19 = (bf16[2,256,256]{2,1,0:T(8,128)(2,1)S(1)}, bf16[2,256,256]{2,1,0:T(8,128)(2,1)S(1)}, u32[]{:S(2)}, u32[]{:S(2)}) collective-permute-start(bf16[2,256,256]{2,1,0:T(8,128)(2,1)S(1)} %pad_maximum_fusion.11), channel_id=1, source_target_pairs={{0,8},{8,0},{16,24},{24,16},{32,40},{40,32},{48,56},{56,48},{64,72... | collective-permute-start | bytes 786440 | tf_op jit(solution)/shard_map/ppermute | solution.py:367
  154.2 10.0 %collective-permute-start.14 = (bf16[2,256,256]{2,1,0:T(8,128)(2,1)S(1)}, bf16[2,256,256]{2,1,0:T(8,128)(2,1)S(1)}, u32[]{:S(2)}, u32[]{:S(2)}) collective-permute-start(bf16[2,256,256]{2,1,0:T(8,128)(2,1)S(1)} %pad_maximum_fusion.10), channel_id=1, source_target_pairs={{0,32},{8,40},{16,48},{24,56},{32,0},{40,8},{48,16},{56,24},{64,96... | collective-permute-start | bytes 786440 | tf_op jit(solution)/shard_map/ppermute | solution.py:364
  161.0 9.1 %collective-permute-start.20 = (bf16[2,256,256]{2,1,0:T(8,128)(2,1)S(1)}, bf16[2,256,256]{2,1,0:T(8,128)(2,1)S(1)}, u32[]{:S(2)}, u32[]{:S(2)}) collective-permute-start(bf16[2,256,256]{2,1,0:T(8,128)(2,1)S(1)} %add_convert_fusion.5), channel_id=1, source_target_pairs={{0,16},{8,24},{16,0},{24,8},{32,48},{40,56},{48,32},{56,40},{64,80... | collective-permute-start | bytes 786440 | tf_op jit(solution)/shard_map/ppermute | solution.py:249
  164.2 11.9 %collective-permute-start.15 = (bf16[2,256,256]{2,1,0:T(8,128)(2,1)S(1)}, bf16[2,256,256]{2,1,0:T(8,128)(2,1)S(1)}, u32[]{:S(2)}, u32[]{:S(2)}) collective-permute-start(bf16[2,256,256]{2,1,0:T(8,128)(2,1)S(1)} %add_convert_fusion.7), channel_id=1, source_target_pairs={{0,64},{8,72},{16,80},{24,88},{32,96},{40,104},{48,112},{56,120},{... | collective-permute-start | bytes 786440 | tf_op jit(solution)/shard_map/ppermute | solution.py:246
  170.2 10.6 %collective-permute-start.21 = (bf16[2,256,256]{2,1,0:T(8,128)(2,1)S(1)}, bf16[2,256,256]{2,1,0:T(8,128)(2,1)S(1)}, u32[]{:S(2)}, u32[]{:S(2)}) collective-permute-start(bf16[2,256,256]{2,1,0:T(8,128)(2,1)S(1)} %add_convert_fusion.4.refs_1_), channel_id=1, source_target_pairs={{0,32},{8,40},{16,48},{24,56},{32,64},{40,72},{48,80},{56,88},{64,... | collective-permute-start | bytes 786440 | tf_op jit(solution)/shard_map/ppermute | solution.py:246
  171.8 14.6 %collective-permute-start.22 = (bf16[2,256,256]{2,1,0:T(8,128)(2,1)S(1)}, bf16[2,256,256]{2,1,0:T(8,128)(2,1)}, u32[]{:S(2)}, u32[]{:S(2)}) collective-permute-start(bf16[2,256,256]{2,1,0:T(8,128)(2,1)S(1)} %add_convert_fusion.4.refs_1_), channel_id=1, source_target_pairs={{0,64},{8,72},{16,80},{24,88},{32,96},{40,104},{48,112},{56,120},{... | collective-permute-start | bytes 786440 | tf_op jit(solution)/shard_map/ppermute | solution.py:246
  174.6 11.8 %collective-permute-start.23 = (bf16[2,256,256]{2,1,0:T(8,128)(2,1)S(1)}, bf16[2,256,256]{2,1,0:T(8,128)(2,1)}, u32[]{:S(2)}, u32[]{:S(2)}) collective-permute-start(bf16[2,256,256]{2,1,0:T(8,128)(2,1)S(1)} %add_convert_fusion.4.refs_1_), channel_id=1, source_target_pairs={{0,96},{8,104},{16,112},{24,120},{32,0},{40,8},{48,16},{56,24},{64... | collective-permute-start | bytes 786440 | tf_op jit(solution)/shard_map/ppermute | solution.py:246
  176.1 13.2 %collective-permute-start.16 = (bf16[2,256,256]{2,1,0:T(8,128)(2,1)S(1)}, bf16[2,256,256]{2,1,0:T(8,128)(2,1)S(1)}, u32[]{:S(2)}, u32[]{:S(2)}) collective-permute-start(bf16[2,256,256]{2,1,0:T(8,128)(2,1)S(1)} %add_convert_fusion.6.refs_1_), channel_id=1, source_target_pairs={{0,8},{8,16},{16,24},{24,0},{32,40},{40,48},{48,56},{56,32},{64,72... | collective-permute-start | bytes 786440 | tf_op jit(solution)/shard_map/ppermute | solution.py:249
  177.7 12.0 %collective-permute-start.17 = (bf16[2,256,256]{2,1,0:T(8,128)(2,1)S(1)}, bf16[2,256,256]{2,1,0:T(8,128)(2,1)S(1)}, u32[]{:S(2)}, u32[]{:S(2)}) collective-permute-start(bf16[2,256,256]{2,1,0:T(8,128)(2,1)S(1)} %add_convert_fusion.6.refs_1_), channel_id=1, source_target_pairs={{0,16},{8,24},{16,0},{24,8},{32,48},{40,56},{48,32},{56,40},{64,80... | collective-permute-start | bytes 786440 | tf_op jit(solution)/shard_map/ppermute | solution.py:249
  181.5 8.2 %collective-permute-start.18 = (bf16[2,256,256]{2,1,0:T(8,128)(2,1)S(1)}, bf16[2,256,256]{2,1,0:T(8,128)(2,1)S(1)}, u32[]{:S(2)}, u32[]{:S(2)}) collective-permute-start(bf16[2,256,256]{2,1,0:T(8,128)(2,1)S(1)} %add_convert_fusion.6.refs_1_), channel_id=1, source_target_pairs={{0,24},{8,0},{16,8},{24,16},{32,56},{40,32},{48,40},{56,48},{64,88... | collective-permute-start | bytes 786440 | tf_op jit(solution)/shard_map/ppermute | solution.py:249
  (13 other events, 86.7 us)
Sparse Core Ops, SparseCore 0:
  9.7 87.3 all-gather.1
